TPU v7x, 32 devices: a whole 2x2x4 slice. The times are simulated.
32 devices in a mesh: tile: 2 (over core), view: 16 (over z, y, x).
Axes of the slice: x: 2, y: 2, z: 4, core: 2. Of those that a mesh axis runs over, the one named last changes fastest.
Arguments:
- estimate: float32 [48, 768, 128], P('tile', 'view'), may hold values from 0.5 to 1.5
- views: float32 [6, 48, 768, 128], P(None, 'tile', 'view'), may hold values from 0.1 to 3
- background: float32 [6], replicated, may hold values from 0.1 to 1
- psf_taps: float32 [6, 3, 11], replicated, may hold values from 0.2 to 1
- psf_lengths: int32 [6, 3], replicated, may hold values from 3 to 11, as said below
- view_offsets: int32 [6, 3], replicated, may hold values from -4 to 4, as said below
- field_rows: int32 [6, 2], replicated, may hold values from 0 to 768, as said below
Outputs:
- restored: float32 [48, 768, 128], P('tile', 'view')
Inputs may be any that keep to these rules, and one draw needn't show every extreme that they name: `psf_lengths`: odd; for each dimension some view has length 11. `view_offsets`: for each dimension some view has offset 4 and another -4. `field_rows`: the first column is at most 192 and the second at least 576; some view starts at row 0 and some ends at row 768.
All inputs are finite; a program needn't handle non-finite values.
Results may differ from a plain program's by a relative error of at most 0.0003.
Values sent between devices are 32-bit elements; how exact they have to be, the bound alone decides.
No kernel may reach another device: no remote copies, remote signals or barrier semaphores. Data moves between devices by JAX's collectives and lax.ppermute only.
A program may use at most 64 MiB of HBM per device.

v0:
```python
import functools

import jax
import jax.numpy as jnp
from jax import lax
from jax.experimental import pallas as pl
from jax.experimental.pallas import tpu as pltpu
from jax.sharding import PartitionSpec as P

ITERS = 2
HALO = 9
FAR = 1 << 20
F32 = jnp.float32
BF16 = jnp.bfloat16


def up(size, unit):
    return -(-size // unit) * unit


class Plan:
    def __init__(self, views, depth, rows, lanes, tiles):
        self.views, self.depth, self.rows, self.lanes = views, depth, rows, lanes
        self.z_stages = 1 if tiles == 2 else 2
        self.z_side = up(HALO, 8)
        self.z_used = depth + self.z_side * self.z_stages
        self.z_slots = up(self.z_used, 16)
        self.y_used = rows + 2 * HALO
        self.y_slots = up(self.y_used, 16)
        self.pitch = self.y_slots + (8 if (self.y_slots // 8) % 2 == 0 else 0)
        self.stack = views * depth


def swaps(count):
    first, second = [], []
    for i in range(0, count - 1, 2):
        first += [(i, i + 1), (i + 1, i)]
    for i in range(1, count - 1, 2):
        second += [(i, i + 1), (i + 1, i)]
    return first, second


def split(value):
    high = value.astype(BF16)
    return high, (value - high.astype(F32)).astype(BF16)


def place(slot, own, side, stages, even):
    after, before = slot, slot - own - side
    first = jnp.where(even == 1, after, before)
    second = jnp.where(even == 1, before - side, after - side)
    far = jnp.full_like(slot, FAR)
    last = jnp.where(slot < own + 2 * side, second, far) if stages == 2 else far
    return jnp.where(slot < own, slot, jnp.where(slot < own + side, first, last))


def bands_kernel(plan, where_ref, start_ref, taps_ref, zf_ref, za_ref, yf_ref, ya_ref, xf_ref, xa_ref, zf_wide):
    views, depth, rows, lanes = plan.views, plan.depth, plan.rows, plan.lanes
    taps = taps_ref.shape[0] // (views * 3)
    even_z, even_y = where_ref[0], where_ref[1]

    def weight(v, d, k):
        return taps_ref[(v * 3 + d) * taps + k]

    def banded(v, d, delta):
        value = jnp.zeros(delta.shape, F32)
        for k in range(taps):
            value = jnp.where(delta == k, weight(v, d, k), value)
        return value

    def parted(value, low):
        high = value.astype(BF16).astype(F32)
        return jnp.where(low, value - high, high)

    def columns(count, period):
        column = lax.broadcasted_iota(jnp.int32, (1, count * period), 1)
        part = jnp.zeros_like(column)
        for i in range(1, count):
            part = part + (column >= i * period).astype(jnp.int32)
        return part, column - part * period

    part, slot = columns(3, plan.z_slots)
    z_in = place(slot, depth, plan.z_side, plan.z_stages, even_z)
    z_out = lax.broadcasted_iota(jnp.int32, (depth, 1), 0)
    for v in range(views):
        value = banded(v, 0, z_in - z_out - start_ref[v * 3])
        zf_wide[v * depth : (v + 1) * depth, :] = parted(value, part == 2)
    zf_ref[...] = zf_wide[...].astype(BF16)

    part, column = columns(3, plan.stack)
    view = jnp.zeros_like(column)
    for v in range(1, views):
        view = view + (column >= v * depth).astype(jnp.int32)
    begin = jnp.zeros_like(column)
    for v in range(views):
        begin = jnp.where(view == v, start_ref[v * 3], begin)
    z_in = column - view * depth
    slot = lax.broadcasted_iota(jnp.int32, (plan.z_slots, 1), 0)
    z_out = place(slot, depth, plan.z_side, plan.z_stages, even_z)
    delta = z_out - (z_in + begin)
    value = jnp.zeros(delta.shape, F32)
    for k in range(taps):
        row = jnp.zeros(column.shape, F32)
        for v in range(views):
            row = jnp.where(view == v, weight(v, 0, k), row)
        value = jnp.where(delta == k, row, value)
    za_ref[...] = parted(value, part == 2).astype(BF16)

    def of_view(v, carry):
        part, slot = columns(3, plan.y_slots)
        y_in = place(slot, rows, HALO, 2, even_y)
        y_out = lax.broadcasted_iota(jnp.int32, (rows, 1), 0)
        value = banded(v, 1, y_in - y_out - start_ref[v * 3 + 1])
        yf_ref[v] = parted(value, part == 2).astype(BF16)

        part, y_in = columns(3, rows)
        slot = lax.broadcasted_iota(jnp.int32, (plan.y_slots, 1), 0)
        y_out = place(slot, rows, HALO, 2, even_y)
        value = banded(v, 1, y_out - y_in - start_ref[v * 3 + 1])
        ya_ref[v] = parted(value, part == 2).astype(BF16)

        x_in = lax.broadcasted_iota(jnp.int32, (lanes, lanes), 0)
        x_out = lax.broadcasted_iota(jnp.int32, (lanes, lanes), 1)
        for ref, delta in ((xf_ref, x_in - x_out), (xa_ref, x_out - x_in)):
            high, low = split(banded(v, 2, delta - start_ref[v * 3 + 2]))
            ref[v, :, :lanes] = high
            ref[v, :, lanes:] = low
        return carry

    lax.fori_loop(0, views, of_view, 0)


def bands(plan, where, start, taps):
    views, lanes = plan.views, plan.lanes
    shapes = (
        (plan.stack, 3 * plan.z_slots),
        (plan.z_slots, 3 * plan.stack),
        (views, plan.rows, 3 * plan.y_slots),
        (views, plan.y_slots, 3 * plan.rows),
        (views, lanes, 2 * lanes),
        (views, lanes, 2 * lanes),
    )
    smem = pl.BlockSpec(memory_space=pltpu.SMEM)
    vmem = pl.BlockSpec(memory_space=pltpu.VMEM)
    return pl.pallas_call(
        functools.partial(bands_kernel, plan),
        out_shape=[jax.ShapeDtypeStruct(shape, BF16) for shape in shapes],
        in_specs=[smem] * 3,
        out_specs=[vmem] * len(shapes),
        scratch_shapes=[pltpu.VMEM(shapes[0], F32)],
        compiler_params=pltpu.CompilerParams(vmem_limit_bytes=24 << 20),
        cost_estimate=pl.CostEstimate(flops=10_000_000, bytes_accessed=4_000_000, transcendentals=0),
        name="bands",
    )(where, start, taps)


def dot(a, b):
    return jnp.dot(a, b, preferred_element_type=F32)


def step_kernel(
    plan, where_ref, field_ref, level_ref, own_ref, side_ref, zf_ref, za_ref, yf_ref, ya_ref, xf_ref, xa_ref, views_hbm,
    own_out, side_out, grid_ref, views_ref, sems,
):
    views, depth, rows, lanes = plan.views, plan.depth, plan.rows, plan.lanes
    pitch, y_slots, stack = plan.pitch, plan.y_slots, plan.stack
    sides = plan.z_used - depth

    def fetch(v):
        return pltpu.make_async_copy(views_hbm.at[v], views_ref.at[v], sems.at[v])

    for v in range(views):
        fetch(v).start()

    blank = jnp.zeros((y_slots - plan.y_used // 8 * 8, lanes), F32)

    def clear(i, carry):
        grid_ref[pl.ds(i * pitch + plan.y_used // 8 * 8, blank.shape[0]), :] = blank
        return carry

    lax.fori_loop(0, stack, clear, 0, unroll=8)

    def three(value):
        high, low = split(value)
        return jnp.concatenate([high, low, high], axis=0)

    def z_forward(pair, carry):
        parts = []
        for i in range(2):
            y = pair * 2 + i
            pieces = [own_ref[y], side_ref[y]]
            if plan.z_slots > plan.z_used:
                pieces.append(jnp.zeros((plan.z_slots - plan.z_used, lanes), F32))
            parts.append(three(jnp.concatenate(pieces, axis=0)))
        out = dot(zf_ref[...], jnp.concatenate(parts, axis=1))
        for i in range(2):
            grid_ref[pl.ds(pair * 2 + i, stack, stride=pitch), :] = out[:, i * lanes : (i + 1) * lanes]
        return carry

    lax.fori_loop(0, plan.y_used // 2, z_forward, 0, unroll=3)

    def of_view(v, carry):
        fetch(v).wait()
        lower, upper, first = field_ref[v * 2], field_ref[v * 2 + 1], where_ref[2]
        level = level_ref[v]
        y = first + lax.broadcasted_iota(jnp.int32, (rows, lanes), 0)
        covered = (y >= lower) & (y < upper)
        lane_forward = jnp.concatenate([xf_ref[v]] * 2, axis=0)
        lane_adjoint = jnp.concatenate([xa_ref[v]] * 2, axis=0)

        def along_x(value, matrix):
            out = dot(jnp.concatenate(split(value), axis=1), matrix)
            return out[:, :lanes] + out[:, lanes:]

        chunk = 8
        for z0 in range(0, depth, chunk):
            base = pl.multiple_of((v * depth + z0) * pitch, 8)
            spread = []
            for z in range(0, chunk, 2):
                parts = [three(grid_ref[pl.ds(base + (z + i) * pitch, y_slots), :]) for i in range(2)]
                out = dot(yf_ref[v], jnp.concatenate(parts, axis=1))
                spread += [out[:, :lanes], out[:, lanes:]]
            blurred = along_x(jnp.concatenate(spread, axis=0), lane_forward).reshape(chunk, rows, lanes)
            ratio = jnp.where(covered[None], views_ref[v, z0 : z0 + chunk] / (blurred + level), 1.0)
            back = along_x(ratio.reshape(chunk * rows, lanes), lane_adjoint)
            for z in range(0, chunk, 2):
                parts = [three(back[(z + i) * rows : (z + i + 1) * rows]) for i in range(2)]
                out = dot(ya_ref[v], jnp.concatenate(parts, axis=1))
                for i in range(2):
                    grid_ref[pl.ds(base + (z + i) * pitch, y_slots), :] = out[:, i * lanes : (i + 1) * lanes]
        return carry

    lax.fori_loop(0, views, of_view, 0)

    def z_adjoint(pair, carry):
        parts = [three(grid_ref[pl.ds(pair * 2 + i, stack, stride=pitch), :]) for i in range(2)]
        out = dot(za_ref[...], jnp.concatenate(parts, axis=1))
        for i in range(2):
            value = out[:, i * lanes : (i + 1) * lanes]
            own_out[pair * 2 + i] = value[:depth]
            side_out[pair * 2 + i] = value[depth : depth + sides]
        return carry

    lax.fori_loop(0, plan.y_used // 2, z_adjoint, 0, unroll=3)


def step(plan, where, field, level, own, side, tables, views):
    smem = pl.BlockSpec(memory_space=pltpu.SMEM)
    vmem = pl.BlockSpec(memory_space=pltpu.VMEM)
    sides = plan.z_used - plan.depth
    return pl.pallas_call(
        functools.partial(step_kernel, plan),
        out_shape=[
            jax.ShapeDtypeStruct((plan.y_used, plan.depth, plan.lanes), F32),
            jax.ShapeDtypeStruct((plan.y_used, sides, plan.lanes), F32),
        ],
        in_specs=[smem] * 3 + [vmem] * 8 + [pl.BlockSpec(memory_space=pl.ANY)],
        out_specs=[vmem] * 2,
        scratch_shapes=[
            pltpu.VMEM((plan.stack * plan.pitch, plan.lanes), F32),
            pltpu.VMEM(views.shape, F32),
            pltpu.SemaphoreType.DMA((plan.views,)),
        ],
        compiler_params=pltpu.CompilerParams(vmem_limit_bytes=40 << 20),
        cost_estimate=pl.CostEstimate(flops=8_000_000_000, bytes_accessed=8_000_000, transcendentals=0),
        name="step",
    )(where, field, level, own, side, *tables, views)


def taps_table(psf_taps, psf_lengths):
    places = jnp.arange(psf_taps.shape[2], dtype=jnp.int32)
    live = (places[None, None, :] < psf_lengths[:, :, None]).astype(jnp.float32)
    raw = psf_taps * live
    return raw / jnp.sum(raw, axis=2, keepdims=True)


def on_device(estimate, views, background, psf_taps, psf_lengths, view_offsets, field_rows):
    count = views.shape[0]
    depth, rows, lanes = estimate.shape
    tiles, blocks = lax.axis_size("tile"), lax.axis_size("view")
    plan = Plan(count, depth, rows, lanes, tiles)
    z_side, halo = plan.z_side, HALO
    tile_at, view_at = lax.axis_index("tile"), lax.axis_index("view")
    even_z, even_y = 1 - tile_at % 2, 1 - view_at % 2
    where = jnp.stack([even_z, even_y, view_at * rows]).astype(jnp.int32)
    weights = taps_table(psf_taps, psf_lengths).reshape(-1)
    start = (view_offsets - psf_lengths // 2).reshape(-1)
    field = field_rows.reshape(-1)
    z_pairs, y_pairs = swaps(tiles), swaps(blocks)

    z_near = [jnp.where(even_z == 1, depth - z_side, 0), jnp.where(even_z == 1, 0, depth - z_side)]
    y_near = [jnp.where(even_y == 1, rows - halo, 0), jnp.where(even_y == 1, 0, rows - halo)]

    def z_swap(values):
        return [lax.ppermute(value, "tile", pairs) for value, pairs in zip(values, z_pairs)]

    def y_swap(values):
        return [lax.ppermute(value, "view", pairs) for value, pairs in zip(values, y_pairs)]

    def z_slabs(value):
        return [lax.dynamic_slice_in_dim(value, at, z_side, 1) for at in z_near[: plan.z_stages]]

    def z_sum(own, side):
        sent = [side[:, i * z_side : (i + 1) * z_side] for i in range(plan.z_stages)]
        for got, at in zip(z_swap(sent), z_near):
            own = lax.dynamic_update_slice_in_dim(own, lax.dynamic_slice_in_dim(own, at, z_side, 1) + got, at, 1)
        return own

    def ends(value):
        return [value[rows : rows + halo], value[rows + halo :]]

    block = jnp.transpose(estimate, (1, 0, 2))
    got = y_swap([lax.dynamic_slice_in_dim(block, at, halo, 0) for at in y_near])
    own = jnp.concatenate([block] + got, axis=0)
    tables = bands(plan, where, start, weights)
    for turn in range(ITERS):
        side = jnp.concatenate(z_swap(z_slabs(own)), axis=1)
        summed, beyond = step(plan, where, field, background, own, side, tables, views)
        summed = z_sum(summed, beyond)
        if turn < ITERS - 1:
            near = [lax.dynamic_slice_in_dim(summed, at, halo, 0) for at in y_near]
            got = y_swap([jnp.concatenate([end, inner], axis=0) for end, inner in zip(ends(summed), near)])
            total = summed[:rows]
            for piece, inner, at in zip(got, near, y_near):
                total = lax.dynamic_update_slice_in_dim(total, inner + piece[:halo], at, 0)
            outer = [end + piece[halo:] for end, piece in zip(ends(summed), got)]
            own = own * jnp.concatenate([total] + outer, axis=0) / count
        else:
            got = y_swap(ends(summed))
            total = summed[:rows]
            for piece, at in zip(got, y_near):
                inner = lax.dynamic_slice_in_dim(total, at, halo, 0)
                total = lax.dynamic_update_slice_in_dim(total, inner + piece, at, 0)
            own = own[:rows] * total / count
    return jnp.transpose(own, (1, 0, 2))


def solution(mesh):
    in_specs = (P("tile", "view", None), P(None, "tile", "view", None), P(), P(), P(), P(), P())
    out_specs = P("tile", "view", None)
    return jax.shard_map(
        on_device, mesh=mesh, in_specs=in_specs, out_specs=out_specs, check_vma=False
    )
```

profile of v0, /device:TPU:16, one launch (start us, length us, event | category | flops | bytes accessed | tf_op | source)
XLA Modules:
  0.0 84.8 jit_solution(6573208713038831859)
XLA Ops:
  0.0 1.3 %copy.24 = f32[24,48,128]{2,0,1:T(8,128)S(1)} copy(f32[24,48,128]{2,1,0:T(8,128)} %param.7) | data formatting | bytes 1179648 | tf_op args[0]
  1.4 1.6 %collective-permute-start = (f32[9,24,128]{2,1,0:T(8,128)S(1)}, f32[9,24,128]{2,1,0:T(8,128)S(1)}, u32[]{:S(2)}, u32[]{:S(2)}) collective-permute-start(f32[9,24,128]{2,1,0:T(8,128)S(1)} %get-tuple-element.37), channel_id=1, source_target_pairs={{0,1},{1,0},{2,3},{3,2},{4,5},{5,4},{6,7},{7,6},{8,9},{9,8},{10,11... | collective-permute-start | bytes 331784 | tf_op jit(solution)/shard_map/ppermute | solution.py:298
  2.9 3.3 %collective-permute-start.1 = (f32[9,24,128]{2,1,0:T(8,128)S(1)}, f32[9,24,128]{2,1,0:T(8,128)S(1)}, u32[]{:S(2)}, u32[]{:S(2)}) collective-permute-start(f32[9,24,128]{2,1,0:T(8,128)S(1)} %get-tuple-element.38), channel_id=1, source_target_pairs={{1,2},{2,1},{3,4},{4,3},{5,6},{6,5},{7,8},{8,7},{9,10},{10,9},{11,... | collective-permute-start | bytes 331784 | tf_op jit(solution)/shard_map/ppermute | solution.py:298
  6.2 0.8 copy.20
  7.0 4.4 %collective-permute-done.1 = f32[9,24,128]{2,1,0:T(8,128)S(1)} collective-permute-done((f32[9,24,128]{2,1,0:T(8,128)S(1)}, f32[9,24,128]{2,1,0:T(8,128)S(1)}, u32[]{:S(2)}, u32[]{:S(2)}) %collective-permute-start.1) | collective-permute-done | bytes 110624 | tf_op jit(solution)/shard_map/ppermute | solution.py:298
  11.6 0.1 copy.19
  11.7 0.1 reshape.12.start_ref
  11.8 0.1 copy.18
  11.8 0.1 reshape.11.field_ref
  11.9 0.2 fusion.1
  12.1 0.1 reshape.13.taps_ref
  12.2 0.1 pad_add_fusion.where_ref
  12.3 2.4 %bands.1 = (bf16[144,144]{1,0:T(8,128)(2,1)S(1)}, bf16[48,432]{1,0:T(8,128)(2,1)S(1)}, bf16[6,48,240]{2,1,0:T(8,128)(2,1)S(1)}, bf16[6,80,144]{2,1,0:T(8,128)(2,...) custom-call(s32[3]{0:T(128)S(1)} %pad_add_fusion.where_ref, s32[18]{0:T(128)S(1)} %reshape.12.start_ref, ...), custom_call_target="tpu_custom_call" | custom-call | flops 10000000 | bytes 4000000 | tf_op jit(solution)/shard_map/bands/pallas_call | solution.py:145
  14.7 2.0 %copy-done = f32[6,24,48,128]{3,2,1,0:T(8,128)S(1)} copy-done((f32[6,24,48,128]{3,2,1,0:T(8,128)S(1)}, f32[6,24,48,128]{3,2,1,0:T(8,128)}, u32[]{:S(2)}) %copy-start) | copy-done | bytes 3538968
  16.7 16.5 %step.2 = (f32[66,24,128]{2,1,0:T(8,128)S(1)}, f32[66,16,128]{2,1,0:T(8,128)S(1)}) custom-call(s32[3]{0:T(128)S(1)} %pad_add_fusion.where_ref, s32[12]{0:T(128)S(1)} %reshape.11.field_ref, f32[6]{0:T(128)S(1)} %copy-done.2, f32[66,24,128]{2,1,0:T(8,128)S(1)} %pad_maximum_fusion.own_ref, f32[66,16,128]{2,1,0:T(8,128)S(1)} %collective-permute-done.2.side_ref, ...), custom_call_target="tpu_custom_call" | custom-call | flops 8000000000 | bytes 8000000 | tf_op jit(solution)/shard_map/step/pallas_call | solution.py:251
  33.2 0.5 collective-permute-start.3
  33.8 1.6 %collective-permute-done.3 = f32[66,16,128]{2,1,0:T(8,128)S(1)} collective-permute-done((f32[66,16,128]{2,1,0:T(8,128)S(1)}, f32[66,16,128]{2,1,0:T(8,128)S(1)}, u32[]{:S(2)}, u32[]{:S(2)}) %collective-permute-start.3) | collective-permute-done | bytes 540704 | tf_op jit(solution)/shard_map/ppermute | solution.py:295
  35.3 0.1 add_dynamic-update-slice_fusion.1
  35.6 7.7 %collective-permute-done.4 = f32[18,24,128]{2,1,0:T(8,128)S(1)} collective-permute-done((f32[18,24,128]{2,1,0:T(8,128)S(1)}, f32[18,24,128]{2,1,0:T(8,128)S(1)}, u32[]{:S(2)}, u32[]{:S(2)}) %collective-permute-start.4) | collective-permute-done | bytes 221216 | tf_op jit(solution)/shard_map/ppermute | solution.py:298
  43.4 3.3 %collective-permute-start.5 = (f32[18,24,128]{2,1,0:T(8,128)S(1)}, f32[18,24,128]{2,1,0:T(8,128)S(1)}, u32[]{:S(2)}, u32[]{:S(2)}) collective-permute-start(f32[18,24,128]{2,1,0:T(8,128)S(1)} %pad_maximum_fusion.2), channel_id=1, source_target_pairs={{1,2},{2,1},{3,4},{4,3},{5,6},{6,5},{7,8},{8,7},{9,10},{10,9},{11,... | collective-permute-start | bytes 663560 | tf_op jit(solution)/shard_map/ppermute | solution.py:298
  46.7 7.4 %collective-permute-done.5 = f32[18,24,128]{2,1,0:T(8,128)S(1)} collective-permute-done((f32[18,24,128]{2,1,0:T(8,128)S(1)}, f32[18,24,128]{2,1,0:T(8,128)S(1)}, u32[]{:S(2)}, u32[]{:S(2)}) %collective-permute-start.5) | collective-permute-done | bytes 221216 | tf_op jit(solution)/shard_map/ppermute | solution.py:298
  54.1 0.1 fusion.2.own_ref
  54.3 1.9 %collective-permute-done.6.side_ref = f32[66,16,128]{2,1,0:T(8,128)S(1)} collective-permute-done((f32[66,16,128]{2,1,0:T(8,128)S(1)}, f32[66,16,128]{2,1,0:T(8,128)S(1)}, u32[]{:S(2)}, u32[]{:S(2)}) %collective-permute-start.6) | collective-permute-done | bytes 540704 | tf_op jit(solution)/shard_map/ppermute | solution.py:295
  56.2 16.5 %step.3 = (f32[66,24,128]{2,1,0:T(8,128)S(1)}, f32[66,16,128]{2,1,0:T(8,128)S(1)}) custom-call(s32[3]{0:T(128)S(1)} %pad_add_fusion.where_ref, s32[12]{0:T(128)S(1)} %reshape.11.field_ref, f32[6]{0:T(128)S(1)} %copy-done.2, f32[66,24,128]{2,1,0:T(8,128)S(1)} %fusion.2.own_ref, f32[66,16,128]{2,1,0:T(8,128)S(1)} %collective-permute-done.6.side_ref, ...), custom_call_target="tpu_custom_call" | custom-call | flops 8000000000 | bytes 8000000 | tf_op jit(solution)/shard_map/step/pallas_call | solution.py:251
  72.7 0.2 collective-permute-start.7
  72.9 1.8 %collective-permute-done.7 = f32[66,16,128]{2,1,0:T(8,128)S(1)} collective-permute-done((f32[66,16,128]{2,1,0:T(8,128)S(1)}, f32[66,16,128]{2,1,0:T(8,128)S(1)}, u32[]{:S(2)}, u32[]{:S(2)}) %collective-permute-start.7) | collective-permute-done | bytes 540704 | tf_op jit(solution)/shard_map/ppermute | solution.py:295
  74.7 0.1 add_dynamic-update-slice_fusion
  75.0 3.3 %collective-permute-start.9 = (f32[9,24,128]{2,1,0:T(8,128)S(1)}, f32[9,24,128]{2,1,0:T(8,128)S(1)}, u32[]{:S(2)}, u32[]{:S(2)}) collective-permute-start(f32[9,24,128]{2,1,0:T(8,128)S(1)} %get-tuple-element.29), channel_id=1, source_target_pairs={{1,2},{2,1},{3,4},{4,3},{5,6},{6,5},{7,8},{8,7},{9,10},{10,9},{11,... | collective-permute-start | bytes 331784 | tf_op jit(solution)/shard_map/ppermute | solution.py:298
  78.3 1.8 %collective-permute-done.8 = f32[9,24,128]{2,1,0:T(8,128)S(1)} collective-permute-done((f32[9,24,128]{2,1,0:T(8,128)S(1)}, f32[9,24,128]{2,1,0:T(8,128)S(1)}, u32[]{:S(2)}, u32[]{:S(2)}) %collective-permute-start.8) | collective-permute-done | bytes 110624 | tf_op jit(solution)/shard_map/ppermute | solution.py:298
  80.1 3.7 %collective-permute-done.9 = f32[9,24,128]{2,1,0:T(8,128)S(1)} collective-permute-done((f32[9,24,128]{2,1,0:T(8,128)S(1)}, f32[9,24,128]{2,1,0:T(8,128)S(1)}, u32[]{:S(2)}, u32[]{:S(2)}) %collective-permute-start.9) | collective-permute-done | bytes 110624 | tf_op jit(solution)/shard_map/ppermute | solution.py:298
  83.8 0.1 fusion.4
  83.9 0.9 %copy.21 = f32[24,48,128]{2,1,0:T(8,128)} copy(f32[24,48,128]{2,0,1:T(8,128)S(1)} %fusion.4) | data formatting | bytes 1179648 | tf_op jit(solution)/shard_map/transpose | solution.py:335
  (34 shorter events, 0.8 us)
Async XLA Ops:
  0.0 11.5 %copy-start.3 = (s32[6,3]{0,1:T(4,128)S(1)}, s32[6,3]{0,1:T(4,128)}, u32[]{:S(2)}) copy-start(s32[6,3]{0,1:T(4,128)} %param.11) | copy-start | bytes 220
  0.0 11.6 %copy-start.4 = (s32[6,3]{0,1:T(4,128)S(1)}, s32[6,3]{0,1:T(4,128)}, u32[]{:S(2)}) copy-start(s32[6,3]{0,1:T(4,128)} %param.12) | copy-start | bytes 220
  0.0 11.8 %copy-start.5 = (s32[6,2]{0,1:T(2,128)S(1)}, s32[6,2]{0,1:T(2,128)}, u32[]{:S(2)}) copy-start(s32[6,2]{0,1:T(2,128)} %param.13) | copy-start | bytes 148
  0.0 11.9 %copy-start.6 = (f32[6,3,11]{2,1,0:T(4,128)S(1)}, f32[6,3,11]{2,1,0:T(4,128)}, u32[]{:S(2)}) copy-start(f32[6,3,11]{2,1,0:T(4,128)} %param.10) | copy-start | bytes 2380
  0.0 14.7 %copy-start.2 = (f32[6]{0:T(128)S(1)}, f32[6]{0:T(128)}, u32[]{:S(2)}) copy-start(f32[6]{0:T(128)} %level_ref.3) | copy-start | bytes 76
  1.4 5.6 %collective-permute-start = (f32[9,24,128]{2,1,0:T(8,128)S(1)}, f32[9,24,128]{2,1,0:T(8,128)S(1)}, u32[]{:S(2)}, u32[]{:S(2)}) collective-permute-start(f32[9,24,128]{2,1,0:T(8,128)S(1)} %get-tuple-element.37), channel_id=1, source_target_pairs={{0,1},{1,0},{2,3},{3,2},{4,5},{5,4},{6,7},{7,6},{8,9},{9,8},{10,11... | collective-permute-start | bytes 331784 | tf_op jit(solution)/shard_map/ppermute | solution.py:298
  2.9 8.4 %collective-permute-start.1 = (f32[9,24,128]{2,1,0:T(8,128)S(1)}, f32[9,24,128]{2,1,0:T(8,128)S(1)}, u32[]{:S(2)}, u32[]{:S(2)}) collective-permute-start(f32[9,24,128]{2,1,0:T(8,128)S(1)} %get-tuple-element.38), channel_id=1, source_target_pairs={{1,2},{2,1},{3,4},{4,3},{5,6},{6,5},{7,8},{8,7},{9,10},{10,9},{11,... | collective-permute-start | bytes 331784 | tf_op jit(solution)/shard_map/ppermute | solution.py:298
  11.5 3.2 %collective-permute-start.2 = (f32[66,16,128]{2,1,0:T(8,128)S(1)}, f32[66,16,128]{2,1,0:T(8,128)S(1)}, u32[]{:S(2)}, u32[]{:S(2)}) collective-permute-start(f32[66,16,128]{2,1,0:T(8,128)S(1)} %constant_dynamic-slice_fusion.3), channel_id=1, source_target_pairs={{0,16},{16,0},{1,17},{17,1},{2,18},{18,2},{3,19},{19,3},{4,20},{20... | collective-permute-start | bytes 1622024 | tf_op jit(solution)/shard_map/ppermute | solution.py:295
  14.7 2.0 %copy-start = (f32[6,24,48,128]{3,2,1,0:T(8,128)S(1)}, f32[6,24,48,128]{3,2,1,0:T(8,128)}, u32[]{:S(2)}) copy-start(f32[6,24,48,128]{3,2,1,0:T(8,128)} %views_hbm.3) | copy-start | bytes 10616836
  33.2 2.1 %collective-permute-start.3 = (f32[66,16,128]{2,1,0:T(8,128)S(1)}, f32[66,16,128]{2,1,0:T(8,128)S(1)}, u32[]{:S(2)}, u32[]{:S(2)}) collective-permute-start(f32[66,16,128]{2,1,0:T(8,128)S(1)} %get-tuple-element.22), channel_id=1, source_target_pairs={{0,16},{16,0},{1,17},{17,1},{2,18},{18,2},{3,19},{19,3},{4,20},{20... | collective-permute-start | bytes 1622024 | tf_op jit(solution)/shard_map/ppermute | solution.py:295
  35.5 20.8 %copy-start.1 = (f32[6,24,48,128]{3,2,1,0:T(8,128)S(1)}, f32[6,24,48,128]{3,2,1,0:T(8,128)}, u32[]{:S(2)}) copy-start(f32[6,24,48,128]{3,2,1,0:T(8,128)} %views_hbm.3) | copy-start | bytes 10616836
  35.5 7.8 %collective-permute-start.4 = (f32[18,24,128]{2,1,0:T(8,128)S(1)}, f32[18,24,128]{2,1,0:T(8,128)S(1)}, u32[]{:S(2)}, u32[]{:S(2)}) collective-permute-start(f32[18,24,128]{2,1,0:T(8,128)S(1)} %pad_maximum_fusion.1), channel_id=1, source_target_pairs={{0,1},{1,0},{2,3},{3,2},{4,5},{5,4},{6,7},{7,6},{8,9},{9,8},{10,11... | collective-permute-start | bytes 663560 | tf_op jit(solution)/shard_map/ppermute | solution.py:298
  43.4 10.7 %collective-permute-start.5 = (f32[18,24,128]{2,1,0:T(8,128)S(1)}, f32[18,24,128]{2,1,0:T(8,128)S(1)}, u32[]{:S(2)}, u32[]{:S(2)}) collective-permute-start(f32[18,24,128]{2,1,0:T(8,128)S(1)} %pad_maximum_fusion.2), channel_id=1, source_target_pairs={{1,2},{2,1},{3,4},{4,3},{5,6},{6,5},{7,8},{8,7},{9,10},{10,9},{11,... | collective-permute-start | bytes 663560 | tf_op jit(solution)/shard_map/ppermute | solution.py:298
  54.2 2.0 %collective-permute-start.6 = (f32[66,16,128]{2,1,0:T(8,128)S(1)}, f32[66,16,128]{2,1,0:T(8,128)S(1)}, u32[]{:S(2)}, u32[]{:S(2)}) collective-permute-start(f32[66,16,128]{2,1,0:T(8,128)S(1)} %constant_dynamic-slice_fusion), channel_id=1, source_target_pairs={{0,16},{16,0},{1,17},{17,1},{2,18},{18,2},{3,19},{19,3},{4,20},{20... | collective-permute-start | bytes 1622024 | tf_op jit(solution)/shard_map/ppermute | solution.py:295
  72.7 2.0 %collective-permute-start.7 = (f32[66,16,128]{2,1,0:T(8,128)S(1)}, f32[66,16,128]{2,1,0:T(8,128)S(1)}, u32[]{:S(2)}, u32[]{:S(2)}) collective-permute-start(f32[66,16,128]{2,1,0:T(8,128)S(1)} %get-tuple-element.24), channel_id=1, source_target_pairs={{0,16},{16,0},{1,17},{17,1},{2,18},{18,2},{3,19},{19,3},{4,20},{20... | collective-permute-start | bytes 1622024 | tf_op jit(solution)/shard_map/ppermute | solution.py:295
  74.9 5.2 %collective-permute-start.8 = (f32[9,24,128]{2,1,0:T(8,128)S(1)}, f32[9,24,128]{2,1,0:T(8,128)S(1)}, u32[]{:S(2)}, u32[]{:S(2)}) collective-permute-start(f32[9,24,128]{2,1,0:T(8,128)S(1)} %get-tuple-element.30), channel_id=1, source_target_pairs={{0,1},{1,0},{2,3},{3,2},{4,5},{5,4},{6,7},{7,6},{8,9},{9,8},{10,11... | collective-permute-start | bytes 331784 | tf_op jit(solution)/shard_map/ppermute | solution.py:298
  75.0 8.8 %collective-permute-start.9 = (f32[9,24,128]{2,1,0:T(8,128)S(1)}, f32[9,24,128]{2,1,0:T(8,128)S(1)}, u32[]{:S(2)}, u32[]{:S(2)}) collective-permute-start(f32[9,24,128]{2,1,0:T(8,128)S(1)} %get-tuple-element.29), channel_id=1, source_target_pairs={{1,2},{2,1},{3,4},{4,3},{5,6},{6,5},{7,8},{8,7},{9,10},{10,9},{11,... | collective-permute-start | bytes 331784 | tf_op jit(solution)/shard_map/ppermute | solution.py:298
where the time goes:
time: 85.1 us; the launch traced here: 84.8 us
  Pallas kernels  35.4 us (42%)
  waiting for transfers between devices  30.2 us (35%)
  starting transfers between devices  12.4 us (15%)
  local copies, waits for them, and re-layouts  5.68 us (7%)
  other arithmetic  0.86 us (1%)
    pallas_call x2, Pallas kernels, step(): pl.pallas_call(functools.partial(step_kernel, plan), out_shape=[jax.Shape...  32.9 us
    ppermute x6, waiting for transfers between devices, y_swap(): lax.ppermute(value, 'view', pairs)  24.9 us
    ppermute x6, starting transfers between devices, y_swap(): lax.ppermute(value, 'view', pairs)  11.5 us
    ppermute x4, waiting for transfers between devices, z_swap(): lax.ppermute(value, 'tile', pairs)  5.29 us
    unnamed x17, local copies, waits for them, and re-layouts  4.17 us
    pallas_call x1, Pallas kernels, bands(): pl.pallas_call(functools.partial(bands_kernel, plan), out_shape=[jax.Shap...  2.42 us
  transfers between devices with their start and end apart: 10, of which 8 were waited for; matrix products, arithmetic and copies ran while one was open for 2% of the time, Pallas kernels for 3%

commit v1 on v0

v1 whole, which is shorter than its diff:
```python
import functools

import jax
import jax.numpy as jnp
from jax import lax
from jax.experimental import pallas as pl
from jax.experimental.pallas import tpu as pltpu
from jax.sharding import PartitionSpec as P

ITERS = 2
HALO = 9
FAR = 1 << 20
UNROLL = 11
F32 = jnp.float32
BF16 = jnp.bfloat16


def up(size, unit):
    return -(-size // unit) * unit


class Plan:
    def __init__(self, views, taps, depth, rows, lanes, tiles):
        self.views, self.taps, self.depth, self.rows, self.lanes = views, taps, depth, rows, lanes
        self.z_stages = 1 if tiles == 2 else 2
        self.z_side = up(HALO, 8)
        self.z_used = depth + self.z_side * self.z_stages
        self.z_slots = up(self.z_used, 16)
        self.y_edge = 4 * HALO
        self.y_used = rows + 2 * HALO
        self.y_slots = up(self.y_used, 16)
        self.pitch = self.y_slots + (8 if (self.y_slots // 8) % 2 == 0 else 0)
        self.stack = views * depth

    def length_at(self, v, d):
        return 3 + v * 3 + d

    def offset_at(self, v, d):
        return 3 + self.views * 3 + v * 3 + d

    def field_at(self, v, end):
        return 3 + self.views * 6 + v * 2 + end

    def tap_at(self, v, d, k):
        return self.views + (v * 3 + d) * self.taps + k


def swaps(count):
    first, second = [], []
    for i in range(0, count - 1, 2):
        first += [(i, i + 1), (i + 1, i)]
    for i in range(1, count - 1, 2):
        second += [(i, i + 1), (i + 1, i)]
    return first, second


def split(value):
    high = value.astype(BF16)
    return high, (value - high.astype(F32)).astype(BF16)


def three(value):
    high, low = split(value)
    return jnp.concatenate([high, low, high], axis=0)


def dot(a, b):
    return jnp.dot(a, b, preferred_element_type=F32)


def z_place(plan, slot, even):
    own, side = plan.depth, plan.z_side
    after, before = slot, slot - own - side
    first = jnp.where(even == 1, after, before)
    second = jnp.where(even == 1, before - side, after - side)
    far = jnp.full_like(slot, FAR)
    last = jnp.where(slot < own + 2 * side, second, far) if plan.z_stages == 2 else far
    return jnp.where(slot < own, slot, jnp.where(slot < own + side, first, last))


def y_first_rows(plan, even):
    rows = plan.rows
    return [
        jnp.where(even == 1, rows, -HALO),
        jnp.where(even == 1, -HALO, rows),
        jnp.where(even == 1, rows - HALO, 0),
        jnp.where(even == 1, 0, rows - HALO),
        HALO,
    ]


def y_place(plan, slot, even):
    place = jnp.full_like(slot, FAR)
    begins = [0, HALO, 2 * HALO, 3 * HALO, 4 * HALO, plan.y_used]
    for begin, end, row in zip(begins, begins[1:], y_first_rows(plan, even)):
        place = jnp.where((slot >= begin) & (slot < end), slot - begin + row, place)
    return place


def bands_kernel(plan, ints, floats, zf_ref, za_ref, yf_ref, ya_ref, xf_ref, xa_ref, zf_wide):
    views, depth, rows, lanes, taps = plan.views, plan.depth, plan.rows, plan.lanes, plan.taps
    even_z, even_y = ints[0], ints[1]

    def start(v, d):
        return ints[plan.offset_at(v, d)] - ints[plan.length_at(v, d)] // 2

    def kernel(v, d):
        length = ints[plan.length_at(v, d)]
        raw = [jnp.where(k < length, floats[plan.tap_at(v, d, k)], 0.0) for k in range(taps)]
        total = raw[0]
        for one in raw[1:]:
            total = total + one
        return raw, 1.0 / jnp.full((1, lanes), total, F32)[:, :1]

    def banded(v, d, delta):
        raw, scale = kernel(v, d)
        value = jnp.zeros(delta.shape, F32)
        for k in range(taps):
            value = jnp.where(delta == k, raw[k], value)
        return value * scale

    def parted(value, low):
        high = value.astype(BF16).astype(F32)
        return jnp.where(low, value - high, high)

    def columns(count, period):
        column = lax.broadcasted_iota(jnp.int32, (1, count * period), 1)
        part = jnp.zeros_like(column)
        for i in range(1, count):
            part = part + (column >= i * period).astype(jnp.int32)
        return part, column - part * period

    part, slot = columns(3, plan.z_slots)
    z_in = z_place(plan, slot, even_z)
    z_out = lax.broadcasted_iota(jnp.int32, (depth, 1), 0)
    for v in range(views):
        value = banded(v, 0, z_in - z_out - start(v, 0))
        zf_wide[v * depth : (v + 1) * depth, :] = parted(value, part == 2)
    zf_ref[...] = zf_wide[...].astype(BF16)

    part, column = columns(3, plan.stack)
    view = jnp.zeros_like(column)
    for v in range(1, views):
        view = view + (column >= v * depth).astype(jnp.int32)
    begin = jnp.zeros_like(column)
    for v in range(views):
        begin = jnp.where(view == v, start(v, 0), begin)
    slot = lax.broadcasted_iota(jnp.int32, (plan.z_slots, 1), 0)
    delta = z_place(plan, slot, even_z) - (column - view * depth + begin)
    kernels = [kernel(v, 0) for v in range(views)]
    value = jnp.zeros(delta.shape, F32)
    for k in range(taps):
        row = jnp.zeros(column.shape, F32)
        for v in range(views):
            row = jnp.where(view == v, kernels[v][0][k] * kernels[v][1], row)
        value = jnp.where(delta == k, row, value)
    za_ref[...] = parted(value, part == 2).astype(BF16)

    def of_view(v, carry):
        part, slot = columns(3, plan.y_slots)
        y_out = lax.broadcasted_iota(jnp.int32, (rows, 1), 0)
        value = banded(v, 1, y_place(plan, slot, even_y) - y_out - start(v, 1))
        yf_ref[v] = parted(value, part == 2).astype(BF16)

        part, y_in = columns(3, rows)
        slot = lax.broadcasted_iota(jnp.int32, (plan.y_slots, 1), 0)
        value = banded(v, 1, y_place(plan, slot, even_y) - y_in - start(v, 1))
        ya_ref[v] = parted(value, part == 2).astype(BF16)

        x_in = lax.broadcasted_iota(jnp.int32, (lanes, lanes), 0)
        x_out = lax.broadcasted_iota(jnp.int32, (lanes, lanes), 1)
        for ref, delta in ((xf_ref, x_in - x_out), (xa_ref, x_out - x_in)):
            high, low = split(banded(v, 2, delta - start(v, 2)))
            ref[v, :, :lanes] = high
            ref[v, :, lanes:] = low
        return carry

    lax.fori_loop(0, views, of_view, 0)


SMEM = pl.BlockSpec(memory_space=pltpu.SMEM)
VMEM = pl.BlockSpec(memory_space=pltpu.VMEM)


def call(body, name, operands, specs, shapes, scratch=(), megabytes=16, flops=1_000_000):
    return pl.pallas_call(
        body,
        out_shape=[jax.ShapeDtypeStruct(*shape) for shape in shapes],
        in_specs=specs,
        out_specs=[VMEM] * len(shapes),
        scratch_shapes=list(scratch),
        compiler_params=pltpu.CompilerParams(vmem_limit_bytes=megabytes << 20),
        cost_estimate=pl.CostEstimate(flops=flops, bytes_accessed=2_000_000, transcendentals=0),
        name=name,
    )(*operands)


def bands(plan, ints, floats):
    views, lanes = plan.views, plan.lanes
    shapes = (
        (plan.stack, 3 * plan.z_slots),
        (plan.z_slots, 3 * plan.stack),
        (views, plan.rows, 3 * plan.y_slots),
        (views, plan.y_slots, 3 * plan.rows),
        (views, lanes, 2 * lanes),
        (views, lanes, 2 * lanes),
    )
    return call(
        functools.partial(bands_kernel, plan), "bands", (ints, floats), [SMEM] * 2, [(shape, BF16) for shape in shapes],
        scratch=[pltpu.VMEM(shapes[0], F32)], flops=2_000_000_000,
    )


def loop(count, body):
    unroll = max(d for d in range(1, UNROLL + 1) if count % d == 0)

    def run(i, carry):
        body(i)
        return carry

    lax.fori_loop(0, count, run, 0, unroll=unroll)


def z_forward(plan, own_ref, side_ref, zf_ref, grid_ref, first, count):
    lanes = plan.lanes

    def pair(at):
        parts = []
        for i in range(2):
            y = first + at * 2 + i
            pieces = [own_ref[y], side_ref[y]]
            if plan.z_slots > plan.z_used:
                pieces.append(jnp.zeros((plan.z_slots - plan.z_used, lanes), F32))
            parts.append(three(jnp.concatenate(pieces, axis=0)))
        out = dot(zf_ref[...], jnp.concatenate(parts, axis=1))
        for i in range(2):
            y = first + at * 2 + i
            grid_ref[pl.ds(y, plan.stack, stride=plan.pitch), :] = out[:, i * lanes : (i + 1) * lanes]

    loop(count // 2, pair)


def z_adjoint(plan, grid_ref, za_ref, own_out, side_out, first, count):
    lanes, depth = plan.lanes, plan.depth

    def pair(at):
        parts = [three(grid_ref[pl.ds(first + at * 2 + i, plan.stack, stride=plan.pitch), :]) for i in range(2)]
        out = dot(za_ref[...], jnp.concatenate(parts, axis=1))
        for i in range(2):
            value = out[:, i * lanes : (i + 1) * lanes]
            own_out[at * 2 + i] = value[:depth]
            side_out[at * 2 + i] = value[depth : plan.z_used]

    loop(count // 2, pair)


def clear_rest(plan, grid_ref):
    begin = plan.y_used // 8 * 8
    blank = jnp.zeros((plan.y_slots - begin, plan.lanes), F32)

    def one(i):
        grid_ref[pl.ds(i * plan.pitch + begin, blank.shape[0]), :] = blank

    loop(plan.stack, one)


def of_views(plan, ints, floats, yf_ref, ya_ref, xf_ref, xa_ref, views_ref, grid_ref, arrived):
    views, depth, rows, lanes = plan.views, plan.depth, plan.rows, plan.lanes
    pitch, y_slots = plan.pitch, plan.y_slots

    def of_view(v, carry):
        arrived(v)
        lower, upper = ints[plan.field_at(v, 0)], ints[plan.field_at(v, 1)]
        y = ints[2] + lax.broadcasted_iota(jnp.int32, (rows, lanes), 0)
        covered = (y >= lower) & (y < upper)
        lane_forward = jnp.concatenate([xf_ref[v]] * 2, axis=0)
        lane_adjoint = jnp.concatenate([xa_ref[v]] * 2, axis=0)

        def along_x(value, matrix):
            out = dot(jnp.concatenate(split(value), axis=1), matrix)
            return out[:, :lanes] + out[:, lanes:]

        base = pl.multiple_of(v * depth * pitch, 8)
        spread = []
        for z in range(0, depth, 2):
            parts = [three(grid_ref[pl.ds(base + (z + i) * pitch, y_slots), :]) for i in range(2)]
            out = dot(yf_ref[v], jnp.concatenate(parts, axis=1))
            spread += [out[:, :lanes], out[:, lanes:]]
        blurred = along_x(jnp.concatenate(spread, axis=0), lane_forward).reshape(depth, rows, lanes)
        ratio = jnp.where(covered[None], views_ref[v] / (blurred + floats[v]), 1.0)
        back = along_x(ratio.reshape(depth * rows, lanes), lane_adjoint)
        for z in range(0, depth, 2):
            parts = [three(back[(z + i) * rows : (z + i + 1) * rows]) for i in range(2)]
            out = dot(ya_ref[v], jnp.concatenate(parts, axis=1))
            for i in range(2):
                grid_ref[pl.ds(base + (z + i) * pitch, y_slots), :] = out[:, i * lanes : (i + 1) * lanes]
        return carry

    lax.fori_loop(0, views, of_view, 0)


def start_views(plan, views_hbm, views_ref, sems):
    def fetch(v):
        return pltpu.make_async_copy(views_hbm.at[v], views_ref.at[v], sems.at[v])

    for v in range(plan.views):
        fetch(v).start()
    return lambda v: fetch(v).wait()


def step_kernel(
    plan, ints, floats, own_ref, side_ref, zf_ref, za_ref, yf_ref, ya_ref, xf_ref, xa_ref, views_hbm, own_out, side_out,
    grid_ref, views_ref, sems,
):
    arrived = start_views(plan, views_hbm, views_ref, sems)
    clear_rest(plan, grid_ref)
    z_forward(plan, own_ref, side_ref, zf_ref, grid_ref, 0, plan.y_used)
    of_views(plan, ints, floats, yf_ref, ya_ref, xf_ref, xa_ref, views_ref, grid_ref, arrived)
    z_adjoint(plan, grid_ref, za_ref, own_out, side_out, 0, plan.y_used)


def first_step_kernel(
    plan, ints, floats, block_ref, block_side_ref, first_ref, second_ref, corner_ref, zf_ref, za_ref, yf_ref, ya_ref, xf_ref, xa_ref,
    views_hbm, own_out, side_out, own_ref, grid_ref, side_ref, views_ref, sems,
):
    arrived = start_views(plan, views_hbm, views_ref, sems)
    clear_rest(plan, grid_ref)
    depth, rows, sides = plan.depth, plan.rows, plan.z_used - plan.depth
    own_ref[:HALO] = first_ref[...]
    own_ref[HALO : 2 * HALO] = second_ref[...]
    side_ref[: 2 * HALO] = corner_ref[...]
    begins = [2 * HALO, 3 * HALO, 4 * HALO, plan.y_used]
    for begin, end, row in zip(begins, begins[1:], y_first_rows(plan, ints[1])[2:]):
        for i in range(end - begin):
            own_ref[begin + i] = block_ref[pl.ds(row + i, depth, stride=rows), :]
            side_ref[begin + i] = block_side_ref[pl.ds(row + i, sides, stride=rows), :]
    z_forward(plan, own_ref, side_ref, zf_ref, grid_ref, 0, plan.y_used)
    of_views(plan, ints, floats, yf_ref, ya_ref, xf_ref, xa_ref, views_ref, grid_ref, arrived)
    z_adjoint(plan, grid_ref, za_ref, own_out, side_out, 0, plan.y_used)


HBM = pl.BlockSpec(memory_space=pltpu.HBM)


def step(plan, ints, floats, own, side, tables, views):
    lanes = plan.lanes
    first = isinstance(own, (list, tuple))
    operands = list(own) if first else [own, side]
    used = (plan.y_used, plan.depth, lanes)
    shapes = [(used, F32), ((plan.y_used, plan.z_used - plan.depth, lanes), F32)] + ([(used, F32)] if first else [])
    scratch = [pltpu.VMEM((plan.stack * plan.pitch, lanes), F32)]
    scratch += [pltpu.VMEM(shapes[1][0], F32)] if first else []
    scratch += [pltpu.VMEM(views.shape, F32), pltpu.SemaphoreType.DMA((plan.views,))]
    return call(
        functools.partial(first_step_kernel if first else step_kernel, plan), "first_step" if first else "step",
        (ints, floats, *operands, *tables, views), [SMEM] * 2 + [VMEM] * (len(operands) + len(tables)) + [HBM], shapes,
        scratch=scratch, megabytes=40, flops=8_000_000_000,
    )


def add_sides(plan, even_z, piece, got_refs, at, count):
    depth, side = plan.depth, plan.z_side
    value = piece
    near = [even_z == 1, even_z != 1]
    for ref, last in zip(got_refs, near):
        got = ref[at : at + count]
        blank = jnp.zeros((count, depth - side, plan.lanes), F32)
        value = value + jnp.where(last, jnp.concatenate([blank, got], axis=1), jnp.concatenate([got, blank], axis=1))
    return value


def sums_kernel(plan, own_halo, ints, summed_ref, *refs):
    got_refs, (out_ref, first_ref, second_ref) = refs[: plan.z_stages], refs[plan.z_stages :]
    for at in range(0, plan.y_used, HALO):
        count = min(HALO, plan.y_used - at)
        out_ref[at : at + count] = add_sides(plan, ints[0], summed_ref[at : at + count], got_refs, at, count)
    for ref, i in ((first_ref, 0), (second_ref, 1)):
        ref[:HALO] = out_ref[i * HALO : (i + 1) * HALO]
        if own_halo:
            ref[HALO:] = out_ref[(i + 2) * HALO : (i + 3) * HALO]


def sums(plan, own_halo, ints, summed, got):
    used, sent = (plan.y_used, plan.depth, plan.lanes), (HALO * (2 if own_halo else 1), plan.depth, plan.lanes)
    return call(
        functools.partial(sums_kernel, plan, own_halo), "sums", (ints, summed, *got), [SMEM] + [VMEM] * (1 + len(got)),
        [(used, F32), (sent, F32), (sent, F32)],
    )


def next_kernel(plan, ints, own_ref, summed_ref, first_ref, second_ref, out_ref, *side_refs):
    scale = 1.0 / plan.views
    for i, ref in ((0, first_ref), (1, second_ref)):
        a, b = i * HALO, (i + 2) * HALO
        out_ref[a : a + HALO] = own_ref[a : a + HALO] * (summed_ref[a : a + HALO] + ref[HALO:]) * scale
        out_ref[b : b + HALO] = own_ref[b : b + HALO] * (summed_ref[b : b + HALO] + ref[:HALO]) * scale
    rest = 4 * HALO
    out_ref[rest:] = own_ref[rest:] * summed_ref[rest:] * scale
    depth, side = plan.depth, plan.z_side
    for ref, last in zip(side_refs, (ints[0] == 1, ints[0] != 1)):
        ref[...] = jnp.where(last, out_ref[:, depth - side :], out_ref[:, :side])


def next_estimate(plan, ints, own, summed, got):
    used, side = (plan.y_used, plan.depth, plan.lanes), (plan.y_used, plan.z_side, plan.lanes)
    return call(
        functools.partial(next_kernel, plan), "next", (ints, own, summed, *got), [SMEM] + [VMEM] * 4,
        [(used, F32)] + [(side, F32)] * plan.z_stages,
    )


def last_kernel(plan, ints, own_ref, summed_ref, first_ref, second_ref, out_ref):
    scale = 1.0 / plan.views
    begins = [2 * HALO, 3 * HALO, 4 * HALO, plan.y_used]
    for begin, end, row, got in zip(begins, begins[1:], y_first_rows(plan, ints[1])[2:], (first_ref, second_ref, None)):
        for i in range(end - begin):
            total = summed_ref[begin + i]
            if got is not None:
                total = total + got[i]
            out_ref[pl.ds(row + i, plan.depth, stride=plan.rows), :] = own_ref[begin + i] * total * scale


def last_estimate(plan, ints, own, summed, got):
    shape = (plan.depth * plan.rows, plan.lanes)
    out = call(functools.partial(last_kernel, plan), "last", (ints, own, summed, *got), [SMEM] + [VMEM] * 4, [(shape, F32)])
    return out[0].reshape(plan.depth, plan.rows, plan.lanes)


def on_device(estimate, views, background, psf_taps, psf_lengths, view_offsets, field_rows):
    depth, rows, lanes = estimate.shape
    tiles, blocks = lax.axis_size("tile"), lax.axis_size("view")
    plan = Plan(views.shape[0], psf_taps.shape[2], depth, rows, lanes, tiles)
    side = plan.z_side
    tile_at, view_at = lax.axis_index("tile"), lax.axis_index("view")
    even_z, even_y = 1 - tile_at % 2, 1 - view_at % 2
    where = jnp.stack([even_z, even_y, view_at * rows]).astype(jnp.int32)
    ints = jnp.concatenate([where, psf_lengths.reshape(-1), view_offsets.reshape(-1), field_rows.reshape(-1)])
    floats = jnp.concatenate([background, psf_taps.reshape(-1)])
    z_pairs, y_pairs = swaps(tiles), swaps(blocks)

    def z_swap(values):
        return [lax.ppermute(value, "tile", pairs) for value, pairs in zip(values, z_pairs)]

    def y_swap(values):
        second = lax.ppermute(values[1], "view", y_pairs[1])
        return [lax.ppermute(values[0], "view", y_pairs[0]), second]

    near = [lax.dynamic_slice_in_dim(estimate, row, HALO, 1).transpose(1, 0, 2) for row in y_first_rows(plan, even_y)[2:4]]
    got = y_swap(near)
    z_near = [jnp.where(even_z == 1, depth - side, 0), jnp.where(even_z == 1, 0, depth - side)][: plan.z_stages]
    block_side = jnp.concatenate(z_swap([lax.dynamic_slice_in_dim(estimate, at, side, 0) for at in z_near]), axis=0)
    tables = bands(plan, ints, floats)
    halo = jnp.concatenate(got, axis=0)
    halo, tables = lax.optimization_barrier((halo, tables))
    corner = jnp.concatenate(z_swap([lax.dynamic_slice_in_dim(halo, at, side, 1) for at in z_near]), axis=1)
    own = (estimate.reshape(depth * rows, lanes), block_side.reshape(-1, lanes), *got, corner)
    summed, beyond, own = step(plan, ints, floats, own, None, tables, views)
    for turn in range(1, ITERS + 1):
        sent = [beyond[:, i * side : (i + 1) * side] for i in range(plan.z_stages)]
        summed, *ends = sums(plan, turn < ITERS, ints, summed, z_swap(sent))
        got = y_swap(ends)
        if turn == ITERS:
            return last_estimate(plan, ints, own, summed, got)
        own, *sent = next_estimate(plan, ints, own, summed, got)
        summed, beyond = step(plan, ints, floats, own, jnp.concatenate(z_swap(sent), axis=1), tables, views)


def solution(mesh):
    in_specs = (P("tile", "view", None), P(None, "tile", "view", None), P(), P(), P(), P(), P())
    out_specs = P("tile", "view", None)
    return jax.shard_map(
        on_device, mesh=mesh, in_specs=in_specs, out_specs=out_specs, check_vma=False
    )
```

time: 85.1 us -> 70.5 us (0.83)
  waiting for transfers between devices: 30.2 us -> 21.1 us
  Pallas kernels: 35.4 us -> 27.5 us
  starting transfers between devices: 12.4 us -> 15 us
    ppermute x6, waiting for transfers between devices: 24.9 us -> 14.8 us  [the longest x3 8.43 us: y_swap(): return [lax.ppermute(values[0], 'view', y_pairs[0]), second]]
    pallas_call x3 -> x7, Pallas kernels: 35.4 us -> 27.5 us  [call(): pl.pallas_call(body, out_shape=[jax.ShapeDtypeStruct(*shape) for shape in...]
    ppermute x6, starting transfers between devices: 11.5 us -> 13.7 us  [the longest x3 8.1 us: y_swap(): second = lax.ppermute(values[1], 'view', y_pairs[1])]
    dynamic_slice x3, local copies, waits for them, and re-layouts: 0.13 us -> 2.1 us  [the longest x1 1.06 us: on_device(): lax.dynamic_slice_in_dim(estimate, row, HALO, 1).transpose(1, 0, 2)]
    unnamed x17 -> x9, local copies, waits for them, and re-layouts: 4.17 us -> 2.39 us
    ppermute x4 -> x5, waiting for transfers between devices: 5.29 us -> 6.3 us  [z_swap(): lax.ppermute(value, 'tile', pairs)]
    transpose x1 -> x0, local copies, waits for them, and re-layouts: 0.92 us -> none  [on_device(): return jnp.transpose(own, (1, 0, 2))]
  transfers between devices with their start and end apart: 10 -> 11, of which waited for: 8 -> 8; matrix products, arithmetic and copies ran while one was open for 2% -> 7% of each run, Pallas kernels for 3% -> 4%
where the time goes in v1:
time: 70.5 us; the launch traced here: 70.1 us
  Pallas kernels  27.5 us (39%)
  waiting for transfers between devices  21.1 us (30%)
  starting transfers between devices  15 us (21%)
  local copies, waits for them, and re-layouts  5.61 us (8%)
  other arithmetic  0.75 us (1%)
    pallas_call x7, Pallas kernels, call(): pl.pallas_call(body, out_shape=[jax.ShapeDtypeStruct(*shape) for shape in...  27.5 us
    ppermute x3, waiting for transfers between devices, y_swap(): return [lax.ppermute(values[0], 'view', y_pairs[0]), second]  8.43 us
    ppermute x3, starting transfers between devices, y_swap(): second = lax.ppermute(values[1], 'view', y_pairs[1])  8.1 us
    ppermute x3, waiting for transfers between devices, y_swap(): second = lax.ppermute(values[1], 'view', y_pairs[1])  6.39 us
    ppermute x5, waiting for transfers between devices, z_swap(): lax.ppermute(value, 'tile', pairs)  6.3 us
    ppermute x3, starting transfers between devices, y_swap(): return [lax.ppermute(values[0], 'view', y_pairs[0]), second]  5.6 us
    unnamed x9, local copies, waits for them, and re-layouts  2.39 us
  transfers between devices with their start and end apart: 11, of which 8 were waited for; matrix products, arithmetic and copies ran while one was open for 7% of the time, Pallas kernels for 4%

profile of v1, /device:TPU:16, one launch (start us, length us, event | category | flops | bytes accessed | tf_op | source)
XLA Modules:
  0.0 70.1 jit_solution(18371990345795993996)
XLA Ops:
  0.0 1.1 %constant_dynamic-slice_fusion.1 = (f32[24,9,128]{2,1,0:T(8,128)S(1)}, f32[24,9,128]{2,1,0:T(8,128)S(1)}) fusion(f32[24,48,128]{2,1,0:T(8,128)} %param.7, s32[]{:T(128)S(6)} %select_n.29, s32[]{:T(128)S(6)} %select_n.28), kind=kLoop, calls=%fused_computation.5 | loop fusion | bytes 442376 | tf_op jit(solution)/shard_map/dynamic_slice | solution.py:448
  1.1 1.6 %collective-permute-start.1 = (f32[9,24,128]{2,1,0:T(8,128)S(1)}, f32[9,24,128]{2,1,0:T(8,128)S(1)}, u32[]{:S(2)}, u32[]{:S(2)}) collective-permute-start(f32[9,24,128]{2,1,0:T(8,128)S(1)} %bitcast.14), channel_id=1, source_target_pairs={{0,1},{1,0},{2,3},{3,2},{4,5},{5,4},{6,7},{7,6},{8,9},{9,8},{10,11... | collective-permute-start | bytes 331784 | tf_op jit(solution)/shard_map/ppermute | solution.py:446
  2.8 3.2 %collective-permute-start.2 = (f32[9,24,128]{2,1,0:T(8,128)S(1)}, f32[9,24,128]{2,1,0:T(8,128)S(1)}, u32[]{:S(2)}, u32[]{:S(2)}) collective-permute-start(f32[9,24,128]{2,1,0:T(8,128)S(1)} %bitcast.15), channel_id=1, source_target_pairs={{1,2},{2,1},{3,4},{4,3},{5,6},{6,5},{7,8},{8,7},{9,10},{10,9},{11,... | collective-permute-start | bytes 331784 | tf_op jit(solution)/shard_map/ppermute | solution.py:445
  6.0 1.0 %constant_dynamic-slice_fusion.3 = f32[16,48,128]{2,1,0:T(8,128)S(1)} fusion(f32[24,48,128]{2,1,0:T(8,128)} %param.7, s32[]{:T(128)S(6)} %select_n.27), kind=kLoop, calls=%fused_computation.7 | loop fusion | bytes 786436 | tf_op jit(solution)/shard_map/dynamic_slice | solution.py:451
  7.1 0.8 %reshape.24 = f32[198]{0:T(256)S(1)} reshape(f32[6,3,11]{2,1,0:T(4,128)} %param.10) | data formatting | bytes 1584 | tf_op jit(solution)/shard_map/reshape | solution.py:438
  7.9 0.8 %copy.13 = s32[6,3]{1,0:T(8,128)S(1)} copy(s32[6,3]{0,1:T(4,128)} %param.11) | data formatting | bytes 144 | tf_op args[4]
  8.7 0.1 reshape.21
  8.8 0.8 %copy.14 = s32[6,3]{1,0:T(8,128)S(1)} copy(s32[6,3]{0,1:T(4,128)} %param.12) | data formatting | bytes 144 | tf_op args[5]
  9.6 0.8 %copy.15 = s32[6,2]{1,0:T(8,128)S(1)} copy(s32[6,2]{0,1:T(2,128)} %param.13) | data formatting | bytes 96 | tf_op args[6]
  10.5 0.7 %pad_maximum_fusion.1.floats = f32[204]{0:T(256)S(1)} fusion(f32[198]{0:T(256)S(1)} %reshape.24, f32[6]{0:T(128)} %param.9), kind=kLoop, calls=%fused_computation.3 | loop fusion | flops 204 | bytes 1632 | tf_op jit(solution)/shard_map/concatenate | solution.py:438
  11.3 2.6 %bands.1 = (bf16[144,144]{1,0:T(8,128)(2,1)S(1)}, bf16[48,432]{1,0:T(8,128)(2,1)S(1)}, bf16[6,48,240]{2,1,0:T(8,128)(2,1)S(1)}, bf16[6,80,144]{2,1,0:T(8,128)(2,...) custom-call(s32[51]{0:T(128)S(1)} %concatenate.9.ints, f32[204]{0:T(256)S(1)} %pad_maximum_fusion.1.floats), custom_call_target="tpu_custom_call" | custom-call | flops 2000000000 | bytes 2000000 | tf_op jit(solution)/shard_map/bands/pallas_call | solution.py:186
  14.0 0.6 collective-permute-start.3
  14.5 1.0 %collective-permute-done.3.corner_ref = f32[18,16,128]{2,1,0:T(8,128)S(1)} collective-permute-done((f32[18,16,128]{2,1,0:T(8,128)S(1)}, f32[18,16,128]{2,1,0:T(8,128)S(1)}, u32[]{:S(2)}, u32[]{:S(2)}) %collective-permute-start.3) | collective-permute-done | bytes 147488 | tf_op jit(solution)/shard_map/ppermute | solution.py:442
  15.5 10.8 %first_step.1 = (f32[66,24,128]{2,1,0:T(8,128)S(1)}, f32[66,16,128]{2,1,0:T(8,128)S(1)}, f32[66,24,128]{2,1,0:T(8,128)S(1)}) custom-call(s32[51]{0:T(128)S(1)} %concatenate.9.ints, f32[204]{0:T(256)S(1)} %pad_maximum_fusion.1.floats, f32[1152,128]{1,0:T(8,128)S(1)} %bitcast.12, f32[768,128]{1,0:T(8,128)S(1)} %bitcast.13, ...), custom_call_target="tpu_custom_call" | custom-call | flops 8000000000 | bytes 2000000 | tf_op jit(solution)/shard_map/first_step/pallas_call | solution.py:186
  26.3 0.4 collective-permute-start.4
  26.7 1.6 %collective-permute-done.4.refs_0_ = f32[66,16,128]{2,1,0:T(8,128)S(1)} collective-permute-done((f32[66,16,128]{2,1,0:T(8,128)S(1)}, f32[66,16,128]{2,1,0:T(8,128)S(1)}, u32[]{:S(2)}, u32[]{:S(2)}) %collective-permute-start.4) | collective-permute-done | bytes 540704 | tf_op jit(solution)/shard_map/ppermute | solution.py:442
  28.3 0.7 sums.2
  29.0 1.7 %collective-permute-start.5 = (f32[18,24,128]{2,1,0:T(8,128)S(1)}, f32[18,24,128]{2,1,0:T(8,128)S(1)}, u32[]{:S(2)}, u32[]{:S(2)}) collective-permute-start(f32[18,24,128]{2,1,0:T(8,128)S(1)} %get-tuple-element.48), channel_id=1, source_target_pairs={{0,1},{1,0},{2,3},{3,2},{4,5},{5,4},{6,7},{7,6},{8,9},{9,8},{10,11... | collective-permute-start | bytes 663560 | tf_op jit(solution)/shard_map/ppermute | solution.py:446
  30.7 2.8 %collective-permute-start.6 = (f32[18,24,128]{2,1,0:T(8,128)S(1)}, f32[18,24,128]{2,1,0:T(8,128)S(1)}, u32[]{:S(2)}, u32[]{:S(2)}) collective-permute-start(f32[18,24,128]{2,1,0:T(8,128)S(1)} %get-tuple-element.49), channel_id=1, source_target_pairs={{1,2},{2,1},{3,4},{4,3},{5,6},{6,5},{7,8},{8,7},{9,10},{10,9},{11,... | collective-permute-start | bytes 663560 | tf_op jit(solution)/shard_map/ppermute | solution.py:445
  33.5 7.2 %collective-permute-done.5.first_ref = f32[18,24,128]{2,1,0:T(8,128)S(1)} collective-permute-done((f32[18,24,128]{2,1,0:T(8,128)S(1)}, f32[18,24,128]{2,1,0:T(8,128)S(1)}, u32[]{:S(2)}, u32[]{:S(2)}) %collective-permute-start.5) | collective-permute-done | bytes 221216 | tf_op jit(solution)/shard_map/ppermute | solution.py:446
  40.7 1.2 %collective-permute-done.6.second_ref = f32[18,24,128]{2,1,0:T(8,128)S(1)} collective-permute-done((f32[18,24,128]{2,1,0:T(8,128)S(1)}, f32[18,24,128]{2,1,0:T(8,128)S(1)}, u32[]{:S(2)}, u32[]{:S(2)}) %collective-permute-start.6) | collective-permute-done | bytes 221216 | tf_op jit(solution)/shard_map/ppermute | solution.py:445
  41.9 0.7 %next.1 = (f32[66,24,128]{2,1,0:T(8,128)S(1)}, f32[66,16,128]{2,1,0:T(8,128)S(1)}) custom-call(s32[51]{0:T(128)S(1)} %concatenate.9.ints, f32[66,24,128]{2,1,0:T(8,128)S(1)} %get-tuple-element.44.own_ref, f32[66,24,128]{2,1,0:T(8,128)S(1)} %get-tuple-element.47.summed_ref, f32[18,24,128]{2,1,0:T(8,128)S(1)} %collective-permute-done.5.first_ref, ...), custom_call_target="tpu_custom_call" | custom-call | flops 1000000 | bytes 2000000 | tf_op jit(solution)/shard_map/next/pallas_call | solution.py:186
  42.7 1.9 %collective-permute-done.7.side_ref = f32[66,16,128]{2,1,0:T(8,128)S(1)} collective-permute-done((f32[66,16,128]{2,1,0:T(8,128)S(1)}, f32[66,16,128]{2,1,0:T(8,128)S(1)}, u32[]{:S(2)}, u32[]{:S(2)}) %collective-permute-start.7) | collective-permute-done | bytes 540704 | tf_op jit(solution)/shard_map/ppermute | solution.py:442
  44.6 10.4 %step.1 = (f32[66,24,128]{2,1,0:T(8,128)S(1)}, f32[66,16,128]{2,1,0:T(8,128)S(1)}) custom-call(s32[51]{0:T(128)S(1)} %concatenate.9.ints, f32[204]{0:T(256)S(1)} %pad_maximum_fusion.1.floats, f32[66,24,128]{2,1,0:T(8,128)S(1)} %get-tuple-element.50.own_ref, f32[66,16,128]{2,1,0:T(8,128)S(1)} %collective-permute-done.7.side_ref, ...), custom_call_target="tpu_custom_call" | custom-call | flops 8000000000 | bytes 2000000 | tf_op jit(solution)/shard_map/step/pallas_call | solution.py:186
  55.1 0.2 collective-permute-start.8
  55.3 1.8 %collective-permute-done.8.refs_0_ = f32[66,16,128]{2,1,0:T(8,128)S(1)} collective-permute-done((f32[66,16,128]{2,1,0:T(8,128)S(1)}, f32[66,16,128]{2,1,0:T(8,128)S(1)}, u32[]{:S(2)}, u32[]{:S(2)}) %collective-permute-start.8) | collective-permute-done | bytes 540704 | tf_op jit(solution)/shard_map/ppermute | solution.py:442
  57.1 0.6 sums.3
  57.7 2.3 %collective-permute-start.9 = (f32[9,24,128]{2,1,0:T(8,128)S(1)}, f32[9,24,128]{2,1,0:T(8,128)S(1)}, u32[]{:S(2)}, u32[]{:S(2)}) collective-permute-start(f32[9,24,128]{2,1,0:T(8,128)S(1)} %get-tuple-element.55), channel_id=1, source_target_pairs={{0,1},{1,0},{2,3},{3,2},{4,5},{5,4},{6,7},{7,6},{8,9},{9,8},{10,11... | collective-permute-start | bytes 331784 | tf_op jit(solution)/shard_map/ppermute | solution.py:446
  60.0 2.1 %collective-permute-start.10 = (f32[9,24,128]{2,1,0:T(8,128)S(1)}, f32[9,24,128]{2,1,0:T(8,128)S(1)}, u32[]{:S(2)}, u32[]{:S(2)}) collective-permute-start(f32[9,24,128]{2,1,0:T(8,128)S(1)} %get-tuple-element.56), channel_id=1, source_target_pairs={{1,2},{2,1},{3,4},{4,3},{5,6},{6,5},{7,8},{8,7},{9,10},{10,9},{11,... | collective-permute-start | bytes 331784 | tf_op jit(solution)/shard_map/ppermute | solution.py:445
  62.1 1.3 %collective-permute-done.9.first_ref = f32[9,24,128]{2,1,0:T(8,128)S(1)} collective-permute-done((f32[9,24,128]{2,1,0:T(8,128)S(1)}, f32[9,24,128]{2,1,0:T(8,128)S(1)}, u32[]{:S(2)}, u32[]{:S(2)}) %collective-permute-start.9) | collective-permute-done | bytes 110624 | tf_op jit(solution)/shard_map/ppermute | solution.py:446
  63.3 5.1 %collective-permute-done.10.second_ref = f32[9,24,128]{2,1,0:T(8,128)S(1)} collective-permute-done((f32[9,24,128]{2,1,0:T(8,128)S(1)}, f32[9,24,128]{2,1,0:T(8,128)S(1)}, u32[]{:S(2)}, u32[]{:S(2)}) %collective-permute-start.10) | collective-permute-done | bytes 110624 | tf_op jit(solution)/shard_map/ppermute | solution.py:445
  68.5 1.6 %last.1 = f32[1152,128]{1,0:T(8,128)} custom-call(s32[51]{0:T(128)S(1)} %concatenate.9.ints, f32[66,24,128]{2,1,0:T(8,128)S(1)} %get-tuple-element.50.own_ref, f32[66,24,128]{2,1,0:T(8,128)S(1)} %get-tuple-element.54.summed_ref, f32[9,24,128]{2,1,0:T(8,128)S(1)} %collective-permute-done.9.first_ref, f32[9,24,128]{2,1,0:T(8,128)S(1)} %collective-permute-done.10.second_ref), custom_call_target="tpu_custom_call" | custom-call | flops 1000000 | bytes 2000000 | tf_op jit(solution)/shard_map/last/pallas_call | solution.py:186
  (16 shorter events, 0.5 us)
Async XLA Ops:
  1.1 12.8 %collective-permute-start.1 = (f32[9,24,128]{2,1,0:T(8,128)S(1)}, f32[9,24,128]{2,1,0:T(8,128)S(1)}, u32[]{:S(2)}, u32[]{:S(2)}) collective-permute-start(f32[9,24,128]{2,1,0:T(8,128)S(1)} %bitcast.14), channel_id=1, source_target_pairs={{0,1},{1,0},{2,3},{3,2},{4,5},{5,4},{6,7},{7,6},{8,9},{9,8},{10,11... | collective-permute-start | bytes 331784 | tf_op jit(solution)/shard_map/ppermute | solution.py:446
  2.8 11.2 %collective-permute-start.2 = (f32[9,24,128]{2,1,0:T(8,128)S(1)}, f32[9,24,128]{2,1,0:T(8,128)S(1)}, u32[]{:S(2)}, u32[]{:S(2)}) collective-permute-start(f32[9,24,128]{2,1,0:T(8,128)S(1)} %bitcast.15), channel_id=1, source_target_pairs={{1,2},{2,1},{3,4},{4,3},{5,6},{6,5},{7,8},{8,7},{9,10},{10,9},{11,... | collective-permute-start | bytes 331784 | tf_op jit(solution)/shard_map/ppermute | solution.py:445
  7.0 8.5 %collective-permute-start = (f32[16,48,128]{2,1,0:T(8,128)S(1)}, f32[16,48,128]{2,1,0:T(8,128)S(1)}, u32[]{:S(2)}, u32[]{:S(2)}) collective-permute-start(f32[16,48,128]{2,1,0:T(8,128)S(1)} %constant_dynamic-slice_fusion.3), channel_id=1, source_target_pairs={{0,16},{16,0},{1,17},{17,1},{2,18},{18,2},{3,19},{19,3},{4,20},{20... | collective-permute-start | bytes 1179656 | tf_op jit(solution)/shard_map/ppermute | solution.py:442
  11.3 4.3 %copy-start = (f32[24,48,128]{2,1,0:T(8,128)S(1)}, f32[24,48,128]{2,1,0:T(8,128)}, u32[]{:S(2)}) copy-start(f32[24,48,128]{2,1,0:T(8,128)} %param.7) | copy-start | bytes 1769476
  11.3 4.3 %copy-start.1 = (f32[6,24,48,128]{3,2,1,0:T(8,128)S(1)}, f32[6,24,48,128]{3,2,1,0:T(8,128)}, u32[]{:S(2)}) copy-start(f32[6,24,48,128]{3,2,1,0:T(8,128)} %views_hbm.3) | copy-start | bytes 10616836
  14.0 1.6 %collective-permute-start.3 = (f32[18,16,128]{2,1,0:T(8,128)S(1)}, f32[18,16,128]{2,1,0:T(8,128)S(1)}, u32[]{:S(2)}, u32[]{:S(2)}) collective-permute-start(f32[18,16,128]{2,1,0:T(8,128)S(1)} %constant_dynamic-slice_fusion), channel_id=1, source_target_pairs={{0,16},{16,0},{1,17},{17,1},{2,18},{18,2},{3,19},{19,3},{4,20},{20... | collective-permute-start | bytes 442376 | tf_op jit(solution)/shard_map/ppermute | solution.py:442
  26.3 2.0 %collective-permute-start.4 = (f32[66,16,128]{2,1,0:T(8,128)S(1)}, f32[66,16,128]{2,1,0:T(8,128)S(1)}, u32[]{:S(2)}, u32[]{:S(2)}) collective-permute-start(f32[66,16,128]{2,1,0:T(8,128)S(1)} %get-tuple-element.46), channel_id=1, source_target_pairs={{0,16},{16,0},{1,17},{17,1},{2,18},{18,2},{3,19},{19,3},{4,20},{20... | collective-permute-start | bytes 1622024 | tf_op jit(solution)/shard_map/ppermute | solution.py:442
  29.0 11.7 %collective-permute-start.5 = (f32[18,24,128]{2,1,0:T(8,128)S(1)}, f32[18,24,128]{2,1,0:T(8,128)S(1)}, u32[]{:S(2)}, u32[]{:S(2)}) collective-permute-start(f32[18,24,128]{2,1,0:T(8,128)S(1)} %get-tuple-element.48), channel_id=1, source_target_pairs={{0,1},{1,0},{2,3},{3,2},{4,5},{5,4},{6,7},{7,6},{8,9},{9,8},{10,11... | collective-permute-start | bytes 663560 | tf_op jit(solution)/shard_map/ppermute | solution.py:446
  30.7 11.2 %collective-permute-start.6 = (f32[18,24,128]{2,1,0:T(8,128)S(1)}, f32[18,24,128]{2,1,0:T(8,128)S(1)}, u32[]{:S(2)}, u32[]{:S(2)}) collective-permute-start(f32[18,24,128]{2,1,0:T(8,128)S(1)} %get-tuple-element.49), channel_id=1, source_target_pairs={{1,2},{2,1},{3,4},{4,3},{5,6},{6,5},{7,8},{8,7},{9,10},{10,9},{11,... | collective-permute-start | bytes 663560 | tf_op jit(solution)/shard_map/ppermute | solution.py:445
  42.6 2.0 %collective-permute-start.7 = (f32[66,16,128]{2,1,0:T(8,128)S(1)}, f32[66,16,128]{2,1,0:T(8,128)S(1)}, u32[]{:S(2)}, u32[]{:S(2)}) collective-permute-start(f32[66,16,128]{2,1,0:T(8,128)S(1)} %get-tuple-element.51), channel_id=1, source_target_pairs={{0,16},{16,0},{1,17},{17,1},{2,18},{18,2},{3,19},{19,3},{4,20},{20... | collective-permute-start | bytes 1622024 | tf_op jit(solution)/shard_map/ppermute | solution.py:442
  55.1 2.0 %collective-permute-start.8 = (f32[66,16,128]{2,1,0:T(8,128)S(1)}, f32[66,16,128]{2,1,0:T(8,128)S(1)}, u32[]{:S(2)}, u32[]{:S(2)}) collective-permute-start(f32[66,16,128]{2,1,0:T(8,128)S(1)} %get-tuple-element.53), channel_id=1, source_target_pairs={{0,16},{16,0},{1,17},{17,1},{2,18},{18,2},{3,19},{19,3},{4,20},{20... | collective-permute-start | bytes 1622024 | tf_op jit(solution)/shard_map/ppermute | solution.py:442
  57.7 5.6 %collective-permute-start.9 = (f32[9,24,128]{2,1,0:T(8,128)S(1)}, f32[9,24,128]{2,1,0:T(8,128)S(1)}, u32[]{:S(2)}, u32[]{:S(2)}) collective-permute-start(f32[9,24,128]{2,1,0:T(8,128)S(1)} %get-tuple-element.55), channel_id=1, source_target_pairs={{0,1},{1,0},{2,3},{3,2},{4,5},{5,4},{6,7},{7,6},{8,9},{9,8},{10,11... | collective-permute-start | bytes 331784 | tf_op jit(solution)/shard_map/ppermute | solution.py:446
  60.0 8.5 %collective-permute-start.10 = (f32[9,24,128]{2,1,0:T(8,128)S(1)}, f32[9,24,128]{2,1,0:T(8,128)S(1)}, u32[]{:S(2)}, u32[]{:S(2)}) collective-permute-start(f32[9,24,128]{2,1,0:T(8,128)S(1)} %get-tuple-element.56), channel_id=1, source_target_pairs={{1,2},{2,1},{3,4},{4,3},{5,6},{6,5},{7,8},{8,7},{9,10},{10,9},{11,... | collective-permute-start | bytes 331784 | tf_op jit(solution)/shard_map/ppermute | solution.py:445

commit v2 on v1

v2 whole, which is shorter than its diff:
```python
import functools

import jax
import jax.numpy as jnp
from jax import lax
from jax.experimental import pallas as pl
from jax.experimental.pallas import tpu as pltpu
from jax.sharding import PartitionSpec as P

ITERS = 2
HALO = 9
FAR = 1 << 20
UNROLL = 18
F32 = jnp.float32
BF16 = jnp.bfloat16


def up(size, unit):
    return -(-size // unit) * unit


def odd_tiles(count):
    return count + (8 if (count // 8) % 2 == 0 else 0)


class Plan:
    def __init__(self, views, taps, depth, rows, lanes, tiles):
        self.views, self.taps, self.depth, self.rows, self.lanes = views, taps, depth, rows, lanes
        self.z_stages = 1 if tiles == 2 else 2
        self.z_side = up(HALO, 8)
        self.z_used = depth + self.z_side * self.z_stages
        self.z_slots = up(self.z_used, 16)
        self.y_edge = 4 * HALO
        self.y_inner = rows - 2 * HALO
        self.edge_pad, self.inner_pad = up(self.y_edge, 8), up(self.y_inner, 8)
        self.y_slots = up(self.edge_pad + self.inner_pad, 16)
        self.edge_pitch, self.inner_pitch = odd_tiles(self.edge_pad), odd_tiles(self.inner_pad)
        self.stack = views * depth


def swaps(count):
    first, second = [], []
    for i in range(0, count - 1, 2):
        first += [(i, i + 1), (i + 1, i)]
    for i in range(1, count - 1, 2):
        second += [(i, i + 1), (i + 1, i)]
    return first, second


def split(value):
    high = value.astype(BF16)
    return high, (value - high.astype(F32)).astype(BF16)


def two(value):
    return jnp.concatenate(split(value), axis=0)


def three(value):
    high, low = split(value)
    return jnp.concatenate([high, low, high], axis=0)


def dot(a, b):
    return jnp.dot(a, b, preferred_element_type=F32)


def z_place(plan, slot, even):
    own, side = plan.depth, plan.z_side
    after, before = slot, slot - own - side
    first = jnp.where(even == 1, after, before)
    second = jnp.where(even == 1, before - side, after - side)
    far = jnp.full_like(slot, FAR)
    last = jnp.where(slot < own + 2 * side, second, far) if plan.z_stages == 2 else far
    return jnp.where(slot < own, slot, jnp.where(slot < own + side, first, last))


def y_first_rows(plan, even):
    rows = plan.rows
    return [
        jnp.where(even == 1, rows, -HALO),
        jnp.where(even == 1, -HALO, rows),
        jnp.where(even == 1, rows - HALO, 0),
        jnp.where(even == 1, 0, rows - HALO),
        HALO,
    ]


def y_place(plan, slot, even):
    place = jnp.full_like(slot, FAR)
    begins = [0, HALO, 2 * HALO, 3 * HALO, plan.edge_pad]
    ends = [HALO, 2 * HALO, 3 * HALO, 4 * HALO, plan.edge_pad + plan.y_inner]
    for begin, end, row in zip(begins, ends, y_first_rows(plan, even)):
        place = jnp.where((slot >= begin) & (slot < end), slot - begin + row, place)
    return place


def evens():
    return 1 - lax.axis_index("tile") % 2, 1 - lax.axis_index("view") % 2


def bands_kernel(
    plan, lengths_hbm, offsets_hbm, taps_hbm, zf_ref, za_ref, yf_ref, ya_ref, xf_ref, xa_ref, zf_wide, lengths, offsets, tap_table, sems,
):
    pairs = ((lengths_hbm, lengths), (offsets_hbm, offsets), (taps_hbm, tap_table))
    copies = [pltpu.make_async_copy(source, target, sems.at[i]) for i, (source, target) in enumerate(pairs)]
    for copy in copies:
        copy.start()
    for copy in copies:
        copy.wait()
    views, depth, rows, lanes, taps = plan.views, plan.depth, plan.rows, plan.lanes, plan.taps
    even_z, even_y = evens()

    def start(v, d):
        return offsets[d, v] - lengths[d, v] // 2

    def kernel(v, d):
        length = lengths[d, v]
        raw = [jnp.where(k < length, tap_table[v, d, k], 0.0) for k in range(taps)]
        total = raw[0]
        for one in raw[1:]:
            total = total + one
        return raw, 1.0 / jnp.full((1, lanes), total, F32)[:, :1]

    def banded(v, d, delta):
        raw, scale = kernel(v, d)
        value = jnp.zeros(delta.shape, F32)
        for k in range(taps):
            value = jnp.where(delta == k, raw[k], value)
        return value * scale

    def parted(value, low):
        high = value.astype(BF16).astype(F32)
        return jnp.where(low, value - high, high)

    def columns(count, period):
        column = lax.broadcasted_iota(jnp.int32, (1, count * period), 1)
        part = jnp.zeros_like(column)
        for i in range(1, count):
            part = part + (column >= i * period).astype(jnp.int32)
        return part, column - part * period

    part, slot = columns(3, plan.z_slots)
    z_in = z_place(plan, slot, even_z)
    z_out = lax.broadcasted_iota(jnp.int32, (depth, 1), 0)
    for v in range(views):
        value = banded(v, 0, z_in - z_out - start(v, 0))
        zf_wide[v * depth : (v + 1) * depth, :] = parted(value, part == 2)
    zf_ref[...] = zf_wide[...].astype(BF16)

    column = columns(1, plan.stack)[1]
    view = jnp.zeros_like(column)
    for v in range(1, views):
        view = view + (column >= v * depth).astype(jnp.int32)
    begin = jnp.zeros_like(column)
    for v in range(views):
        begin = jnp.where(view == v, start(v, 0), begin)
    slot = lax.broadcasted_iota(jnp.int32, (plan.z_slots, 1), 0)
    delta = z_place(plan, slot, even_z) - (column - view * depth + begin)
    kernels = [kernel(v, 0) for v in range(views)]
    value = jnp.zeros(delta.shape, F32)
    for k in range(taps):
        row = jnp.zeros(column.shape, F32)
        for v in range(views):
            row = jnp.where(view == v, kernels[v][0][k] * kernels[v][1], row)
        value = jnp.where(delta == k, row, value)
    za_ref[: plan.z_slots], za_ref[plan.z_slots :] = split(value)

    def of_view(v, carry):
        slot = columns(2, plan.y_slots)[1]
        y_out = lax.broadcasted_iota(jnp.int32, (rows, 1), 0)
        high, low = split(banded(v, 1, y_place(plan, slot, even_y) - y_out - start(v, 1)))
        yf_ref[v, :rows] = high
        yf_ref[v, rows:] = low

        part, y_in = columns(3, rows)
        slot = lax.broadcasted_iota(jnp.int32, (plan.y_slots, 1), 0)
        value = banded(v, 1, y_place(plan, slot, even_y) - y_in - start(v, 1))
        ya_ref[v] = parted(value, part == 2).astype(BF16)

        x_in = lax.broadcasted_iota(jnp.int32, (lanes, lanes), 0)
        x_out = lax.broadcasted_iota(jnp.int32, (lanes, lanes), 1)
        for ref, delta in ((xf_ref, x_in - x_out), (xa_ref, x_out - x_in)):
            high, low = split(banded(v, 2, delta - start(v, 2)))
            ref[v, :, :lanes] = high
            ref[v, :, lanes:] = low
        return carry

    lax.fori_loop(0, views, of_view, 0)


SMEM = pl.BlockSpec(memory_space=pltpu.SMEM)
VMEM = pl.BlockSpec(memory_space=pltpu.VMEM)
HBM = pl.BlockSpec(memory_space=pltpu.HBM)


def call(body, operands, shapes, scalars=0, in_hbm=0, scratch=(), megabytes=24, flops=1_000):
    return pl.pallas_call(
        body,
        out_shape=[jax.ShapeDtypeStruct(*shape) for shape in shapes],
        in_specs=[SMEM] * scalars + [HBM] * in_hbm + [VMEM] * (len(operands) - scalars - in_hbm),
        out_specs=[VMEM] * len(shapes),
        scratch_shapes=list(scratch),
        compiler_params=pltpu.CompilerParams(vmem_limit_bytes=megabytes << 20),
        cost_estimate=pl.CostEstimate(flops=flops, bytes_accessed=flops, transcendentals=0),
        name=(body.func if hasattr(body, "func") else body).__name__,
    )(*operands)


def bands(plan, lengths, offsets, taps):
    views, lanes = plan.views, plan.lanes
    shapes = (
        (plan.stack, 3 * plan.z_slots),
        (2 * plan.z_slots, plan.stack),
        (views, 2 * plan.rows, 2 * plan.y_slots),
        (views, plan.y_slots, 3 * plan.rows),
        (views, lanes, 2 * lanes),
        (views, lanes, 2 * lanes),
    )
    return call(
        functools.partial(bands_kernel, plan), (lengths, offsets, taps), [(shape, BF16) for shape in shapes], in_hbm=3,
        scratch=[pltpu.VMEM(shapes[0], F32)] + [pltpu.SMEM(v.shape, v.dtype) for v in (lengths, offsets, taps)] + [pltpu.SemaphoreType.DMA((3,))],
        flops=1_000,
    )


def loop(count, body):
    unroll = max(d for d in range(1, UNROLL + 1) if count % d == 0)

    def run(i, carry):
        body(i)
        return carry

    lax.fori_loop(0, count, run, 0, unroll=unroll)


def z_forward(plan, own_ref, side_refs, zf_ref, grid_ref, pitch):
    lanes = plan.lanes

    def pair(at):
        parts = []
        for i in range(2):
            y = at * 2 + i
            pieces = [own_ref[y]] + [ref[y] for ref in side_refs]
            if plan.z_slots > plan.z_used:
                pieces.append(jnp.zeros((plan.z_slots - plan.z_used, lanes), F32))
            parts.append(three(jnp.concatenate(pieces, axis=0)))
        out = dot(zf_ref[...], jnp.concatenate(parts, axis=1))
        for i in range(2):
            grid_ref[pl.ds(at * 2 + i, plan.stack, stride=pitch), :] = out[:, i * lanes : (i + 1) * lanes]

    loop(own_ref.shape[0] // 2, pair)


def z_adjoint(plan, grid_ref, za_ref, own_out, side_outs, pitch):
    lanes, depth, side = plan.lanes, plan.depth, plan.z_side

    def pair(at):
        parts = [split(grid_ref[pl.ds(at * 2 + i, plan.stack, stride=pitch), :]) for i in range(2)]
        high, low = (jnp.concatenate(pieces, axis=1) for pieces in zip(*parts))
        both = dot(za_ref[...], high)
        out = both[: plan.z_slots] + both[plan.z_slots :] + dot(za_ref[: plan.z_slots], low)
        for i in range(2):
            value = out[:, i * lanes : (i + 1) * lanes]
            own_out[at * 2 + i] = value[:depth]
            for stage, ref in enumerate(side_outs):
                ref[at * 2 + i] = value[depth + stage * side : depth + (stage + 1) * side]

    loop(own_out.shape[0] // 2, pair)


def clear_rest(plan, grid_ref, used, padded, pitch):
    begin = used // 8 * 8
    if begin == padded:
        return
    blank = jnp.zeros((padded - begin, plan.lanes), F32)

    def one(i):
        grid_ref[pl.ds(i * pitch + begin, padded - begin), :] = blank

    loop(plan.stack, one)


def of_views(plan, field, level, yf_ref, ya_ref, xf_ref, xa_ref, views_ref, edge_ref, inner_in, inner_out):
    views, depth, rows, lanes = plan.views, plan.depth, plan.rows, plan.lanes
    edge, inner, y_slots = plan.edge_pad, plan.inner_pad, plan.y_slots

    def of_view(v, carry):
        lower, upper = field[0, v], field[1, v]
        y = lax.axis_index("view") * rows + lax.broadcasted_iota(jnp.int32, (rows, lanes), 0)
        covered = (y >= lower) & (y < upper)
        lane_forward = jnp.concatenate([xf_ref[v]] * 2, axis=0)
        lane_adjoint = jnp.concatenate([xa_ref[v]] * 2, axis=0)

        def along_x(value, matrix):
            out = dot(jnp.concatenate(split(value), axis=1), matrix)
            return out[:, :lanes] + out[:, lanes:]

        edge_base = pl.multiple_of(v * depth * plan.edge_pitch, 8)
        inner_base = pl.multiple_of(v * depth * plan.inner_pitch, 8)

        def edge_at(z):
            return pl.ds(edge_base + z * plan.edge_pitch, edge)

        def inner_at(z):
            return pl.ds(inner_base + z * plan.inner_pitch, inner)

        def slots(z):
            pieces = [edge_ref[edge_at(z), :], inner_in[inner_at(z), :]]
            if y_slots > edge + inner:
                pieces.append(jnp.zeros((y_slots - edge - inner, lanes), F32))
            return two(jnp.concatenate(pieces, axis=0))

        spread = []
        for z in range(0, depth, 2):
            parts = [slots(z + i) for i in range(2)]
            out = dot(yf_ref[v], jnp.concatenate(parts, axis=1))
            out = out[:rows] + out[rows:]
            spread += [out[:, :lanes], out[:, lanes:]]
        blurred = along_x(jnp.concatenate(spread, axis=0), lane_forward).reshape(depth, rows, lanes)
        ratio = jnp.where(covered[None], views_ref[v] / (blurred + level[v]), 1.0)
        back = along_x(ratio.reshape(depth * rows, lanes), lane_adjoint)
        for z in range(0, depth, 2):
            parts = [three(back[(z + i) * rows : (z + i + 1) * rows]) for i in range(2)]
            out = dot(ya_ref[v], jnp.concatenate(parts, axis=1))
            for i in range(2):
                edge_ref[edge_at(z + i), :] = out[:edge, i * lanes : (i + 1) * lanes]
                inner_out[inner_at(z + i), :] = out[edge : edge + inner, i * lanes : (i + 1) * lanes]
        return carry

    lax.fori_loop(0, views, of_view, 0, unroll=True)


def edges_kernel(plan, block_ref, first_ref, second_ref, inner_ref, *side_refs):
    even_z, even_y = evens()
    depth, rows, side = plan.depth, plan.rows, plan.z_side
    lasts = (even_z == 1, even_z != 1)
    for at, count, row, out_ref in (
        (0, HALO, y_first_rows(plan, even_y)[2], first_ref),
        (HALO, HALO, y_first_rows(plan, even_y)[3], second_ref),
        (2 * HALO, plan.y_inner, HALO, inner_ref),
    ):
        for i in range(count):
            value = block_ref[pl.ds(row + i, depth, stride=rows), :]
            out_ref[i] = value
            for ref, last in zip(side_refs, lasts):
                ref[at + i] = jnp.where(last, value[depth - side :], value[:side])


def grow_kernel(plan, inner_ref, zf_ref, *refs):
    side_refs, (grid_ref,) = refs[: plan.z_stages], refs[plan.z_stages :]
    clear_rest(plan, grid_ref, plan.y_inner, plan.inner_pad, plan.inner_pitch)
    z_forward(plan, inner_ref, side_refs, zf_ref, grid_ref, plan.inner_pitch)


def main_kernel(plan, inner_first, field, level, own_ref, zf_ref, za_ref, yf_ref, ya_ref, xf_ref, xa_ref, views_ref, inner_in, *refs):
    side_refs, (grid_out, own_out, *side_outs), grid_kept = refs[: plan.z_stages], refs[plan.z_stages : -1], refs[-1]
    edge_ref, inner_out = (grid_out, grid_kept) if inner_first else (grid_kept, grid_out)
    clear_rest(plan, edge_ref, plan.y_edge, plan.edge_pad, plan.edge_pitch)
    z_forward(plan, own_ref, side_refs, zf_ref, edge_ref, plan.edge_pitch)
    of_views(plan, field, level, yf_ref, ya_ref, xf_ref, xa_ref, views_ref, edge_ref, inner_in, inner_out)
    z_adjoint(plan, grid_kept, za_ref, own_out, side_outs, plan.inner_pitch if inner_first else plan.edge_pitch)


def rest_kernel(plan, pitch, grid_ref, za_ref, own_out, *side_outs):
    z_adjoint(plan, grid_ref, za_ref, own_out, side_outs, pitch)


def add_sides(plan, ref, got_refs, at, count):
    depth, side = plan.depth, plan.z_side
    even_z = evens()[0]
    value = ref[at : at + count]
    blank = jnp.zeros((count, depth - side, plan.lanes), F32)
    for got_ref, last in zip(got_refs, (even_z == 1, even_z != 1)):
        got = got_ref[at : at + count]
        value = value + jnp.where(last, jnp.concatenate([blank, got], axis=1), jnp.concatenate([got, blank], axis=1))
    return value


def sums_kernel(plan, own_halo, summed_ref, *refs):
    got_refs, (out_ref, first_ref, second_ref) = refs[: plan.z_stages], refs[plan.z_stages :]
    for i, ref in enumerate((first_ref, second_ref, first_ref, second_ref)):
        value = add_sides(plan, summed_ref, got_refs, i * HALO, HALO)
        out_ref[i * HALO : (i + 1) * HALO] = value
        if i < 2:
            ref[:HALO] = value
        elif own_halo:
            ref[HALO:] = value


def near_side(plan, value, stage):
    even_z = evens()[0]
    last = (even_z == 1, even_z != 1)[stage]
    return jnp.where(last, value[:, plan.depth - plan.z_side :], value[:, : plan.z_side])


def next_inner_kernel(plan, own_ref, summed_ref, *refs):
    got_refs, (out_ref, *side_refs) = refs[: plan.z_stages], refs[plan.z_stages :]
    for at in range(0, own_ref.shape[0], HALO + 1):
        end = min(at + HALO + 1, own_ref.shape[0])
        value = own_ref[at:end] * add_sides(plan, summed_ref, got_refs, at, end - at) * (1.0 / plan.views)
        out_ref[at:end] = value
        for stage, ref in enumerate(side_refs):
            ref[at:end] = near_side(plan, value, stage)


def next_edge_kernel(plan, own_ref, summed_ref, first_ref, second_ref, out_ref, *side_refs):
    for i, ref in enumerate((first_ref, second_ref, first_ref, second_ref)):
        a, b = i * HALO, (i + 1) * HALO
        got = ref[HALO:] if i < 2 else ref[:HALO]
        value = own_ref[a:b] * (summed_ref[a:b] + got) * (1.0 / plan.views)
        out_ref[a:b] = value
        for stage, side in enumerate(side_refs):
            side[a:b] = near_side(plan, value, stage)


def last_kernel(plan, edge_ref, inner_ref, summed_edge_ref, summed_inner_ref, first_ref, second_ref, *refs):
    got_refs, (out_ref,) = refs[: plan.z_stages], refs[plan.z_stages :]
    scale = 1.0 / plan.views
    first_row, second_row, inner_row = y_first_rows(plan, evens()[1])[2:]

    def put(row, value):
        out_ref[pl.ds(row, plan.depth, stride=plan.rows), :] = value

    for ref, row, at in ((first_ref, first_row, 2 * HALO), (second_ref, second_row, 3 * HALO)):
        for i in range(HALO):
            put(row + i, edge_ref[at + i] * (summed_edge_ref[at + i] + ref[i]) * scale)
    for i in range(inner_ref.shape[0]):
        total = add_sides(plan, summed_inner_ref, got_refs, i, 1)[0]
        put(inner_row + i, inner_ref[i] * total * scale)


def on_device(estimate, views, background, psf_taps, psf_lengths, view_offsets, field_rows):
    depth, rows, lanes = estimate.shape
    tiles, blocks = lax.axis_size("tile"), lax.axis_size("view")
    plan = Plan(views.shape[0], psf_taps.shape[2], depth, rows, lanes, tiles)
    z_pairs, y_pairs = swaps(tiles), swaps(blocks)
    side, stages, edge, inner = plan.z_side, plan.z_stages, plan.y_edge, plan.y_inner
    inner_grid = ((plan.stack * plan.inner_pitch, lanes), F32)
    edge_grid = ((plan.stack * plan.edge_pitch, lanes), F32)
    field = field_rows.T

    def own_of(count):
        return ((count, depth, lanes), F32)

    def sides_of(count):
        return [((count, side, lanes), F32)] * stages

    def run(body, operands, shapes, *static, **more):
        return call(functools.partial(body, plan, *static), operands, shapes, **more)

    def z_swap(values):
        return [lax.ppermute(value, "tile", pairs) for value, pairs in zip(values, z_pairs)]

    def y_swap(values):
        second = lax.ppermute(values[1], "view", y_pairs[1])
        return [lax.ppermute(values[0], "view", y_pairs[0]), second]

    first, second, own_inner, *sent = run(
        edges_kernel, (estimate.reshape(depth * rows, lanes),), [own_of(HALO), own_of(HALO), own_of(inner)] + sides_of(rows)
    )
    got = y_swap([first, second])
    own_side = z_swap(sent)
    zf, za, *tables = bands(plan, *[pltpu.with_memory_space_constraint(a, pltpu.HBM) for a in (psf_lengths.T, view_offsets.T, psf_taps)])
    (grown,) = run(grow_kernel, (own_inner, zf, *[value[2 * HALO :] for value in own_side]), [inner_grid])
    got, grown = lax.optimization_barrier((got, grown))
    halo = jnp.concatenate(got, axis=0)
    even_z = 1 - lax.axis_index("tile") % 2
    z_near = [jnp.where(even_z == 1, depth - side, 0), jnp.where(even_z == 1, 0, depth - side)][:stages]
    corner = z_swap([lax.dynamic_slice_in_dim(halo, at, side, 1) for at in z_near])
    edge_side = [jnp.concatenate([a, b[: 2 * HALO]], axis=0) for a, b in zip(corner, own_side)]
    own_edge = jnp.concatenate([halo, first, second], axis=0)
    for turn in range(ITERS):
        more = turn < ITERS - 1
        rows_of = {True: (inner, inner_grid), False: (edge, edge_grid)}
        (one, kept), (other, handed) = rows_of[more], rows_of[not more]
        grown, summed, *beyond = run(
            main_kernel, (field, background, own_edge, zf, za, *tables, views, grown, *edge_side),
            [handed, own_of(one)] + sides_of(one), more, scalars=2, scratch=[pltpu.VMEM(*kept)],
        )
        got_one = z_swap(beyond)
        pitch = plan.edge_pitch if more else plan.inner_pitch
        rest, *beyond = run(rest_kernel, (grown, za), [own_of(other)] + sides_of(other), pitch)
        got_one, rest, beyond = lax.optimization_barrier((got_one, rest, beyond))
        got_other = z_swap(beyond)
        (summed_inner, got_inner), (summed_edge, got_edge) = ((summed, got_one), (rest, got_other))[:: 1 if more else -1]
        sent = own_of(2 * HALO if more else HALO)
        summed_edge, *ends = run(sums_kernel, (summed_edge, *got_edge), [own_of(edge), sent, sent], more)
        got = y_swap(ends)
        if not more:
            out = run(
                last_kernel, (own_edge, own_inner, summed_edge, summed_inner, *got, *got_inner), [((depth * rows, lanes), F32)]
            )
            return out[0].reshape(depth, rows, lanes)
        own_inner, *sent = run(next_inner_kernel, (own_inner, summed_inner, *got_inner), [own_of(inner)] + sides_of(inner))
        (grown,) = run(grow_kernel, (own_inner, zf, *z_swap(sent)), [inner_grid])
        got, grown = lax.optimization_barrier((got, grown))
        own_edge, *sent = run(next_edge_kernel, (own_edge, summed_edge, *got), [own_of(edge)] + sides_of(edge))
        edge_side = z_swap(sent)


def solution(mesh):
    in_specs = (P("tile", "view", None), P(None, "tile", "view", None), P(), P(), P(), P(), P())
    out_specs = P("tile", "view", None)
    return jax.shard_map(
        on_device, mesh=mesh, in_specs=in_specs, out_specs=out_specs, check_vma=False
    )
```

time: 70.5 us -> 57.6 us (0.82)
  Pallas kernels: 27.5 us -> 20.7 us
  local copies, waits for them, and re-layouts: 5.61 us -> 1.15 us
  waiting for transfers between devices: 21.1 us -> 19.2 us
  starting transfers between devices: 15 us -> 15.9 us
  other arithmetic: 0.75 us -> 0.04 us
    pallas_call x7 -> x13, Pallas kernels: 27.5 us -> 20.7 us  [call(): pl.pallas_call(body, out_shape=[jax.ShapeDtypeStruct(*shape) for shape in...]
    ppermute x3, waiting for transfers between devices: 8.43 us -> 5.77 us  [y_swap(): return [lax.ppermute(values[0], 'view', y_pairs[0]), second]]
    ppermute x3, starting transfers between devices: 8.1 us -> 10.5 us  [y_swap(): second = lax.ppermute(values[1], 'view', y_pairs[1])]
    dynamic_slice x3 -> x0, local copies, waits for them, and re-layouts: 2.1 us -> none  [the longest x1 1.06 us: on_device(): lax.dynamic_slice_in_dim(estimate, row, HALO, 1).transpose(1, 0, 2)]
    ppermute x3, waiting for transfers between devices: 6.39 us -> 8.37 us  [y_swap(): second = lax.ppermute(values[1], 'view', y_pairs[1])]
    ppermute x3, starting transfers between devices: 5.6 us -> 4.12 us  [y_swap(): return [lax.ppermute(values[0], 'view', y_pairs[0]), second]]
    unnamed x9 -> x11, local copies, waits for them, and re-layouts: 2.39 us -> 1.11 us
    ppermute x5 -> x8, waiting for transfers between devices: 6.3 us -> 5.06 us  [z_swap(): lax.ppermute(value, 'tile', pairs)]
  transfers between devices with their start and end apart: 11 -> 14, of which waited for: 8 -> 10; matrix products, arithmetic and copies ran while one was open for 7% -> 0% of each run, Pallas kernels for 4% -> 10%
where the time goes in v2:
time: 57.6 us; the launch traced here: 57.3 us
  Pallas kernels  20.7 us (36%)
  waiting for transfers between devices  19.2 us (33%)
  starting transfers between devices  15.9 us (28%)
  local copies, waits for them, and re-layouts  1.15 us (2%)
    pallas_call x13, Pallas kernels, call(): pl.pallas_call(body, out_shape=[jax.ShapeDtypeStruct(*shape) for shape in...  20.7 us
    ppermute x3, starting transfers between devices, y_swap(): second = lax.ppermute(values[1], 'view', y_pairs[1])  10.5 us
    ppermute x3, waiting for transfers between devices, y_swap(): second = lax.ppermute(values[1], 'view', y_pairs[1])  8.37 us
    ppermute x3, waiting for transfers between devices, y_swap(): return [lax.ppermute(values[0], 'view', y_pairs[0]), second]  5.77 us
    ppermute x8, waiting for transfers between devices, z_swap(): lax.ppermute(value, 'tile', pairs)  5.06 us
    ppermute x3, starting transfers between devices, y_swap(): return [lax.ppermute(values[0], 'view', y_pairs[0]), second]  4.12 us
    ppermute x8, starting transfers between devices, z_swap(): lax.ppermute(value, 'tile', pairs)  1.3 us
  transfers between devices with their start and end apart: 14, of which 10 were waited for; matrix products, arithmetic and copies ran while one was open for 0% of the time, Pallas kernels for 10%

profile of v2, /device:TPU:16, one launch (start us, length us, event | category | flops | bytes accessed | tf_op | source)
XLA Modules:
  0.0 57.3 jit_solution(4239931401710754337)
XLA Ops:
  0.0 1.1 %copy-done.1 = f32[24,48,128]{2,1,0:T(8,128)S(1)} copy-done((f32[24,48,128]{2,1,0:T(8,128)S(1)}, f32[24,48,128]{2,1,0:T(8,128)}, u32[]{:S(2)}) %copy-start.1) | copy-done | bytes 589848
  1.1 0.2 edges_kernel.1
  1.3 0.1 collective-permute-start.2
  1.4 1.6 %collective-permute-start = (f32[9,24,128]{2,1,0:T(8,128)S(1)}, f32[9,24,128]{2,1,0:T(8,128)S(1)}, u32[]{:S(2)}, u32[]{:S(2)}) collective-permute-start(f32[9,24,128]{2,1,0:T(8,128)S(1)} %get-tuple-element.47), channel_id=1, source_target_pairs={{0,1},{1,0},{2,3},{3,2},{4,5},{5,4},{6,7},{7,6},{8,9},{9,8},{10,11... | collective-permute-start | bytes 331784 | tf_op jit(solution)/shard_map/ppermute | solution.py:457
  2.9 3.3 %collective-permute-start.1 = (f32[9,24,128]{2,1,0:T(8,128)S(1)}, f32[9,24,128]{2,1,0:T(8,128)S(1)}, u32[]{:S(2)}, u32[]{:S(2)}) collective-permute-start(f32[9,24,128]{2,1,0:T(8,128)S(1)} %get-tuple-element.48), channel_id=1, source_target_pairs={{1,2},{2,1},{3,4},{4,3},{5,6},{6,5},{7,8},{8,7},{9,10},{10,9},{11,... | collective-permute-start | bytes 331784 | tf_op jit(solution)/shard_map/ppermute | solution.py:456
  6.2 2.8 %bands_kernel.1 = (bf16[144,144]{1,0:T(8,128)(2,1)S(1)}, bf16[96,144]{1,0:T(8,128)(2,1)S(1)}, bf16[6,96,160]{2,1,0:T(8,128)(2,1)S(1)}, bf16[6,80,144]{2,1,0:T(8,...) custom-call(s32[3,6]{1,0:T(4,128)} %bitcast.8, s32[3,6]{1,0:T(4,128)} %bitcast.9, ...), custom_call_target="tpu_custom_call" | custom-call | flops 1000 | bytes 1000 | tf_op jit(solution)/shard_map/bands_kernel/pallas_call | solution.py:198
  9.1 0.6 %grow_kernel.2.inner_in = f32[5760,128]{1,0:T(8,128)S(1)} custom-call(f32[30,24,128]{2,1,0:T(8,128)S(1)} %get-tuple-element.49.inner_ref.own_ref, bf16[144,144]{1,0:T(8,128)(2,1)S(1)} %get-tuple-element.50.zf_ref, f32[30,16,128]{2,1,0:T(8,128)S(1)} %slice.8.refs_0_), custom_call_target="tpu_custom_call" | custom-call | flops 1000 | bytes 1000 | tf_op jit(solution)/shard_map/grow_kernel/pallas_call | solution.py:198
  9.7 2.0 %collective-permute-done.1 = f32[9,24,128]{2,1,0:T(8,128)S(1)} collective-permute-done((f32[9,24,128]{2,1,0:T(8,128)S(1)}, f32[9,24,128]{2,1,0:T(8,128)S(1)}, u32[]{:S(2)}, u32[]{:S(2)}) %collective-permute-start.1) | collective-permute-done | bytes 110624 | tf_op jit(solution)/shard_map/ppermute | solution.py:456
  11.9 1.3 %collective-permute-done.3 = f32[18,16,128]{2,1,0:T(8,128)S(1)} collective-permute-done((f32[18,16,128]{2,1,0:T(8,128)S(1)}, f32[18,16,128]{2,1,0:T(8,128)S(1)}, u32[]{:S(2)}, u32[]{:S(2)}) %collective-permute-start.3) | collective-permute-done | bytes 147488 | tf_op jit(solution)/shard_map/ppermute | solution.py:453
  13.3 6.8 %main_kernel.2 = (f32[5760,128]{1,0:T(8,128)S(1)}, f32[30,24,128]{2,1,0:T(8,128)S(1)}, f32[30,16,128]{2,1,0:T(8,128)S(1)}) custom-call(s32[2,6]{1,0:T(2,128)S(1)} %bitcast.6, f32[6]{0:T(128)S(1)} %copy-done.3, f32[36,24,128]{2,1,0:T(8,128)S(1)} %constant_dynamic-update-slice_fusion.own_ref, bf16[144,144]{1,0:T(8,128)(2,1)S(1)} %get-tuple-element.50.zf_ref, ...), custom_call_target="tpu_custom_call" | custom-call | flops 1000 | bytes 1000 | tf_op jit(solution)/shard_map/main_kernel/pallas_call | solution.py:198
  20.0 0.2 collective-permute-start.4
  20.2 0.9 %rest_kernel.2 = (f32[36,24,128]{2,1,0:T(8,128)S(1)}, f32[36,16,128]{2,1,0:T(8,128)S(1)}) custom-call(f32[5760,128]{1,0:T(8,128)S(1)} %get-tuple-element.61.grid_ref, bf16[96,144]{1,0:T(8,128)(2,1)S(1)} %get-tuple-element.54.za_ref), custom_call_target="tpu_custom_call" | custom-call | flops 1000 | bytes 1000 | tf_op jit(solution)/shard_map/rest_kernel/pallas_call | solution.py:198
  21.1 0.5 collective-permute-done.4.refs_0_
  21.6 0.1 collective-permute-start.5
  21.8 0.4 collective-permute-start.8
  22.2 0.9 %collective-permute-done.5.refs_0_ = f32[36,16,128]{2,1,0:T(8,128)S(1)} collective-permute-done((f32[36,16,128]{2,1,0:T(8,128)S(1)}, f32[36,16,128]{2,1,0:T(8,128)S(1)}, u32[]{:S(2)}, u32[]{:S(2)}) %collective-permute-start.5) | collective-permute-done | bytes 294944 | tf_op jit(solution)/shard_map/ppermute | solution.py:453
  23.3 4.0 %collective-permute-start.7 = (f32[18,24,128]{2,1,0:T(8,128)S(1)}, f32[18,24,128]{2,1,0:T(8,128)S(1)}, u32[]{:S(2)}, u32[]{:S(2)}) collective-permute-start(f32[18,24,128]{2,1,0:T(8,128)S(1)} %get-tuple-element.68), channel_id=1, source_target_pairs={{1,2},{2,1},{3,4},{4,3},{5,6},{6,5},{7,8},{8,7},{9,10},{10,9},{11,... | collective-permute-start | bytes 663560 | tf_op jit(solution)/shard_map/ppermute | solution.py:456
  27.4 0.6 %grow_kernel.3.inner_in = f32[5760,128]{1,0:T(8,128)S(1)} custom-call(f32[30,24,128]{2,1,0:T(8,128)S(1)} %get-tuple-element.71.inner_ref, bf16[144,144]{1,0:T(8,128)(2,1)S(1)} %get-tuple-element.50.zf_ref, f32[30,16,128]{2,1,0:T(8,128)S(1)} %collective-permute-done.8.refs_0_), custom_call_target="tpu_custom_call" | custom-call | flops 1000 | bytes 1000 | tf_op jit(solution)/shard_map/grow_kernel/pallas_call | solution.py:198
  27.9 5.4 %collective-permute-done.6.first_ref = f32[18,24,128]{2,1,0:T(8,128)S(1)} collective-permute-done((f32[18,24,128]{2,1,0:T(8,128)S(1)}, f32[18,24,128]{2,1,0:T(8,128)S(1)}, u32[]{:S(2)}, u32[]{:S(2)}) %collective-permute-start.6) | collective-permute-done | bytes 221216 | tf_op jit(solution)/shard_map/ppermute | solution.py:457
  33.4 1.2 %collective-permute-done.7.second_ref = f32[18,24,128]{2,1,0:T(8,128)S(1)} collective-permute-done((f32[18,24,128]{2,1,0:T(8,128)S(1)}, f32[18,24,128]{2,1,0:T(8,128)S(1)}, u32[]{:S(2)}, u32[]{:S(2)}) %collective-permute-start.7) | collective-permute-done | bytes 221216 | tf_op jit(solution)/shard_map/ppermute | solution.py:456
  34.6 0.1 next_edge_kernel.1
  34.8 1.6 %collective-permute-done.9.refs_0_ = f32[36,16,128]{2,1,0:T(8,128)S(1)} collective-permute-done((f32[36,16,128]{2,1,0:T(8,128)S(1)}, f32[36,16,128]{2,1,0:T(8,128)S(1)}, u32[]{:S(2)}, u32[]{:S(2)}) %collective-permute-start.9) | collective-permute-done | bytes 294944 | tf_op jit(solution)/shard_map/ppermute | solution.py:453
  36.3 6.8 %main_kernel.3 = (f32[5760,128]{1,0:T(8,128)S(1)}, f32[36,24,128]{2,1,0:T(8,128)S(1)}, f32[36,16,128]{2,1,0:T(8,128)S(1)}) custom-call(s32[2,6]{1,0:T(2,128)S(1)} %bitcast.7, f32[6]{0:T(128)S(1)} %copy-done.3, f32[36,24,128]{2,1,0:T(8,128)S(1)} %get-tuple-element.75.own_ref.edge_ref, bf16[144,144]{1,0:T(8,128)(2,1)S(1)} %get-tuple-element.50.zf_ref, ...), custom_call_target="tpu_custom_call" | custom-call | flops 1000 | bytes 1000 | tf_op jit(solution)/shard_map/main_kernel/pallas_call | solution.py:198
  43.1 0.2 collective-permute-start.10
  43.3 0.7 %rest_kernel.3 = (f32[30,24,128]{2,1,0:T(8,128)S(1)}, f32[30,16,128]{2,1,0:T(8,128)S(1)}) custom-call(f32[5760,128]{1,0:T(8,128)S(1)} %get-tuple-element.80.grid_ref, bf16[96,144]{1,0:T(8,128)(2,1)S(1)} %get-tuple-element.54.za_ref), custom_call_target="tpu_custom_call" | custom-call | flops 1000 | bytes 1000 | tf_op jit(solution)/shard_map/rest_kernel/pallas_call | solution.py:198
  44.0 0.8 %collective-permute-done.10.refs_0_ = f32[36,16,128]{2,1,0:T(8,128)S(1)} collective-permute-done((f32[36,16,128]{2,1,0:T(8,128)S(1)}, f32[36,16,128]{2,1,0:T(8,128)S(1)}, u32[]{:S(2)}, u32[]{:S(2)}) %collective-permute-start.10) | collective-permute-done | bytes 294944 | tf_op jit(solution)/shard_map/ppermute | solution.py:453
  44.7 0.1 collective-permute-start.13
  44.9 2.5 %collective-permute-start.11 = (f32[9,24,128]{2,1,0:T(8,128)S(1)}, f32[9,24,128]{2,1,0:T(8,128)S(1)}, u32[]{:S(2)}, u32[]{:S(2)}) collective-permute-start(f32[9,24,128]{2,1,0:T(8,128)S(1)} %get-tuple-element.86), channel_id=1, source_target_pairs={{0,1},{1,0},{2,3},{3,2},{4,5},{5,4},{6,7},{7,6},{8,9},{9,8},{10,11... | collective-permute-start | bytes 331784 | tf_op jit(solution)/shard_map/ppermute | solution.py:457
  47.4 3.2 %collective-permute-start.12 = (f32[9,24,128]{2,1,0:T(8,128)S(1)}, f32[9,24,128]{2,1,0:T(8,128)S(1)}, u32[]{:S(2)}, u32[]{:S(2)}) collective-permute-start(f32[9,24,128]{2,1,0:T(8,128)S(1)} %get-tuple-element.87), channel_id=1, source_target_pairs={{1,2},{2,1},{3,4},{4,3},{5,6},{6,5},{7,8},{8,7},{9,10},{10,9},{11,... | collective-permute-start | bytes 331784 | tf_op jit(solution)/shard_map/ppermute | solution.py:456
  50.6 0.4 collective-permute-done.11.first_ref
  51.0 5.1 %collective-permute-done.12.second_ref = f32[9,24,128]{2,1,0:T(8,128)S(1)} collective-permute-done((f32[9,24,128]{2,1,0:T(8,128)S(1)}, f32[9,24,128]{2,1,0:T(8,128)S(1)}, u32[]{:S(2)}, u32[]{:S(2)}) %collective-permute-start.12) | collective-permute-done | bytes 110624 | tf_op jit(solution)/shard_map/ppermute | solution.py:456
  56.2 1.1 %last_kernel.1 = f32[1152,128]{1,0:T(8,128)} custom-call(f32[36,24,128]{2,1,0:T(8,128)S(1)} %get-tuple-element.75.own_ref.edge_ref, f32[30,24,128]{2,1,0:T(8,128)S(1)} %get-tuple-element.71.inner_ref, f32[36,24,128]{2,1,0:T(8,128)S(1)} %get-tuple-element.84.summed_edge_ref, f32[30,24,128]{2,1,0:T(8,128)S(1)} %get-tuple-element.85.summed_inner_ref, ...), custom_call_target="tpu_custom_call" | custom-call | flops 1000 | bytes 1000 | tf_op jit(solution)/shard_map/last_kernel/pallas_call | solution.py:198
  (25 shorter events, 0.5 us)
Async XLA Ops:
  0.0 1.1 %copy-start.1 = (f32[24,48,128]{2,1,0:T(8,128)S(1)}, f32[24,48,128]{2,1,0:T(8,128)}, u32[]{:S(2)}) copy-start(f32[24,48,128]{2,1,0:T(8,128)} %param.7) | copy-start | bytes 1769476
  1.3 7.8 %collective-permute-start.2 = (f32[48,16,128]{2,1,0:T(8,128)S(1)}, f32[48,16,128]{2,1,0:T(8,128)S(1)}, u32[]{:S(2)}, u32[]{:S(2)}) collective-permute-start(f32[48,16,128]{2,1,0:T(8,128)S(1)} %get-tuple-element.51), channel_id=1, source_target_pairs={{0,16},{16,0},{1,17},{17,1},{2,18},{18,2},{3,19},{19,3},{4,20},{20... | collective-permute-start | bytes 1179656 | tf_op jit(solution)/shard_map/ppermute | solution.py:453
  1.4 8.4 %collective-permute-start = (f32[9,24,128]{2,1,0:T(8,128)S(1)}, f32[9,24,128]{2,1,0:T(8,128)S(1)}, u32[]{:S(2)}, u32[]{:S(2)}) collective-permute-start(f32[9,24,128]{2,1,0:T(8,128)S(1)} %get-tuple-element.47), channel_id=1, source_target_pairs={{0,1},{1,0},{2,3},{3,2},{4,5},{5,4},{6,7},{7,6},{8,9},{9,8},{10,11... | collective-permute-start | bytes 331784 | tf_op jit(solution)/shard_map/ppermute | solution.py:457
  2.9 8.8 %collective-permute-start.1 = (f32[9,24,128]{2,1,0:T(8,128)S(1)}, f32[9,24,128]{2,1,0:T(8,128)S(1)}, u32[]{:S(2)}, u32[]{:S(2)}) collective-permute-start(f32[9,24,128]{2,1,0:T(8,128)S(1)} %get-tuple-element.48), channel_id=1, source_target_pairs={{1,2},{2,1},{3,4},{4,3},{5,6},{6,5},{7,8},{8,7},{9,10},{10,9},{11,... | collective-permute-start | bytes 331784 | tf_op jit(solution)/shard_map/ppermute | solution.py:456
  9.1 4.2 %copy-start = (f32[6,24,48,128]{3,2,1,0:T(8,128)S(1)}, f32[6,24,48,128]{3,2,1,0:T(8,128)}, u32[]{:S(2)}) copy-start(f32[6,24,48,128]{3,2,1,0:T(8,128)} %views_ref.3) | copy-start | bytes 10616836
  9.1 4.1 %copy-start.2 = (s32[6,2]{0,1:T(2,128)S(1)}, s32[6,2]{0,1:T(2,128)}, u32[]{:S(2)}) copy-start(s32[6,2]{0,1:T(2,128)} %param.13) | copy-start | bytes 148
  9.1 4.1 %copy-start.3 = (f32[6]{0:T(128)S(1)}, f32[6]{0:T(128)}, u32[]{:S(2)}) copy-start(f32[6]{0:T(128)} %level.3) | copy-start | bytes 76
  11.8 1.4 %collective-permute-start.3 = (f32[18,16,128]{2,1,0:T(8,128)S(1)}, f32[18,16,128]{2,1,0:T(8,128)S(1)}, u32[]{:S(2)}, u32[]{:S(2)}) collective-permute-start(f32[18,16,128]{2,1,0:T(8,128)S(1)} %fusion), channel_id=1, source_target_pairs={{0,16},{16,0},{1,17},{17,1},{2,18},{18,2},{3,19},{19,3},{4,20},{20... | collective-permute-start | bytes 442376 | tf_op jit(solution)/shard_map/ppermute | solution.py:453
  20.0 1.6 %collective-permute-start.4 = (f32[30,16,128]{2,1,0:T(8,128)S(1)}, f32[30,16,128]{2,1,0:T(8,128)S(1)}, u32[]{:S(2)}, u32[]{:S(2)}) collective-permute-start(f32[30,16,128]{2,1,0:T(8,128)S(1)} %get-tuple-element.60), channel_id=1, source_target_pairs={{0,16},{16,0},{1,17},{17,1},{2,18},{18,2},{3,19},{19,3},{4,20},{20... | collective-permute-start | bytes 737288 | tf_op jit(solution)/shard_map/ppermute | solution.py:453
  21.6 1.6 %collective-permute-start.5 = (f32[36,16,128]{2,1,0:T(8,128)S(1)}, f32[36,16,128]{2,1,0:T(8,128)S(1)}, u32[]{:S(2)}, u32[]{:S(2)}) collective-permute-start(f32[36,16,128]{2,1,0:T(8,128)S(1)} %get-tuple-element.65), channel_id=1, source_target_pairs={{0,16},{16,0},{1,17},{17,1},{2,18},{18,2},{3,19},{19,3},{4,20},{20... | collective-permute-start | bytes 884744 | tf_op jit(solution)/shard_map/ppermute | solution.py:453
  21.8 5.6 %collective-permute-start.8 = (f32[30,16,128]{2,1,0:T(8,128)S(1)}, f32[30,16,128]{2,1,0:T(8,128)S(1)}, u32[]{:S(2)}, u32[]{:S(2)}) collective-permute-start(f32[30,16,128]{2,1,0:T(8,128)S(1)} %get-tuple-element.72), channel_id=1, source_target_pairs={{0,16},{16,0},{1,17},{17,1},{2,18},{18,2},{3,19},{19,3},{4,20},{20... | collective-permute-start | bytes 737288 | tf_op jit(solution)/shard_map/ppermute | solution.py:453
  23.2 10.1 %collective-permute-start.6 = (f32[18,24,128]{2,1,0:T(8,128)S(1)}, f32[18,24,128]{2,1,0:T(8,128)S(1)}, u32[]{:S(2)}, u32[]{:S(2)}) collective-permute-start(f32[18,24,128]{2,1,0:T(8,128)S(1)} %get-tuple-element.67), channel_id=1, source_target_pairs={{0,1},{1,0},{2,3},{3,2},{4,5},{5,4},{6,7},{7,6},{8,9},{9,8},{10,11... | collective-permute-start | bytes 663560 | tf_op jit(solution)/shard_map/ppermute | solution.py:457
  23.3 11.3 %collective-permute-start.7 = (f32[18,24,128]{2,1,0:T(8,128)S(1)}, f32[18,24,128]{2,1,0:T(8,128)S(1)}, u32[]{:S(2)}, u32[]{:S(2)}) collective-permute-start(f32[18,24,128]{2,1,0:T(8,128)S(1)} %get-tuple-element.68), channel_id=1, source_target_pairs={{1,2},{2,1},{3,4},{4,3},{5,6},{6,5},{7,8},{8,7},{9,10},{10,9},{11,... | collective-permute-start | bytes 663560 | tf_op jit(solution)/shard_map/ppermute | solution.py:456
  34.7 1.6 %collective-permute-start.9 = (f32[36,16,128]{2,1,0:T(8,128)S(1)}, f32[36,16,128]{2,1,0:T(8,128)S(1)}, u32[]{:S(2)}, u32[]{:S(2)}) collective-permute-start(f32[36,16,128]{2,1,0:T(8,128)S(1)} %get-tuple-element.77), channel_id=1, source_target_pairs={{0,16},{16,0},{1,17},{17,1},{2,18},{18,2},{3,19},{19,3},{4,20},{20... | collective-permute-start | bytes 884744 | tf_op jit(solution)/shard_map/ppermute | solution.py:453
  43.1 1.6 %collective-permute-start.10 = (f32[36,16,128]{2,1,0:T(8,128)S(1)}, f32[36,16,128]{2,1,0:T(8,128)S(1)}, u32[]{:S(2)}, u32[]{:S(2)}) collective-permute-start(f32[36,16,128]{2,1,0:T(8,128)S(1)} %get-tuple-element.79), channel_id=1, source_target_pairs={{0,16},{16,0},{1,17},{17,1},{2,18},{18,2},{3,19},{19,3},{4,20},{20... | collective-permute-start | bytes 884744 | tf_op jit(solution)/shard_map/ppermute | solution.py:453
  44.7 11.4 %collective-permute-start.13 = (f32[30,16,128]{2,1,0:T(8,128)S(1)}, f32[30,16,128]{2,1,0:T(8,128)S(1)}, u32[]{:S(2)}, u32[]{:S(2)}) collective-permute-start(f32[30,16,128]{2,1,0:T(8,128)S(1)} %get-tuple-element.88), channel_id=1, source_target_pairs={{0,16},{16,0},{1,17},{17,1},{2,18},{18,2},{3,19},{19,3},{4,20},{20... | collective-permute-start | bytes 737288 | tf_op jit(solution)/shard_map/ppermute | solution.py:453
  44.9 6.1 %collective-permute-start.11 = (f32[9,24,128]{2,1,0:T(8,128)S(1)}, f32[9,24,128]{2,1,0:T(8,128)S(1)}, u32[]{:S(2)}, u32[]{:S(2)}) collective-permute-start(f32[9,24,128]{2,1,0:T(8,128)S(1)} %get-tuple-element.86), channel_id=1, source_target_pairs={{0,1},{1,0},{2,3},{3,2},{4,5},{5,4},{6,7},{7,6},{8,9},{9,8},{10,11... | collective-permute-start | bytes 331784 | tf_op jit(solution)/shard_map/ppermute | solution.py:457
  47.4 8.7 %collective-permute-start.12 = (f32[9,24,128]{2,1,0:T(8,128)S(1)}, f32[9,24,128]{2,1,0:T(8,128)S(1)}, u32[]{:S(2)}, u32[]{:S(2)}) collective-permute-start(f32[9,24,128]{2,1,0:T(8,128)S(1)} %get-tuple-element.87), channel_id=1, source_target_pairs={{1,2},{2,1},{3,4},{4,3},{5,6},{6,5},{7,8},{8,7},{9,10},{10,9},{11,... | collective-permute-start | bytes 331784 | tf_op jit(solution)/shard_map/ppermute | solution.py:456

commit v3 on v2

--- a/solution.py
+++ b/solution.py
@@ -32,9 +32,9 @@
         self.z_slots = up(self.z_used, 16)
         self.y_edge = 4 * HALO
         self.y_inner = rows - 2 * HALO
-        self.edge_pad, self.inner_pad = up(self.y_edge, 8), up(self.y_inner, 8)
-        self.y_slots = up(self.edge_pad + self.inner_pad, 16)
-        self.edge_pitch, self.inner_pitch = odd_tiles(self.edge_pad), odd_tiles(self.inner_pad)
+        self.pair_pad, self.inner_pad = up(2 * HALO, 8), up(self.y_inner, 8)
+        self.y_slots = up(2 * self.pair_pad + self.inner_pad, 16)
+        self.pair_pitch, self.inner_pitch = odd_tiles(self.pair_pad), odd_tiles(self.inner_pad)
         self.stack = views * depth
 
 
@@ -88,8 +88,9 @@
 
 def y_place(plan, slot, even):
     place = jnp.full_like(slot, FAR)
-    begins = [0, HALO, 2 * HALO, 3 * HALO, plan.edge_pad]
-    ends = [HALO, 2 * HALO, 3 * HALO, 4 * HALO, plan.edge_pad + plan.y_inner]
+    pad = plan.pair_pad
+    begins = [0, HALO, pad, pad + HALO, 2 * pad]
+    ends = [HALO, 2 * HALO, pad + HALO, pad + 2 * HALO, 2 * pad + plan.y_inner]
     for begin, end, row in zip(begins, ends, y_first_rows(plan, even)):
         place = jnp.where((slot >= begin) & (slot < end), slot - begin + row, place)
     return place
@@ -234,13 +235,13 @@
     lax.fori_loop(0, count, run, 0, unroll=unroll)
 
 
-def z_forward(plan, own_ref, side_refs, zf_ref, grid_ref, pitch):
+def z_forward(plan, own_ref, side_refs, zf_ref, grid_ref, pitch, first=0, count=None):
     lanes = plan.lanes
 
     def pair(at):
         parts = []
         for i in range(2):
-            y = at * 2 + i
+            y = first + at * 2 + i
             pieces = [own_ref[y]] + [ref[y] for ref in side_refs]
             if plan.z_slots > plan.z_used:
                 pieces.append(jnp.zeros((plan.z_slots - plan.z_used, lanes), F32))
@@ -249,10 +250,10 @@
         for i in range(2):
             grid_ref[pl.ds(at * 2 + i, plan.stack, stride=pitch), :] = out[:, i * lanes : (i + 1) * lanes]
 
-    loop(own_ref.shape[0] // 2, pair)
-
-
-def z_adjoint(plan, grid_ref, za_ref, own_out, side_outs, pitch):
+    loop((own_ref.shape[0] if count is None else count) // 2, pair)
+
+
+def z_adjoint(plan, grid_ref, za_ref, own_out, side_outs, pitch, count=None, at_out=0):
     lanes, depth, side = plan.lanes, plan.depth, plan.z_side
 
     def pair(at):
@@ -262,11 +263,11 @@
         out = both[: plan.z_slots] + both[plan.z_slots :] + dot(za_ref[: plan.z_slots], low)
         for i in range(2):
             value = out[:, i * lanes : (i + 1) * lanes]
-            own_out[at * 2 + i] = value[:depth]
+            own_out[at_out + at * 2 + i] = value[:depth]
             for stage, ref in enumerate(side_outs):
-                ref[at * 2 + i] = value[depth + stage * side : depth + (stage + 1) * side]
-
-    loop(own_out.shape[0] // 2, pair)
+                ref[at_out + at * 2 + i] = value[depth + stage * side : depth + (stage + 1) * side]
+
+    loop((own_out.shape[0] if count is None else count) // 2, pair)
 
 
 def clear_rest(plan, grid_ref, used, padded, pitch):
@@ -281,9 +282,10 @@
     loop(plan.stack, one)
 
 
-def of_views(plan, field, level, yf_ref, ya_ref, xf_ref, xa_ref, views_ref, edge_ref, inner_in, inner_out):
+def of_views(plan, field, level, yf_ref, ya_ref, xf_ref, xa_ref, views_ref, grids_in, grids_out):
     views, depth, rows, lanes = plan.views, plan.depth, plan.rows, plan.lanes
-    edge, inner, y_slots = plan.edge_pad, plan.inner_pad, plan.y_slots
+    pads, y_slots = (plan.pair_pad, plan.pair_pad, plan.inner_pad), plan.y_slots
+    pitches = (plan.pair_pitch, plan.pair_pitch, plan.inner_pitch)
 
     def of_view(v, carry):
         lower, upper = field[0, v], field[1, v]
@@ -296,19 +298,13 @@
             out = dot(jnp.concatenate(split(value), axis=1), matrix)
             return out[:, :lanes] + out[:, lanes:]
 
-        edge_base = pl.multiple_of(v * depth * plan.edge_pitch, 8)
-        inner_base = pl.multiple_of(v * depth * plan.inner_pitch, 8)
-
-        def edge_at(z):
-            return pl.ds(edge_base + z * plan.edge_pitch, edge)
-
-        def inner_at(z):
-            return pl.ds(inner_base + z * plan.inner_pitch, inner)
+        def places(z):
+            return [pl.ds((v * depth + z) * pitch, pad) for pitch, pad in zip(pitches, pads)]
 
         def slots(z):
-            pieces = [edge_ref[edge_at(z), :], inner_in[inner_at(z), :]]
-            if y_slots > edge + inner:
-                pieces.append(jnp.zeros((y_slots - edge - inner, lanes), F32))
+            pieces = [ref[place, :] for ref, place in zip(grids_in, places(z))]
+            if y_slots > sum(pads):
+                pieces.append(jnp.zeros((y_slots - sum(pads), lanes), F32))
             return two(jnp.concatenate(pieces, axis=0))
 
         spread = []
@@ -324,8 +320,10 @@
             parts = [three(back[(z + i) * rows : (z + i + 1) * rows]) for i in range(2)]
             out = dot(ya_ref[v], jnp.concatenate(parts, axis=1))
             for i in range(2):
-                edge_ref[edge_at(z + i), :] = out[:edge, i * lanes : (i + 1) * lanes]
-                inner_out[inner_at(z + i), :] = out[edge : edge + inner, i * lanes : (i + 1) * lanes]
+                at = 0
+                for ref, place, pad in zip(grids_out, places(z + i), pads):
+                    ref[place, :] = out[at : at + pad, i * lanes : (i + 1) * lanes]
+                    at += pad
         return carry
 
     lax.fori_loop(0, views, of_view, 0, unroll=True)
@@ -353,17 +351,41 @@
     z_forward(plan, inner_ref, side_refs, zf_ref, grid_ref, plan.inner_pitch)
 
 
-def main_kernel(plan, inner_first, field, level, own_ref, zf_ref, za_ref, yf_ref, ya_ref, xf_ref, xa_ref, views_ref, inner_in, *refs):
-    side_refs, (grid_out, own_out, *side_outs), grid_kept = refs[: plan.z_stages], refs[plan.z_stages : -1], refs[-1]
-    edge_ref, inner_out = (grid_out, grid_kept) if inner_first else (grid_kept, grid_out)
-    clear_rest(plan, edge_ref, plan.y_edge, plan.edge_pad, plan.edge_pitch)
-    z_forward(plan, own_ref, side_refs, zf_ref, edge_ref, plan.edge_pitch)
-    of_views(plan, field, level, yf_ref, ya_ref, xf_ref, xa_ref, views_ref, edge_ref, inner_in, inner_out)
-    z_adjoint(plan, grid_kept, za_ref, own_out, side_outs, plan.inner_pitch if inner_first else plan.edge_pitch)
-
-
-def rest_kernel(plan, pitch, grid_ref, za_ref, own_out, *side_outs):
-    z_adjoint(plan, grid_ref, za_ref, own_out, side_outs, pitch)
+def grow_near_kernel(plan, near_ref, zf_ref, *refs):
+    side_refs, (grid_ref,) = refs[: plan.z_stages], refs[plan.z_stages :]
+    pair_along_z(plan, near_ref, side_refs, zf_ref, grid_ref, 0)
+
+
+def pair_along_z(plan, own_ref, side_refs, zf_ref, grid_ref, first):
+    clear_rest(plan, grid_ref, 2 * HALO, plan.pair_pad, plan.pair_pitch)
+    z_forward(plan, own_ref, side_refs, zf_ref, grid_ref, plan.pair_pitch, first, 2 * HALO)
+
+
+def main_kernel(plan, field, level, halo_ref, zf_ref, za_ref, yf_ref, ya_ref, xf_ref, xa_ref, views_ref, near_in, inner_in, *refs):
+    side_refs, (halo_grid, near_out, own_out, *side_outs), inner_out = refs[: plan.z_stages], refs[plan.z_stages : -1], refs[-1]
+    pair_along_z(plan, halo_ref, side_refs, zf_ref, halo_grid, 0)
+    grids = (halo_grid, near_in, inner_in), (halo_grid, near_out, inner_out)
+    of_views(plan, field, level, yf_ref, ya_ref, xf_ref, xa_ref, views_ref, *grids)
+    z_adjoint(plan, inner_out, za_ref, own_out, side_outs, plan.inner_pitch)
+
+
+def last_main_kernel(plan, field, level, edge_ref, zf_ref, za_ref, yf_ref, ya_ref, xf_ref, xa_ref, views_ref, inner_in, *refs):
+    side_refs, (near_grid, inner_out, own_out, *side_outs), halo_grid = refs[: plan.z_stages], refs[plan.z_stages : -1], refs[-1]
+    pair_along_z(plan, edge_ref, side_refs, zf_ref, halo_grid, 0)
+    pair_along_z(plan, edge_ref, side_refs, zf_ref, near_grid, 2 * HALO)
+    grids = (halo_grid, near_grid, inner_in), (halo_grid, near_grid, inner_out)
+    of_views(plan, field, level, yf_ref, ya_ref, xf_ref, xa_ref, views_ref, *grids)
+    z_adjoint(plan, halo_grid, za_ref, own_out, side_outs, plan.pair_pitch)
+
+
+def edge_rest_kernel(plan, halo_ref, near_ref, za_ref, own_out, *side_outs):
+    z_adjoint(plan, halo_ref, za_ref, own_out, side_outs, plan.pair_pitch, 2 * HALO)
+    z_adjoint(plan, near_ref, za_ref, own_out, side_outs, plan.pair_pitch, 2 * HALO, 2 * HALO)
+
+
+def own_rest_kernel(plan, near_ref, inner_ref, za_ref, own_out, *side_outs):
+    z_adjoint(plan, near_ref, za_ref, own_out, side_outs, plan.pair_pitch, 2 * HALO)
+    z_adjoint(plan, inner_ref, za_ref, own_out, side_outs, plan.inner_pitch, plan.y_inner, 2 * HALO)
 
 
 def add_sides(plan, ref, got_refs, at, count):
@@ -377,15 +399,19 @@
     return value
 
 
-def sums_kernel(plan, own_halo, summed_ref, *refs):
+def sums_kernel(plan, summed_ref, *refs):
     got_refs, (out_ref, first_ref, second_ref) = refs[: plan.z_stages], refs[plan.z_stages :]
     for i, ref in enumerate((first_ref, second_ref, first_ref, second_ref)):
         value = add_sides(plan, summed_ref, got_refs, i * HALO, HALO)
         out_ref[i * HALO : (i + 1) * HALO] = value
-        if i < 2:
-            ref[:HALO] = value
-        elif own_halo:
-            ref[HALO:] = value
+        at = 0 if i < 2 else HALO
+        ref[at : at + HALO] = value
+
+
+def last_sums_kernel(plan, summed_ref, *refs):
+    got_refs, refs = refs[: plan.z_stages], refs[plan.z_stages :]
+    for i, ref in enumerate(refs):
+        ref[...] = add_sides(plan, summed_ref, got_refs, i * HALO, HALO)
 
 
 def near_side(plan, value, stage):
@@ -414,7 +440,7 @@
             side[a:b] = near_side(plan, value, stage)
 
 
-def last_kernel(plan, edge_ref, inner_ref, summed_edge_ref, summed_inner_ref, first_ref, second_ref, *refs):
+def last_kernel(plan, edge_ref, inner_ref, summed_ref, first_ref, second_ref, *refs):
     got_refs, (out_ref,) = refs[: plan.z_stages], refs[plan.z_stages :]
     scale = 1.0 / plan.views
     first_row, second_row, inner_row = y_first_rows(plan, evens()[1])[2:]
@@ -422,12 +448,14 @@
     def put(row, value):
         out_ref[pl.ds(row, plan.depth, stride=plan.rows), :] = value
 
-    for ref, row, at in ((first_ref, first_row, 2 * HALO), (second_ref, second_row, 3 * HALO)):
-        for i in range(HALO):
-            put(row + i, edge_ref[at + i] * (summed_edge_ref[at + i] + ref[i]) * scale)
-    for i in range(inner_ref.shape[0]):
-        total = add_sides(plan, summed_inner_ref, got_refs, i, 1)[0]
-        put(inner_row + i, inner_ref[i] * total * scale)
+    for i in range(plan.rows):
+        total = add_sides(plan, summed_ref, got_refs, i, 1)[0]
+        if i < HALO:
+            put(first_row + i, edge_ref[2 * HALO + i] * (total + first_ref[i]) * scale)
+        elif i < 2 * HALO:
+            put(second_row + i - HALO, edge_ref[2 * HALO + i] * (total + second_ref[i - HALO]) * scale)
+        else:
+            put(inner_row + i - 2 * HALO, inner_ref[i - 2 * HALO] * total * scale)
 
 
 def on_device(estimate, views, background, psf_taps, psf_lengths, view_offsets, field_rows):
@@ -437,7 +465,7 @@
     z_pairs, y_pairs = swaps(tiles), swaps(blocks)
     side, stages, edge, inner = plan.z_side, plan.z_stages, plan.y_edge, plan.y_inner
     inner_grid = ((plan.stack * plan.inner_pitch, lanes), F32)
-    edge_grid = ((plan.stack * plan.edge_pitch, lanes), F32)
+    pair_grid = ((plan.stack * plan.pair_pitch, lanes), F32)
     field = field_rows.T
 
     def own_of(count):
@@ -463,35 +491,38 @@
     own_side = z_swap(sent)
     zf, za, *tables = bands(plan, *[pltpu.with_memory_space_constraint(a, pltpu.HBM) for a in (psf_lengths.T, view_offsets.T, psf_taps)])
     (grown,) = run(grow_kernel, (own_inner, zf, *[value[2 * HALO :] for value in own_side]), [inner_grid])
-    got, grown = lax.optimization_barrier((got, grown))
+    near = jnp.concatenate([first, second], axis=0)
+    (near_grown,) = run(grow_near_kernel, (near, zf, *[value[: 2 * HALO] for value in own_side]), [pair_grid])
+    got, grown, near_grown = lax.optimization_barrier((got, grown, near_grown))
     halo = jnp.concatenate(got, axis=0)
     even_z = 1 - lax.axis_index("tile") % 2
     z_near = [jnp.where(even_z == 1, depth - side, 0), jnp.where(even_z == 1, 0, depth - side)][:stages]
-    corner = z_swap([lax.dynamic_slice_in_dim(halo, at, side, 1) for at in z_near])
-    edge_side = [jnp.concatenate([a, b[: 2 * HALO]], axis=0) for a, b in zip(corner, own_side)]
-    own_edge = jnp.concatenate([halo, first, second], axis=0)
+    edge_side = z_swap([lax.dynamic_slice_in_dim(halo, at, side, 1) for at in z_near])
+    own_edge = jnp.concatenate([halo, near], axis=0)
+    tables = (zf, za, *tables, views)
     for turn in range(ITERS):
-        more = turn < ITERS - 1
-        rows_of = {True: (inner, inner_grid), False: (edge, edge_grid)}
-        (one, kept), (other, handed) = rows_of[more], rows_of[not more]
-        grown, summed, *beyond = run(
-            main_kernel, (field, background, own_edge, zf, za, *tables, views, grown, *edge_side),
-            [handed, own_of(one)] + sides_of(one), more, scalars=2, scratch=[pltpu.VMEM(*kept)],
+        if turn == ITERS - 1:
+            near_grown, inner_grown, summed, *beyond = run(
+                last_main_kernel, (field, background, own_edge, *tables, grown, *edge_side),
+                [pair_grid, inner_grid, own_of(2 * HALO)] + sides_of(2 * HALO), scalars=2, scratch=[pltpu.VMEM(*pair_grid)],
+            )
+            got_halo = z_swap(beyond)
+            summed_own, *beyond = run(own_rest_kernel, (near_grown, inner_grown, za), [own_of(rows)] + sides_of(rows))
+            got_halo, summed_own, beyond = lax.optimization_barrier((got_halo, summed_own, beyond))
+            got_own = z_swap(beyond)
+            got = y_swap(run(last_sums_kernel, (summed, *got_halo), [own_of(HALO), own_of(HALO)]))
+            out = run(last_kernel, (own_edge, own_inner, summed_own, *got, *got_own), [((depth * rows, lanes), F32)])
+            return out[0].reshape(depth, rows, lanes)
+        halo_grown, near_grown, summed_inner, *beyond = run(
+            main_kernel, (field, background, halo, *tables, near_grown, grown, *edge_side),
+            [pair_grid, pair_grid, own_of(inner)] + sides_of(inner), scalars=2, scratch=[pltpu.VMEM(*inner_grid)],
         )
-        got_one = z_swap(beyond)
-        pitch = plan.edge_pitch if more else plan.inner_pitch
-        rest, *beyond = run(rest_kernel, (grown, za), [own_of(other)] + sides_of(other), pitch)
-        got_one, rest, beyond = lax.optimization_barrier((got_one, rest, beyond))
-        got_other = z_swap(beyond)
-        (summed_inner, got_inner), (summed_edge, got_edge) = ((summed, got_one), (rest, got_other))[:: 1 if more else -1]
-        sent = own_of(2 * HALO if more else HALO)
-        summed_edge, *ends = run(sums_kernel, (summed_edge, *got_edge), [own_of(edge), sent, sent], more)
+        got_inner = z_swap(beyond)
+        summed_edge, *beyond = run(edge_rest_kernel, (halo_grown, near_grown, za), [own_of(edge)] + sides_of(edge))
+        got_inner, summed_edge, beyond = lax.optimization_barrier((got_inner, summed_edge, beyond))
+        got_edge = z_swap(beyond)
+        summed_edge, *ends = run(sums_kernel, (summed_edge, *got_edge), [own_of(edge), own_of(2 * HALO), own_of(2 * HALO)])
         got = y_swap(ends)
-        if not more:
-            out = run(
-                last_kernel, (own_edge, own_inner, summed_edge, summed_inner, *got, *got_inner), [((depth * rows, lanes), F32)]
-            )
-            return out[0].reshape(depth, rows, lanes)
         own_inner, *sent = run(next_inner_kernel, (own_inner, summed_inner, *got_inner), [own_of(inner)] + sides_of(inner))
         (grown,) = run(grow_kernel, (own_inner, zf, *z_swap(sent)), [inner_grid])
         got, grown = lax.optimization_barrier((got, grown))

time: 57.6 us -> 56.7 us (0.984)
  waiting for transfers between devices: 19.2 us -> 17.9 us
    pallas_call x13 -> x14, Pallas kernels: 20.7 us -> 20.9 us  [call(): pl.pallas_call(body, out_shape=[jax.ShapeDtypeStruct(*shape) for shape in...]
  transfers between devices with their start and end apart: 14 -> 14, of which waited for: 10 -> 10; matrix products, arithmetic and copies ran while one was open for 0% -> 0% of each run, Pallas kernels for 10% -> 12%
where the time goes in v3:
time: 56.7 us; the launch traced here: 56.4 us
  Pallas kernels  20.9 us (37%)
  waiting for transfers between devices  17.9 us (32%)
  starting transfers between devices  16.2 us (29%)
  local copies, waits for them, and re-layouts  1.15 us (2%)
    pallas_call x14, Pallas kernels, call(): pl.pallas_call(body, out_shape=[jax.ShapeDtypeStruct(*shape) for shape in...  20.9 us
    ppermute x3, starting transfers between devices, y_swap(): second = lax.ppermute(values[1], 'view', y_pairs[1])  10.5 us
    ppermute x3, waiting for transfers between devices, y_swap(): second = lax.ppermute(values[1], 'view', y_pairs[1])  7.91 us
    ppermute x3, waiting for transfers between devices, y_swap(): return [lax.ppermute(values[0], 'view', y_pairs[0]), second]  5.54 us
    ppermute x8, waiting for transfers between devices, z_swap(): lax.ppermute(value, 'tile', pairs)  4.49 us
    ppermute x3, starting transfers between devices, y_swap(): return [lax.ppermute(values[0], 'view', y_pairs[0]), second]  4.21 us
    ppermute x8, starting transfers between devices, z_swap(): lax.ppermute(value, 'tile', pairs)  1.49 us
  transfers between devices with their start and end apart: 14, of which 10 were waited for; matrix products, arithmetic and copies ran while one was open for 0% of the time, Pallas kernels for 12%

profile of v3, /device:TPU:16, one launch (start us, length us, event | category | flops | bytes accessed | tf_op | source)
XLA Modules:
  0.0 56.4 jit_solution(14223164844620792078)
XLA Ops:
  0.0 1.1 %copy-done.1 = f32[24,48,128]{2,1,0:T(8,128)S(1)} copy-done((f32[24,48,128]{2,1,0:T(8,128)S(1)}, f32[24,48,128]{2,1,0:T(8,128)}, u32[]{:S(2)}) %copy-start.1) | copy-done | bytes 589848
  1.1 0.2 edges_kernel.1
  1.4 1.6 %collective-permute-start = (f32[9,24,128]{2,1,0:T(8,128)S(1)}, f32[9,24,128]{2,1,0:T(8,128)S(1)}, u32[]{:S(2)}, u32[]{:S(2)}) collective-permute-start(f32[9,24,128]{2,1,0:T(8,128)S(1)} %get-tuple-element.49), channel_id=1, source_target_pairs={{0,1},{1,0},{2,3},{3,2},{4,5},{5,4},{6,7},{7,6},{8,9},{9,8},{10,11... | collective-permute-start | bytes 331784 | tf_op jit(solution)/shard_map/ppermute | solution.py:485
  2.9 3.3 %collective-permute-start.1 = (f32[9,24,128]{2,1,0:T(8,128)S(1)}, f32[9,24,128]{2,1,0:T(8,128)S(1)}, u32[]{:S(2)}, u32[]{:S(2)}) collective-permute-start(f32[9,24,128]{2,1,0:T(8,128)S(1)} %get-tuple-element.50), channel_id=1, source_target_pairs={{1,2},{2,1},{3,4},{4,3},{5,6},{6,5},{7,8},{8,7},{9,10},{10,9},{11,... | collective-permute-start | bytes 331784 | tf_op jit(solution)/shard_map/ppermute | solution.py:484
  6.2 2.8 %bands_kernel.1 = (bf16[144,144]{1,0:T(8,128)(2,1)S(1)}, bf16[96,144]{1,0:T(8,128)(2,1)S(1)}, bf16[6,96,160]{2,1,0:T(8,128)(2,1)S(1)}, bf16[6,80,144]{2,1,0:T(8,...) custom-call(s32[3,6]{1,0:T(4,128)} %bitcast.8, s32[3,6]{1,0:T(4,128)} %bitcast.9, ...), custom_call_target="tpu_custom_call" | custom-call | flops 1000 | bytes 1000 | tf_op jit(solution)/shard_map/bands_kernel/pallas_call | solution.py:199
  9.1 0.4 grow_near_kernel.1.near_in
  9.6 0.6 %grow_kernel.2.inner_in = f32[5760,128]{1,0:T(8,128)S(1)} custom-call(f32[30,24,128]{2,1,0:T(8,128)S(1)} %get-tuple-element.51.inner_ref.own_ref, bf16[144,144]{1,0:T(8,128)(2,1)S(1)} %get-tuple-element.52.zf_ref, f32[30,16,128]{2,1,0:T(8,128)S(1)} %slice.8.refs_0_), custom_call_target="tpu_custom_call" | custom-call | flops 1000 | bytes 1000 | tf_op jit(solution)/shard_map/grow_kernel/pallas_call | solution.py:199
  10.2 1.5 %collective-permute-done.1 = f32[9,24,128]{2,1,0:T(8,128)S(1)} collective-permute-done((f32[9,24,128]{2,1,0:T(8,128)S(1)}, f32[9,24,128]{2,1,0:T(8,128)S(1)}, u32[]{:S(2)}, u32[]{:S(2)}) %collective-permute-start.1) | collective-permute-done | bytes 110624 | tf_op jit(solution)/shard_map/ppermute | solution.py:484
  11.9 1.4 %collective-permute-done.3.refs_0_ = f32[18,16,128]{2,1,0:T(8,128)S(1)} collective-permute-done((f32[18,16,128]{2,1,0:T(8,128)S(1)}, f32[18,16,128]{2,1,0:T(8,128)S(1)}, u32[]{:S(2)}, u32[]{:S(2)}) %collective-permute-start.3) | collective-permute-done | bytes 147488 | tf_op jit(solution)/shard_map/ppermute | solution.py:481
  13.2 6.4 %main_kernel.1 = (f32[3456,128]{1,0:T(8,128)S(1)}, f32[3456,128]{1,0:T(8,128)S(1)}, f32[30,24,128]{2,1,0:T(8,128)S(1)}, f32[30,16,128]{2,1,0:T(8,128)S(1)}) custom-call(s32[2,6]{1,0:T(2,128)S(1)} %bitcast.6, f32[6]{0:T(128)S(1)} %copy-done.3, f32[18,24,128]{2,1,0:T(8,128)S(1)} %constant_dynamic-update-slice_fusion.halo_ref, ...), custom_call_target="tpu_custom_call" | custom-call | flops 1000 | bytes 1000 | tf_op jit(solution)/shard_map/main_kernel/pallas_call | solution.py:199
  19.6 0.2 collective-permute-start.4
  19.8 0.9 %edge_rest_kernel.1 = (f32[36,24,128]{2,1,0:T(8,128)S(1)}, f32[36,16,128]{2,1,0:T(8,128)S(1)}) custom-call(f32[3456,128]{1,0:T(8,128)S(1)} %get-tuple-element.64.halo_ref, f32[3456,128]{1,0:T(8,128)S(1)} %get-tuple-element.65.near_ref, bf16[96,144]{1,0:T(8,128)(2,1)S(1)} %get-tuple-element.56.za_ref), custom_call_target="tpu_custom_call" | custom-call | flops 1000 | bytes 1000 | tf_op jit(solution)/shard_map/edge_rest_kernel/pallas_call | solution.py:199
  20.7 0.5 collective-permute-done.4.refs_0_
  21.2 0.1 collective-permute-start.5
  21.4 0.4 collective-permute-start.8
  21.8 0.9 %collective-permute-done.5.refs_0_ = f32[36,16,128]{2,1,0:T(8,128)S(1)} collective-permute-done((f32[36,16,128]{2,1,0:T(8,128)S(1)}, f32[36,16,128]{2,1,0:T(8,128)S(1)}, u32[]{:S(2)}, u32[]{:S(2)}) %collective-permute-start.5) | collective-permute-done | bytes 294944 | tf_op jit(solution)/shard_map/ppermute | solution.py:481
  22.8 0.2 collective-permute-start.6
  23.0 4.0 %collective-permute-start.7 = (f32[18,24,128]{2,1,0:T(8,128)S(1)}, f32[18,24,128]{2,1,0:T(8,128)S(1)}, u32[]{:S(2)}, u32[]{:S(2)}) collective-permute-start(f32[18,24,128]{2,1,0:T(8,128)S(1)} %get-tuple-element.72), channel_id=1, source_target_pairs={{1,2},{2,1},{3,4},{4,3},{5,6},{6,5},{7,8},{8,7},{9,10},{10,9},{11,... | collective-permute-start | bytes 663560 | tf_op jit(solution)/shard_map/ppermute | solution.py:484
  27.0 0.6 %grow_kernel.3.inner_in = f32[5760,128]{1,0:T(8,128)S(1)} custom-call(f32[30,24,128]{2,1,0:T(8,128)S(1)} %get-tuple-element.75.inner_ref, bf16[144,144]{1,0:T(8,128)(2,1)S(1)} %get-tuple-element.52.zf_ref, f32[30,16,128]{2,1,0:T(8,128)S(1)} %collective-permute-done.8.refs_0_), custom_call_target="tpu_custom_call" | custom-call | flops 1000 | bytes 1000 | tf_op jit(solution)/shard_map/grow_kernel/pallas_call | solution.py:199
  27.6 5.4 %collective-permute-done.6.first_ref = f32[18,24,128]{2,1,0:T(8,128)S(1)} collective-permute-done((f32[18,24,128]{2,1,0:T(8,128)S(1)}, f32[18,24,128]{2,1,0:T(8,128)S(1)}, u32[]{:S(2)}, u32[]{:S(2)}) %collective-permute-start.6) | collective-permute-done | bytes 221216 | tf_op jit(solution)/shard_map/ppermute | solution.py:485
  33.0 1.2 %collective-permute-done.7.second_ref = f32[18,24,128]{2,1,0:T(8,128)S(1)} collective-permute-done((f32[18,24,128]{2,1,0:T(8,128)S(1)}, f32[18,24,128]{2,1,0:T(8,128)S(1)}, u32[]{:S(2)}, u32[]{:S(2)}) %collective-permute-start.7) | collective-permute-done | bytes 221216 | tf_op jit(solution)/shard_map/ppermute | solution.py:484
  34.4 1.6 %collective-permute-done.9.refs_0_ = f32[36,16,128]{2,1,0:T(8,128)S(1)} collective-permute-done((f32[36,16,128]{2,1,0:T(8,128)S(1)}, f32[36,16,128]{2,1,0:T(8,128)S(1)}, u32[]{:S(2)}, u32[]{:S(2)}) %collective-permute-start.9) | collective-permute-done | bytes 294944 | tf_op jit(solution)/shard_map/ppermute | solution.py:481
  35.9 6.5 %last_main_kernel.1 = (f32[3456,128]{1,0:T(8,128)S(1)}, f32[5760,128]{1,0:T(8,128)S(1)}, f32[18,24,128]{2,1,0:T(8,128)S(1)}, f32[18,16,128]{2,1,0:T(8,128)S(1)}) custom-call(s32[2,6]{1,0:T(2,128)S(1)} %bitcast.7, f32[6]{0:T(128)S(1)} %copy-done.3, f32[36,24,128]{2,1,0:T(8,128)S(1)} %get-tuple-element.79.edge_ref, ...), custom_call_target="tpu_custom_call" | custom-call | flops 1000 | bytes 1000 | tf_op jit(solution)/shard_map/last_main_kernel/pallas_call | solution.py:199
  42.5 0.2 collective-permute-start.10
  42.6 1.1 %own_rest_kernel.1 = (f32[48,24,128]{2,1,0:T(8,128)S(1)}, f32[48,16,128]{2,1,0:T(8,128)S(1)}) custom-call(f32[3456,128]{1,0:T(8,128)S(1)} %get-tuple-element.83.near_ref, f32[5760,128]{1,0:T(8,128)S(1)} %get-tuple-element.84.inner_ref, bf16[96,144]{1,0:T(8,128)(2,1)S(1)} %get-tuple-element.56.za_ref), custom_call_target="tpu_custom_call" | custom-call | flops 1000 | bytes 1000 | tf_op jit(solution)/shard_map/own_rest_kernel/pallas_call | solution.py:199
  43.7 0.1 collective-permute-done.10.refs_0_
  43.9 0.3 collective-permute-start.13
  44.2 2.5 %collective-permute-start.11 = (f32[9,24,128]{2,1,0:T(8,128)S(1)}, f32[9,24,128]{2,1,0:T(8,128)S(1)}, u32[]{:S(2)}, u32[]{:S(2)}) collective-permute-start(f32[9,24,128]{2,1,0:T(8,128)S(1)} %get-tuple-element.90), channel_id=1, source_target_pairs={{0,1},{1,0},{2,3},{3,2},{4,5},{5,4},{6,7},{7,6},{8,9},{9,8},{10,11... | collective-permute-start | bytes 331784 | tf_op jit(solution)/shard_map/ppermute | solution.py:485
  46.7 3.2 %collective-permute-start.12 = (f32[9,24,128]{2,1,0:T(8,128)S(1)}, f32[9,24,128]{2,1,0:T(8,128)S(1)}, u32[]{:S(2)}, u32[]{:S(2)}) collective-permute-start(f32[9,24,128]{2,1,0:T(8,128)S(1)} %get-tuple-element.91), channel_id=1, source_target_pairs={{1,2},{2,1},{3,4},{4,3},{5,6},{6,5},{7,8},{8,7},{9,10},{10,9},{11,... | collective-permute-start | bytes 331784 | tf_op jit(solution)/shard_map/ppermute | solution.py:484
  49.9 0.2 collective-permute-done.11.first_ref
  50.1 5.1 %collective-permute-done.12.second_ref = f32[9,24,128]{2,1,0:T(8,128)S(1)} collective-permute-done((f32[9,24,128]{2,1,0:T(8,128)S(1)}, f32[9,24,128]{2,1,0:T(8,128)S(1)}, u32[]{:S(2)}, u32[]{:S(2)}) %collective-permute-start.12) | collective-permute-done | bytes 110624 | tf_op jit(solution)/shard_map/ppermute | solution.py:484
  55.3 1.1 %last_kernel.1 = f32[1152,128]{1,0:T(8,128)} custom-call(f32[36,24,128]{2,1,0:T(8,128)S(1)} %get-tuple-element.79.edge_ref, f32[30,24,128]{2,1,0:T(8,128)S(1)} %get-tuple-element.75.inner_ref, f32[48,24,128]{2,1,0:T(8,128)S(1)} %get-tuple-element.87.summed_ref, f32[9,24,128]{2,1,0:T(8,128)S(1)} %collective-permute-done.11.first_ref, ...), custom_call_target="tpu_custom_call" | custom-call | flops 1000 | bytes 1000 | tf_op jit(solution)/shard_map/last_kernel/pallas_call | solution.py:199
  (25 shorter events, 0.6 us)
Async XLA Ops:
  0.0 1.1 %copy-start.1 = (f32[24,48,128]{2,1,0:T(8,128)S(1)}, f32[24,48,128]{2,1,0:T(8,128)}, u32[]{:S(2)}) copy-start(f32[24,48,128]{2,1,0:T(8,128)} %param.7) | copy-start | bytes 1769476
  1.3 7.8 %collective-permute-start.2 = (f32[48,16,128]{2,1,0:T(8,128)S(1)}, f32[48,16,128]{2,1,0:T(8,128)S(1)}, u32[]{:S(2)}, u32[]{:S(2)}) collective-permute-start(f32[48,16,128]{2,1,0:T(8,128)S(1)} %get-tuple-element.53), channel_id=1, source_target_pairs={{0,16},{16,0},{1,17},{17,1},{2,18},{18,2},{3,19},{19,3},{4,20},{20... | collective-permute-start | bytes 1179656 | tf_op jit(solution)/shard_map/ppermute | solution.py:481
  1.4 8.8 %collective-permute-start = (f32[9,24,128]{2,1,0:T(8,128)S(1)}, f32[9,24,128]{2,1,0:T(8,128)S(1)}, u32[]{:S(2)}, u32[]{:S(2)}) collective-permute-start(f32[9,24,128]{2,1,0:T(8,128)S(1)} %get-tuple-element.49), channel_id=1, source_target_pairs={{0,1},{1,0},{2,3},{3,2},{4,5},{5,4},{6,7},{7,6},{8,9},{9,8},{10,11... | collective-permute-start | bytes 331784 | tf_op jit(solution)/shard_map/ppermute | solution.py:485
  2.9 8.8 %collective-permute-start.1 = (f32[9,24,128]{2,1,0:T(8,128)S(1)}, f32[9,24,128]{2,1,0:T(8,128)S(1)}, u32[]{:S(2)}, u32[]{:S(2)}) collective-permute-start(f32[9,24,128]{2,1,0:T(8,128)S(1)} %get-tuple-element.50), channel_id=1, source_target_pairs={{1,2},{2,1},{3,4},{4,3},{5,6},{6,5},{7,8},{8,7},{9,10},{10,9},{11,... | collective-permute-start | bytes 331784 | tf_op jit(solution)/shard_map/ppermute | solution.py:484
  9.5 3.7 %copy-start = (f32[6,24,48,128]{3,2,1,0:T(8,128)S(1)}, f32[6,24,48,128]{3,2,1,0:T(8,128)}, u32[]{:S(2)}) copy-start(f32[6,24,48,128]{3,2,1,0:T(8,128)} %views_ref.3) | copy-start | bytes 10616836
  9.5 3.7 %copy-start.2 = (s32[6,2]{0,1:T(2,128)S(1)}, s32[6,2]{0,1:T(2,128)}, u32[]{:S(2)}) copy-start(s32[6,2]{0,1:T(2,128)} %param.13) | copy-start | bytes 148
  9.5 3.7 %copy-start.3 = (f32[6]{0:T(128)S(1)}, f32[6]{0:T(128)}, u32[]{:S(2)}) copy-start(f32[6]{0:T(128)} %level.3) | copy-start | bytes 76
  11.8 1.4 %collective-permute-start.3 = (f32[18,16,128]{2,1,0:T(8,128)S(1)}, f32[18,16,128]{2,1,0:T(8,128)S(1)}, u32[]{:S(2)}, u32[]{:S(2)}) collective-permute-start(f32[18,16,128]{2,1,0:T(8,128)S(1)} %constant_dynamic-slice_fusion), channel_id=1, source_target_pairs={{0,16},{16,0},{1,17},{17,1},{2,18},{18,2},{3,19},{19,3},{4,20},{20... | collective-permute-start | bytes 442376 | tf_op jit(solution)/shard_map/ppermute | solution.py:481
  19.6 1.6 %collective-permute-start.4 = (f32[30,16,128]{2,1,0:T(8,128)S(1)}, f32[30,16,128]{2,1,0:T(8,128)S(1)}, u32[]{:S(2)}, u32[]{:S(2)}) collective-permute-start(f32[30,16,128]{2,1,0:T(8,128)S(1)} %get-tuple-element.63), channel_id=1, source_target_pairs={{0,16},{16,0},{1,17},{17,1},{2,18},{18,2},{3,19},{19,3},{4,20},{20... | collective-permute-start | bytes 737288 | tf_op jit(solution)/shard_map/ppermute | solution.py:481
  21.2 1.6 %collective-permute-start.5 = (f32[36,16,128]{2,1,0:T(8,128)S(1)}, f32[36,16,128]{2,1,0:T(8,128)S(1)}, u32[]{:S(2)}, u32[]{:S(2)}) collective-permute-start(f32[36,16,128]{2,1,0:T(8,128)S(1)} %get-tuple-element.69), channel_id=1, source_target_pairs={{0,16},{16,0},{1,17},{17,1},{2,18},{18,2},{3,19},{19,3},{4,20},{20... | collective-permute-start | bytes 884744 | tf_op jit(solution)/shard_map/ppermute | solution.py:481
  21.4 5.6 %collective-permute-start.8 = (f32[30,16,128]{2,1,0:T(8,128)S(1)}, f32[30,16,128]{2,1,0:T(8,128)S(1)}, u32[]{:S(2)}, u32[]{:S(2)}) collective-permute-start(f32[30,16,128]{2,1,0:T(8,128)S(1)} %get-tuple-element.76), channel_id=1, source_target_pairs={{0,16},{16,0},{1,17},{17,1},{2,18},{18,2},{3,19},{19,3},{4,20},{20... | collective-permute-start | bytes 737288 | tf_op jit(solution)/shard_map/ppermute | solution.py:481
  22.8 10.1 %collective-permute-start.6 = (f32[18,24,128]{2,1,0:T(8,128)S(1)}, f32[18,24,128]{2,1,0:T(8,128)S(1)}, u32[]{:S(2)}, u32[]{:S(2)}) collective-permute-start(f32[18,24,128]{2,1,0:T(8,128)S(1)} %get-tuple-element.71), channel_id=1, source_target_pairs={{0,1},{1,0},{2,3},{3,2},{4,5},{5,4},{6,7},{7,6},{8,9},{9,8},{10,11... | collective-permute-start | bytes 663560 | tf_op jit(solution)/shard_map/ppermute | solution.py:485
  23.0 11.2 %collective-permute-start.7 = (f32[18,24,128]{2,1,0:T(8,128)S(1)}, f32[18,24,128]{2,1,0:T(8,128)S(1)}, u32[]{:S(2)}, u32[]{:S(2)}) collective-permute-start(f32[18,24,128]{2,1,0:T(8,128)S(1)} %get-tuple-element.72), channel_id=1, source_target_pairs={{1,2},{2,1},{3,4},{4,3},{5,6},{6,5},{7,8},{8,7},{9,10},{10,9},{11,... | collective-permute-start | bytes 663560 | tf_op jit(solution)/shard_map/ppermute | solution.py:484
  34.3 1.6 %collective-permute-start.9 = (f32[36,16,128]{2,1,0:T(8,128)S(1)}, f32[36,16,128]{2,1,0:T(8,128)S(1)}, u32[]{:S(2)}, u32[]{:S(2)}) collective-permute-start(f32[36,16,128]{2,1,0:T(8,128)S(1)} %get-tuple-element.81), channel_id=1, source_target_pairs={{0,16},{16,0},{1,17},{17,1},{2,18},{18,2},{3,19},{19,3},{4,20},{20... | collective-permute-start | bytes 884744 | tf_op jit(solution)/shard_map/ppermute | solution.py:481
  42.5 1.4 %collective-permute-start.10 = (f32[18,16,128]{2,1,0:T(8,128)S(1)}, f32[18,16,128]{2,1,0:T(8,128)S(1)}, u32[]{:S(2)}, u32[]{:S(2)}) collective-permute-start(f32[18,16,128]{2,1,0:T(8,128)S(1)} %get-tuple-element.82), channel_id=1, source_target_pairs={{0,16},{16,0},{1,17},{17,1},{2,18},{18,2},{3,19},{19,3},{4,20},{20... | collective-permute-start | bytes 442376 | tf_op jit(solution)/shard_map/ppermute | solution.py:481
  43.9 11.4 %collective-permute-start.13 = (f32[48,16,128]{2,1,0:T(8,128)S(1)}, f32[48,16,128]{2,1,0:T(8,128)S(1)}, u32[]{:S(2)}, u32[]{:S(2)}) collective-permute-start(f32[48,16,128]{2,1,0:T(8,128)S(1)} %get-tuple-element.92), channel_id=1, source_target_pairs={{0,16},{16,0},{1,17},{17,1},{2,18},{18,2},{3,19},{19,3},{4,20},{20... | collective-permute-start | bytes 1179656 | tf_op jit(solution)/shard_map/ppermute | solution.py:481
  44.2 5.9 %collective-permute-start.11 = (f32[9,24,128]{2,1,0:T(8,128)S(1)}, f32[9,24,128]{2,1,0:T(8,128)S(1)}, u32[]{:S(2)}, u32[]{:S(2)}) collective-permute-start(f32[9,24,128]{2,1,0:T(8,128)S(1)} %get-tuple-element.90), channel_id=1, source_target_pairs={{0,1},{1,0},{2,3},{3,2},{4,5},{5,4},{6,7},{7,6},{8,9},{9,8},{10,11... | collective-permute-start | bytes 331784 | tf_op jit(solution)/shard_map/ppermute | solution.py:485
  46.7 8.6 %collective-permute-start.12 = (f32[9,24,128]{2,1,0:T(8,128)S(1)}, f32[9,24,128]{2,1,0:T(8,128)S(1)}, u32[]{:S(2)}, u32[]{:S(2)}) collective-permute-start(f32[9,24,128]{2,1,0:T(8,128)S(1)} %get-tuple-element.91), channel_id=1, source_target_pairs={{1,2},{2,1},{3,4},{4,3},{5,6},{6,5},{7,8},{8,7},{9,10},{10,9},{11,... | collective-permute-start | bytes 331784 | tf_op jit(solution)/shard_map/ppermute | solution.py:484

commit v4 on v3

--- a/solution.py
+++ b/solution.py
@@ -253,7 +253,7 @@
     loop((own_ref.shape[0] if count is None else count) // 2, pair)
 
 
-def z_adjoint(plan, grid_ref, za_ref, own_out, side_outs, pitch, count=None, at_out=0):
+def z_adjoint(plan, grid_ref, za_ref, own_out, side_outs, pitch, count=None, at_out=0, with_near=False):
     lanes, depth, side = plan.lanes, plan.depth, plan.z_side
 
     def pair(at):
@@ -265,7 +265,10 @@
             value = out[:, i * lanes : (i + 1) * lanes]
             own_out[at_out + at * 2 + i] = value[:depth]
             for stage, ref in enumerate(side_outs):
-                ref[at_out + at * 2 + i] = value[depth + stage * side : depth + (stage + 1) * side]
+                sent = value[depth + stage * side : depth + (stage + 1) * side]
+                if with_near:
+                    sent = jnp.concatenate([sent, near_side(plan, value[:depth], stage)], axis=0)
+                ref[at_out + at * 2 + i] = sent
 
     loop((own_out.shape[0] if count is None else count) // 2, pair)
 
@@ -362,11 +365,13 @@
 
 
 def main_kernel(plan, field, level, halo_ref, zf_ref, za_ref, yf_ref, ya_ref, xf_ref, xa_ref, views_ref, near_in, inner_in, *refs):
-    side_refs, (halo_grid, near_out, own_out, *side_outs), inner_out = refs[: plan.z_stages], refs[plan.z_stages : -1], refs[-1]
+    side_refs, refs = refs[: plan.z_stages], refs[plan.z_stages :]
+    (inner_out, own_out, *side_outs), (halo_grid, near_out) = refs[:-2], refs[-2:]
     pair_along_z(plan, halo_ref, side_refs, zf_ref, halo_grid, 0)
     grids = (halo_grid, near_in, inner_in), (halo_grid, near_out, inner_out)
     of_views(plan, field, level, yf_ref, ya_ref, xf_ref, xa_ref, views_ref, *grids)
-    z_adjoint(plan, inner_out, za_ref, own_out, side_outs, plan.inner_pitch)
+    z_adjoint(plan, halo_grid, za_ref, own_out, side_outs, plan.pair_pitch, 2 * HALO)
+    z_adjoint(plan, near_out, za_ref, own_out, side_outs, plan.pair_pitch, 2 * HALO, 2 * HALO)
 
 
 def last_main_kernel(plan, field, level, edge_ref, zf_ref, za_ref, yf_ref, ya_ref, xf_ref, xa_ref, views_ref, inner_in, *refs):
@@ -378,9 +383,8 @@
     z_adjoint(plan, halo_grid, za_ref, own_out, side_outs, plan.pair_pitch)
 
 
-def edge_rest_kernel(plan, halo_ref, near_ref, za_ref, own_out, *side_outs):
-    z_adjoint(plan, halo_ref, za_ref, own_out, side_outs, plan.pair_pitch, 2 * HALO)
-    z_adjoint(plan, near_ref, za_ref, own_out, side_outs, plan.pair_pitch, 2 * HALO, 2 * HALO)
+def inner_rest_kernel(plan, inner_ref, za_ref, own_out, *side_outs):
+    z_adjoint(plan, inner_ref, za_ref, own_out, side_outs, plan.inner_pitch, with_near=True)
 
 
 def own_rest_kernel(plan, near_ref, inner_ref, za_ref, own_out, *side_outs):
@@ -394,7 +398,7 @@
     value = ref[at : at + count]
     blank = jnp.zeros((count, depth - side, plan.lanes), F32)
     for got_ref, last in zip(got_refs, (even_z == 1, even_z != 1)):
-        got = got_ref[at : at + count]
+        got = got_ref[at : at + count, : plan.z_side]
         value = value + jnp.where(last, jnp.concatenate([blank, got], axis=1), jnp.concatenate([got, blank], axis=1))
     return value
 
@@ -417,17 +421,17 @@
 def near_side(plan, value, stage):
     even_z = evens()[0]
     last = (even_z == 1, even_z != 1)[stage]
-    return jnp.where(last, value[:, plan.depth - plan.z_side :], value[:, : plan.z_side])
+    return jnp.where(last, value[..., plan.depth - plan.z_side :, :], value[..., : plan.z_side, :])
 
 
 def next_inner_kernel(plan, own_ref, summed_ref, *refs):
-    got_refs, (out_ref, *side_refs) = refs[: plan.z_stages], refs[plan.z_stages :]
+    stages, side, scale = plan.z_stages, plan.z_side, 1.0 / plan.views
+    side_refs, beyond_refs, got_refs, (out_ref, *side_outs) = [refs[i * stages : (i + 1) * stages] for i in range(3)] + [refs[3 * stages :]]
     for at in range(0, own_ref.shape[0], HALO + 1):
         end = min(at + HALO + 1, own_ref.shape[0])
-        value = own_ref[at:end] * add_sides(plan, summed_ref, got_refs, at, end - at) * (1.0 / plan.views)
-        out_ref[at:end] = value
-        for stage, ref in enumerate(side_refs):
-            ref[at:end] = near_side(plan, value, stage)
+        out_ref[at:end] = own_ref[at:end] * add_sides(plan, summed_ref, got_refs, at, end - at) * scale
+        for old, mine, theirs, new in zip(side_refs, beyond_refs, got_refs, side_outs):
+            new[at:end] = old[at:end] * (mine[at:end, :side] + theirs[at:end, side:]) * scale
 
 
 def next_edge_kernel(plan, own_ref, summed_ref, first_ref, second_ref, out_ref, *side_refs):
@@ -441,12 +445,12 @@
 
 
 def last_kernel(plan, edge_ref, inner_ref, summed_ref, first_ref, second_ref, *refs):
-    got_refs, (out_ref,) = refs[: plan.z_stages], refs[plan.z_stages :]
+    got_refs, (out_ref, turned_ref) = refs[: plan.z_stages], refs[plan.z_stages :]
     scale = 1.0 / plan.views
     first_row, second_row, inner_row = y_first_rows(plan, evens()[1])[2:]
 
     def put(row, value):
-        out_ref[pl.ds(row, plan.depth, stride=plan.rows), :] = value
+        turned_ref[pl.ds(row, plan.depth, stride=odd_tiles(plan.rows)), :] = value
 
     for i in range(plan.rows):
         total = add_sides(plan, summed_ref, got_refs, i, 1)[0]
@@ -456,6 +460,8 @@
             put(second_row + i - HALO, edge_ref[2 * HALO + i] * (total + second_ref[i - HALO]) * scale)
         else:
             put(inner_row + i - 2 * HALO, inner_ref[i - 2 * HALO] * total * scale)
+    for z in range(plan.depth):
+        out_ref[z * plan.rows : (z + 1) * plan.rows] = turned_ref[pl.ds(z * odd_tiles(plan.rows), plan.rows), :]
 
 
 def on_device(estimate, views, background, psf_taps, psf_lengths, view_offsets, field_rows):
@@ -490,7 +496,8 @@
     got = y_swap([first, second])
     own_side = z_swap(sent)
     zf, za, *tables = bands(plan, *[pltpu.with_memory_space_constraint(a, pltpu.HBM) for a in (psf_lengths.T, view_offsets.T, psf_taps)])
-    (grown,) = run(grow_kernel, (own_inner, zf, *[value[2 * HALO :] for value in own_side]), [inner_grid])
+    inner_side = [value[2 * HALO :] for value in own_side]
+    (grown,) = run(grow_kernel, (own_inner, zf, *inner_side), [inner_grid])
     near = jnp.concatenate([first, second], axis=0)
     (near_grown,) = run(grow_near_kernel, (near, zf, *[value[: 2 * HALO] for value in own_side]), [pair_grid])
     got, grown, near_grown = lax.optimization_barrier((got, grown, near_grown))
@@ -511,23 +518,29 @@
             got_halo, summed_own, beyond = lax.optimization_barrier((got_halo, summed_own, beyond))
             got_own = z_swap(beyond)
             got = y_swap(run(last_sums_kernel, (summed, *got_halo), [own_of(HALO), own_of(HALO)]))
-            out = run(last_kernel, (own_edge, own_inner, summed_own, *got, *got_own), [((depth * rows, lanes), F32)])
+            out = run(
+                last_kernel, (own_edge, own_inner, summed_own, *got, *got_own), [((depth * rows, lanes), F32)],
+                scratch=[pltpu.VMEM((depth * odd_tiles(rows), lanes), F32)],
+            )
             return out[0].reshape(depth, rows, lanes)
-        halo_grown, near_grown, summed_inner, *beyond = run(
+        inner_grown, summed_edge, *beyond = run(
             main_kernel, (field, background, halo, *tables, near_grown, grown, *edge_side),
-            [pair_grid, pair_grid, own_of(inner)] + sides_of(inner), scalars=2, scratch=[pltpu.VMEM(*inner_grid)],
+            [inner_grid, own_of(edge)] + sides_of(edge), scalars=2, scratch=[pltpu.VMEM(*pair_grid)] * 2,
         )
+        got_edge = z_swap(beyond)
+        both = [((inner, 2 * side, lanes), F32)] * stages
+        summed_inner, *beyond = run(inner_rest_kernel, (inner_grown, za), [own_of(inner)] + both)
+        got_edge, summed_inner, beyond = lax.optimization_barrier((got_edge, summed_inner, beyond))
         got_inner = z_swap(beyond)
-        summed_edge, *beyond = run(edge_rest_kernel, (halo_grown, near_grown, za), [own_of(edge)] + sides_of(edge))
-        got_inner, summed_edge, beyond = lax.optimization_barrier((got_inner, summed_edge, beyond))
-        got_edge = z_swap(beyond)
         summed_edge, *ends = run(sums_kernel, (summed_edge, *got_edge), [own_of(edge), own_of(2 * HALO), own_of(2 * HALO)])
         got = y_swap(ends)
-        own_inner, *sent = run(next_inner_kernel, (own_inner, summed_inner, *got_inner), [own_of(inner)] + sides_of(inner))
-        (grown,) = run(grow_kernel, (own_inner, zf, *z_swap(sent)), [inner_grid])
-        got, grown = lax.optimization_barrier((got, grown))
+        got, got_inner = lax.optimization_barrier((got, got_inner))
         own_edge, *sent = run(next_edge_kernel, (own_edge, summed_edge, *got), [own_of(edge)] + sides_of(edge))
         edge_side = z_swap(sent)
+        own_inner, *inner_side = run(
+            next_inner_kernel, (own_inner, summed_inner, *inner_side, *beyond, *got_inner), [own_of(inner)] + sides_of(inner)
+        )
+        (grown,) = run(grow_kernel, (own_inner, zf, *inner_side), [inner_grid])
 
 
 def solution(mesh):

time: 56.7 us -> 55.6 us (0.981)
  waiting for transfers between devices: 17.9 us -> 17.3 us
    ppermute x8 -> x7, waiting for transfers between devices: 4.49 us -> 3.1 us  [z_swap(): lax.ppermute(value, 'tile', pairs)]
    ppermute x3, waiting for transfers between devices: 5.54 us -> 6.34 us  [y_swap(): return [lax.ppermute(values[0], 'view', y_pairs[0]), second]]
    ppermute x8 -> x7, starting transfers between devices: 1.49 us -> 1.08 us  [z_swap(): lax.ppermute(value, 'tile', pairs)]
  transfers between devices with their start and end apart: 14 -> 13, of which waited for: 10 -> 9; matrix products, arithmetic and copies ran while one was open for 0% -> 0% of each run, Pallas kernels for 12% -> 12%
where the time goes in v4:
time: 55.6 us; the launch traced here: 55.3 us
  Pallas kernels  20.8 us (37%)
  waiting for transfers between devices  17.3 us (31%)
  starting transfers between devices  15.7 us (28%)
  local copies, waits for them, and re-layouts  1.15 us (2%)
    pallas_call x14, Pallas kernels, call(): pl.pallas_call(body, out_shape=[jax.ShapeDtypeStruct(*shape) for shape in...  20.8 us
    ppermute x3, starting transfers between devices, y_swap(): second = lax.ppermute(values[1], 'view', y_pairs[1])  10.5 us
    ppermute x3, waiting for transfers between devices, y_swap(): second = lax.ppermute(values[1], 'view', y_pairs[1])  7.9 us
    ppermute x3, waiting for transfers between devices, y_swap(): return [lax.ppermute(values[0], 'view', y_pairs[0]), second]  6.34 us
    ppermute x3, starting transfers between devices, y_swap(): return [lax.ppermute(values[0], 'view', y_pairs[0]), second]  4.18 us
    ppermute x7, waiting for transfers between devices, z_swap(): lax.ppermute(value, 'tile', pairs)  3.1 us
  transfers between devices with their start and end apart: 13, of which 9 were waited for; matrix products, arithmetic and copies ran while one was open for 0% of the time, Pallas kernels for 12%

profile of v4, /device:TPU:16, one launch (start us, length us, event | category | flops | bytes accessed | tf_op | source)
XLA Modules:
  0.0 55.3 jit_solution(3061087148202574807)
XLA Ops:
  0.0 1.1 %copy-done.1 = f32[24,48,128]{2,1,0:T(8,128)S(1)} copy-done((f32[24,48,128]{2,1,0:T(8,128)S(1)}, f32[24,48,128]{2,1,0:T(8,128)}, u32[]{:S(2)}) %copy-start.1) | copy-done | bytes 589848
  1.1 0.2 edges_kernel.1
  1.4 1.6 %collective-permute-start = (f32[9,24,128]{2,1,0:T(8,128)S(1)}, f32[9,24,128]{2,1,0:T(8,128)S(1)}, u32[]{:S(2)}, u32[]{:S(2)}) collective-permute-start(f32[9,24,128]{2,1,0:T(8,128)S(1)} %get-tuple-element.48), channel_id=1, source_target_pairs={{0,1},{1,0},{2,3},{3,2},{4,5},{5,4},{6,7},{7,6},{8,9},{9,8},{10,11... | collective-permute-start | bytes 331784 | tf_op jit(solution)/shard_map/ppermute | solution.py:491
  2.9 3.3 %collective-permute-start.1 = (f32[9,24,128]{2,1,0:T(8,128)S(1)}, f32[9,24,128]{2,1,0:T(8,128)S(1)}, u32[]{:S(2)}, u32[]{:S(2)}) collective-permute-start(f32[9,24,128]{2,1,0:T(8,128)S(1)} %get-tuple-element.49), channel_id=1, source_target_pairs={{1,2},{2,1},{3,4},{4,3},{5,6},{6,5},{7,8},{8,7},{9,10},{10,9},{11,... | collective-permute-start | bytes 331784 | tf_op jit(solution)/shard_map/ppermute | solution.py:490
  6.2 2.8 %bands_kernel.1 = (bf16[144,144]{1,0:T(8,128)(2,1)S(1)}, bf16[96,144]{1,0:T(8,128)(2,1)S(1)}, bf16[6,96,160]{2,1,0:T(8,128)(2,1)S(1)}, bf16[6,80,144]{2,1,0:T(8,...) custom-call(s32[3,6]{1,0:T(4,128)} %bitcast.8, s32[3,6]{1,0:T(4,128)} %bitcast.9, ...), custom_call_target="tpu_custom_call" | custom-call | flops 1000 | bytes 1000 | tf_op jit(solution)/shard_map/bands_kernel/pallas_call | solution.py:199
  9.1 0.4 grow_near_kernel.1.near_in
  9.6 0.6 %grow_kernel.2.inner_in = f32[5760,128]{1,0:T(8,128)S(1)} custom-call(f32[30,24,128]{2,1,0:T(8,128)S(1)} %get-tuple-element.50.inner_ref.own_ref, bf16[144,144]{1,0:T(8,128)(2,1)S(1)} %get-tuple-element.51.zf_ref, f32[30,16,128]{2,1,0:T(8,128)S(1)} %slice.8.refs_0_), custom_call_target="tpu_custom_call" | custom-call | flops 1000 | bytes 1000 | tf_op jit(solution)/shard_map/grow_kernel/pallas_call | solution.py:199
  10.2 1.5 %collective-permute-done.1 = f32[9,24,128]{2,1,0:T(8,128)S(1)} collective-permute-done((f32[9,24,128]{2,1,0:T(8,128)S(1)}, f32[9,24,128]{2,1,0:T(8,128)S(1)}, u32[]{:S(2)}, u32[]{:S(2)}) %collective-permute-start.1) | collective-permute-done | bytes 110624 | tf_op jit(solution)/shard_map/ppermute | solution.py:490
  11.9 1.4 %collective-permute-done.3.refs_0_ = f32[18,16,128]{2,1,0:T(8,128)S(1)} collective-permute-done((f32[18,16,128]{2,1,0:T(8,128)S(1)}, f32[18,16,128]{2,1,0:T(8,128)S(1)}, u32[]{:S(2)}, u32[]{:S(2)}) %collective-permute-start.3) | collective-permute-done | bytes 147488 | tf_op jit(solution)/shard_map/ppermute | solution.py:487
  13.2 6.6 %main_kernel.1 = (f32[5760,128]{1,0:T(8,128)S(1)}, f32[36,24,128]{2,1,0:T(8,128)S(1)}, f32[36,16,128]{2,1,0:T(8,128)S(1)}) custom-call(s32[2,6]{1,0:T(2,128)S(1)} %bitcast.6, f32[6]{0:T(128)S(1)} %copy-done.3, f32[18,24,128]{2,1,0:T(8,128)S(1)} %constant_dynamic-update-slice_fusion.halo_ref, bf16[144,144]{1,0:T(8,128)(2,1)S(1)} %get-tuple-element.51.zf_ref, ...), custom_call_target="tpu_custom_call" | custom-call | flops 1000 | bytes 1000 | tf_op jit(solution)/shard_map/main_kernel/pallas_call | solution.py:199
  19.8 0.2 collective-permute-start.4
  20.0 0.7 %inner_rest_kernel.1 = (f32[30,24,128]{2,1,0:T(8,128)S(1)}, f32[30,32,128]{2,1,0:T(8,128)S(1)}) custom-call(f32[5760,128]{1,0:T(8,128)S(1)} %get-tuple-element.64.inner_ref, bf16[96,144]{1,0:T(8,128)(2,1)S(1)} %get-tuple-element.55.za_ref), custom_call_target="tpu_custom_call" | custom-call | flops 1000 | bytes 1000 | tf_op jit(solution)/shard_map/inner_rest_kernel/pallas_call | solution.py:199
  20.7 0.7 %collective-permute-done.4.refs_0_ = f32[36,16,128]{2,1,0:T(8,128)S(1)} collective-permute-done((f32[36,16,128]{2,1,0:T(8,128)S(1)}, f32[36,16,128]{2,1,0:T(8,128)S(1)}, u32[]{:S(2)}, u32[]{:S(2)}) %collective-permute-start.4) | collective-permute-done | bytes 294944 | tf_op jit(solution)/shard_map/ppermute | solution.py:487
  21.4 0.1 collective-permute-start.7
  21.7 0.1 collective-permute-start.5
  21.8 4.0 %collective-permute-start.6 = (f32[18,24,128]{2,1,0:T(8,128)S(1)}, f32[18,24,128]{2,1,0:T(8,128)S(1)}, u32[]{:S(2)}, u32[]{:S(2)}) collective-permute-start(f32[18,24,128]{2,1,0:T(8,128)S(1)} %get-tuple-element.70), channel_id=1, source_target_pairs={{1,2},{2,1},{3,4},{4,3},{5,6},{6,5},{7,8},{8,7},{9,10},{10,9},{11,... | collective-permute-start | bytes 663560 | tf_op jit(solution)/shard_map/ppermute | solution.py:490
  25.8 6.2 %collective-permute-done.5.first_ref = f32[18,24,128]{2,1,0:T(8,128)S(1)} collective-permute-done((f32[18,24,128]{2,1,0:T(8,128)S(1)}, f32[18,24,128]{2,1,0:T(8,128)S(1)}, u32[]{:S(2)}, u32[]{:S(2)}) %collective-permute-start.5) | collective-permute-done | bytes 221216 | tf_op jit(solution)/shard_map/ppermute | solution.py:491
  32.0 1.2 %collective-permute-done.6.second_ref = f32[18,24,128]{2,1,0:T(8,128)S(1)} collective-permute-done((f32[18,24,128]{2,1,0:T(8,128)S(1)}, f32[18,24,128]{2,1,0:T(8,128)S(1)}, u32[]{:S(2)}, u32[]{:S(2)}) %collective-permute-start.6) | collective-permute-done | bytes 221216 | tf_op jit(solution)/shard_map/ppermute | solution.py:490
  33.2 0.1 next_edge_kernel.1
  33.4 0.1 next_inner_kernel.1
  33.5 0.6 %grow_kernel.3.inner_in = f32[5760,128]{1,0:T(8,128)S(1)} custom-call(f32[30,24,128]{2,1,0:T(8,128)S(1)} %get-tuple-element.77.inner_ref, bf16[144,144]{1,0:T(8,128)(2,1)S(1)} %get-tuple-element.51.zf_ref, f32[30,16,128]{2,1,0:T(8,128)S(1)} %get-tuple-element.78.refs_0_), custom_call_target="tpu_custom_call" | custom-call | flops 1000 | bytes 1000 | tf_op jit(solution)/shard_map/grow_kernel/pallas_call | solution.py:199
  34.1 0.9 %collective-permute-done.8.refs_0_ = f32[36,16,128]{2,1,0:T(8,128)S(1)} collective-permute-done((f32[36,16,128]{2,1,0:T(8,128)S(1)}, f32[36,16,128]{2,1,0:T(8,128)S(1)}, u32[]{:S(2)}, u32[]{:S(2)}) %collective-permute-start.8) | collective-permute-done | bytes 294944 | tf_op jit(solution)/shard_map/ppermute | solution.py:487
  35.0 6.5 %last_main_kernel.1 = (f32[3456,128]{1,0:T(8,128)S(1)}, f32[5760,128]{1,0:T(8,128)S(1)}, f32[18,24,128]{2,1,0:T(8,128)S(1)}, f32[18,16,128]{2,1,0:T(8,128)S(1)}) custom-call(s32[2,6]{1,0:T(2,128)S(1)} %bitcast.7, f32[6]{0:T(128)S(1)} %copy-done.3, f32[36,24,128]{2,1,0:T(8,128)S(1)} %get-tuple-element.74.edge_ref, ...), custom_call_target="tpu_custom_call" | custom-call | flops 1000 | bytes 1000 | tf_op jit(solution)/shard_map/last_main_kernel/pallas_call | solution.py:199
  41.5 0.2 collective-permute-start.9
  41.7 1.1 %own_rest_kernel.1 = (f32[48,24,128]{2,1,0:T(8,128)S(1)}, f32[48,16,128]{2,1,0:T(8,128)S(1)}) custom-call(f32[3456,128]{1,0:T(8,128)S(1)} %get-tuple-element.81.near_ref, f32[5760,128]{1,0:T(8,128)S(1)} %get-tuple-element.82.inner_ref, bf16[96,144]{1,0:T(8,128)(2,1)S(1)} %get-tuple-element.55.za_ref), custom_call_target="tpu_custom_call" | custom-call | flops 1000 | bytes 1000 | tf_op jit(solution)/shard_map/own_rest_kernel/pallas_call | solution.py:199
  42.8 0.1 collective-permute-done.9.refs_0_
  42.9 0.3 collective-permute-start.12
  43.3 2.5 %collective-permute-start.10 = (f32[9,24,128]{2,1,0:T(8,128)S(1)}, f32[9,24,128]{2,1,0:T(8,128)S(1)}, u32[]{:S(2)}, u32[]{:S(2)}) collective-permute-start(f32[9,24,128]{2,1,0:T(8,128)S(1)} %get-tuple-element.88), channel_id=1, source_target_pairs={{0,1},{1,0},{2,3},{3,2},{4,5},{5,4},{6,7},{7,6},{8,9},{9,8},{10,11... | collective-permute-start | bytes 331784 | tf_op jit(solution)/shard_map/ppermute | solution.py:491
  45.8 3.2 %collective-permute-start.11 = (f32[9,24,128]{2,1,0:T(8,128)S(1)}, f32[9,24,128]{2,1,0:T(8,128)S(1)}, u32[]{:S(2)}, u32[]{:S(2)}) collective-permute-start(f32[9,24,128]{2,1,0:T(8,128)S(1)} %get-tuple-element.89), channel_id=1, source_target_pairs={{1,2},{2,1},{3,4},{4,3},{5,6},{6,5},{7,8},{8,7},{9,10},{10,9},{11,... | collective-permute-start | bytes 331784 | tf_op jit(solution)/shard_map/ppermute | solution.py:490
  49.0 0.2 collective-permute-done.10.first_ref
  49.2 5.1 %collective-permute-done.11.second_ref = f32[9,24,128]{2,1,0:T(8,128)S(1)} collective-permute-done((f32[9,24,128]{2,1,0:T(8,128)S(1)}, f32[9,24,128]{2,1,0:T(8,128)S(1)}, u32[]{:S(2)}, u32[]{:S(2)}) %collective-permute-start.11) | collective-permute-done | bytes 110624 | tf_op jit(solution)/shard_map/ppermute | solution.py:490
  54.3 1.0 %last_kernel.1 = f32[1152,128]{1,0:T(8,128)} custom-call(f32[36,24,128]{2,1,0:T(8,128)S(1)} %get-tuple-element.74.edge_ref, f32[30,24,128]{2,1,0:T(8,128)S(1)} %get-tuple-element.77.inner_ref, f32[48,24,128]{2,1,0:T(8,128)S(1)} %get-tuple-element.85.summed_ref, f32[9,24,128]{2,1,0:T(8,128)S(1)} %collective-permute-done.10.first_ref, ...), custom_call_target="tpu_custom_call" | custom-call | flops 1000 | bytes 1000 | tf_op jit(solution)/shard_map/last_kernel/pallas_call | solution.py:199
  (23 shorter events, 0.5 us)
Async XLA Ops:
  0.0 1.1 %copy-start.1 = (f32[24,48,128]{2,1,0:T(8,128)S(1)}, f32[24,48,128]{2,1,0:T(8,128)}, u32[]{:S(2)}) copy-start(f32[24,48,128]{2,1,0:T(8,128)} %param.7) | copy-start | bytes 1769476
  1.3 7.8 %collective-permute-start.2 = (f32[48,16,128]{2,1,0:T(8,128)S(1)}, f32[48,16,128]{2,1,0:T(8,128)S(1)}, u32[]{:S(2)}, u32[]{:S(2)}) collective-permute-start(f32[48,16,128]{2,1,0:T(8,128)S(1)} %get-tuple-element.52), channel_id=1, source_target_pairs={{0,16},{16,0},{1,17},{17,1},{2,18},{18,2},{3,19},{19,3},{4,20},{20... | collective-permute-start | bytes 1179656 | tf_op jit(solution)/shard_map/ppermute | solution.py:487
  1.4 8.8 %collective-permute-start = (f32[9,24,128]{2,1,0:T(8,128)S(1)}, f32[9,24,128]{2,1,0:T(8,128)S(1)}, u32[]{:S(2)}, u32[]{:S(2)}) collective-permute-start(f32[9,24,128]{2,1,0:T(8,128)S(1)} %get-tuple-element.48), channel_id=1, source_target_pairs={{0,1},{1,0},{2,3},{3,2},{4,5},{5,4},{6,7},{7,6},{8,9},{9,8},{10,11... | collective-permute-start | bytes 331784 | tf_op jit(solution)/shard_map/ppermute | solution.py:491
  2.9 8.8 %collective-permute-start.1 = (f32[9,24,128]{2,1,0:T(8,128)S(1)}, f32[9,24,128]{2,1,0:T(8,128)S(1)}, u32[]{:S(2)}, u32[]{:S(2)}) collective-permute-start(f32[9,24,128]{2,1,0:T(8,128)S(1)} %get-tuple-element.49), channel_id=1, source_target_pairs={{1,2},{2,1},{3,4},{4,3},{5,6},{6,5},{7,8},{8,7},{9,10},{10,9},{11,... | collective-permute-start | bytes 331784 | tf_op jit(solution)/shard_map/ppermute | solution.py:490
  9.5 3.7 %copy-start = (f32[6,24,48,128]{3,2,1,0:T(8,128)S(1)}, f32[6,24,48,128]{3,2,1,0:T(8,128)}, u32[]{:S(2)}) copy-start(f32[6,24,48,128]{3,2,1,0:T(8,128)} %views_ref.3) | copy-start | bytes 10616836
  9.5 3.7 %copy-start.2 = (s32[6,2]{0,1:T(2,128)S(1)}, s32[6,2]{0,1:T(2,128)}, u32[]{:S(2)}) copy-start(s32[6,2]{0,1:T(2,128)} %param.13) | copy-start | bytes 148
  9.5 3.7 %copy-start.3 = (f32[6]{0:T(128)S(1)}, f32[6]{0:T(128)}, u32[]{:S(2)}) copy-start(f32[6]{0:T(128)} %level.3) | copy-start | bytes 76
  11.8 1.4 %collective-permute-start.3 = (f32[18,16,128]{2,1,0:T(8,128)S(1)}, f32[18,16,128]{2,1,0:T(8,128)S(1)}, u32[]{:S(2)}, u32[]{:S(2)}) collective-permute-start(f32[18,16,128]{2,1,0:T(8,128)S(1)} %constant_dynamic-slice_fusion), channel_id=1, source_target_pairs={{0,16},{16,0},{1,17},{17,1},{2,18},{18,2},{3,19},{19,3},{4,20},{20... | collective-permute-start | bytes 442376 | tf_op jit(solution)/shard_map/ppermute | solution.py:487
  19.8 1.6 %collective-permute-start.4 = (f32[36,16,128]{2,1,0:T(8,128)S(1)}, f32[36,16,128]{2,1,0:T(8,128)S(1)}, u32[]{:S(2)}, u32[]{:S(2)}) collective-permute-start(f32[36,16,128]{2,1,0:T(8,128)S(1)} %get-tuple-element.63), channel_id=1, source_target_pairs={{0,16},{16,0},{1,17},{17,1},{2,18},{18,2},{3,19},{19,3},{4,20},{20... | collective-permute-start | bytes 884744 | tf_op jit(solution)/shard_map/ppermute | solution.py:487
  21.4 11.8 %collective-permute-start.7 = (f32[30,32,128]{2,1,0:T(8,128)S(1)}, f32[30,32,128]{2,1,0:T(8,128)S(1)}, u32[]{:S(2)}, u32[]{:S(2)}) collective-permute-start(f32[30,32,128]{2,1,0:T(8,128)S(1)} %get-tuple-element.71.refs_1_), channel_id=1, source_target_pairs={{0,16},{16,0},{1,17},{17,1},{2,18},{18,2},{3,19},{19,3},{4,20},{20... | collective-permute-start | bytes 1474568 | tf_op jit(solution)/shard_map/ppermute | solution.py:487
  21.7 10.3 %collective-permute-start.5 = (f32[18,24,128]{2,1,0:T(8,128)S(1)}, f32[18,24,128]{2,1,0:T(8,128)S(1)}, u32[]{:S(2)}, u32[]{:S(2)}) collective-permute-start(f32[18,24,128]{2,1,0:T(8,128)S(1)} %get-tuple-element.69), channel_id=1, source_target_pairs={{0,1},{1,0},{2,3},{3,2},{4,5},{5,4},{6,7},{7,6},{8,9},{9,8},{10,11... | collective-permute-start | bytes 663560 | tf_op jit(solution)/shard_map/ppermute | solution.py:491
  21.8 11.4 %collective-permute-start.6 = (f32[18,24,128]{2,1,0:T(8,128)S(1)}, f32[18,24,128]{2,1,0:T(8,128)S(1)}, u32[]{:S(2)}, u32[]{:S(2)}) collective-permute-start(f32[18,24,128]{2,1,0:T(8,128)S(1)} %get-tuple-element.70), channel_id=1, source_target_pairs={{1,2},{2,1},{3,4},{4,3},{5,6},{6,5},{7,8},{8,7},{9,10},{10,9},{11,... | collective-permute-start | bytes 663560 | tf_op jit(solution)/shard_map/ppermute | solution.py:490
  33.3 1.6 %collective-permute-start.8 = (f32[36,16,128]{2,1,0:T(8,128)S(1)}, f32[36,16,128]{2,1,0:T(8,128)S(1)}, u32[]{:S(2)}, u32[]{:S(2)}) collective-permute-start(f32[36,16,128]{2,1,0:T(8,128)S(1)} %get-tuple-element.79), channel_id=1, source_target_pairs={{0,16},{16,0},{1,17},{17,1},{2,18},{18,2},{3,19},{19,3},{4,20},{20... | collective-permute-start | bytes 884744 | tf_op jit(solution)/shard_map/ppermute | solution.py:487
  41.5 1.4 %collective-permute-start.9 = (f32[18,16,128]{2,1,0:T(8,128)S(1)}, f32[18,16,128]{2,1,0:T(8,128)S(1)}, u32[]{:S(2)}, u32[]{:S(2)}) collective-permute-start(f32[18,16,128]{2,1,0:T(8,128)S(1)} %get-tuple-element.80), channel_id=1, source_target_pairs={{0,16},{16,0},{1,17},{17,1},{2,18},{18,2},{3,19},{19,3},{4,20},{20... | collective-permute-start | bytes 442376 | tf_op jit(solution)/shard_map/ppermute | solution.py:487
  42.9 11.4 %collective-permute-start.12 = (f32[48,16,128]{2,1,0:T(8,128)S(1)}, f32[48,16,128]{2,1,0:T(8,128)S(1)}, u32[]{:S(2)}, u32[]{:S(2)}) collective-permute-start(f32[48,16,128]{2,1,0:T(8,128)S(1)} %get-tuple-element.90), channel_id=1, source_target_pairs={{0,16},{16,0},{1,17},{17,1},{2,18},{18,2},{3,19},{19,3},{4,20},{20... | collective-permute-start | bytes 1179656 | tf_op jit(solution)/shard_map/ppermute | solution.py:487
  43.3 5.9 %collective-permute-start.10 = (f32[9,24,128]{2,1,0:T(8,128)S(1)}, f32[9,24,128]{2,1,0:T(8,128)S(1)}, u32[]{:S(2)}, u32[]{:S(2)}) collective-permute-start(f32[9,24,128]{2,1,0:T(8,128)S(1)} %get-tuple-element.88), channel_id=1, source_target_pairs={{0,1},{1,0},{2,3},{3,2},{4,5},{5,4},{6,7},{7,6},{8,9},{9,8},{10,11... | collective-permute-start | bytes 331784 | tf_op jit(solution)/shard_map/ppermute | solution.py:491
  45.8 8.6 %collective-permute-start.11 = (f32[9,24,128]{2,1,0:T(8,128)S(1)}, f32[9,24,128]{2,1,0:T(8,128)S(1)}, u32[]{:S(2)}, u32[]{:S(2)}) collective-permute-start(f32[9,24,128]{2,1,0:T(8,128)S(1)} %get-tuple-element.89), channel_id=1, source_target_pairs={{1,2},{2,1},{3,4},{4,3},{5,6},{6,5},{7,8},{8,7},{9,10},{10,9},{11,... | collective-permute-start | bytes 331784 | tf_op jit(solution)/shard_map/ppermute | solution.py:490
